TPU v7x, 32 devices: a whole 2x2x4 slice. The times are simulated.
32 devices in a mesh: ctx: 16 (over z, x, core), head: 2 (over y).
Axes of the slice: x: 2, y: 2, z: 4, core: 2. Of those that a mesh axis runs over, the one named last changes fastest.
Arguments:
- kv_latent: bfloat16 [8192, 576], P('ctx'), may hold values from -4 to 4
- queries: bfloat16 [8192, 3072], P('ctx', 'head'), may hold values from -22 to 22
- grad_out: bfloat16 [8192, 2048], P('ctx', 'head'), may hold values from -6 to 6
- kv_up_weight: bfloat16 [512, 4096], P(None, 'head'), may hold values from -0.25 to 0.25
- doc_ids: int32 [8192], replicated, may hold values from 0 to 7, never falling along the last dimension, each value on 1 to 1536 neighbouring positions
Outputs:
- grad_queries: bfloat16 [8192, 3072], P('ctx', 'head')
- grad_latent: bfloat16 [8192, 576], P('ctx')
- grad_weight: float32 [512, 4096], P('ctx', 'head')
Inputs may be any that keep to these rules, and one draw needn't show every extreme that they name: `doc_ids`: document ids never fall along the sequence; every document has 1 to 1536 tokens, and one has exactly 1536.
All inputs are finite; a program needn't handle non-finite values.
Results may differ from a plain program's by a relative error of at most 0.0076.
Values may be sent and summed in bfloat16 or wider, within the bound.
No kernel may reach another device: no remote copies, remote signals or barrier semaphores. Data moves between devices by JAX's collectives and lax.ppermute only.
A program may use at most 128 MiB of HBM per device.

v0:
```python
import functools
import math

import jax
import jax.numpy as jnp
from jax import lax
from jax.experimental import pallas as pl
from jax.experimental.pallas import tpu as pltpu
from jax.sharding import PartitionSpec as P

NOPE = 128
ROPE = 64
VDIM = 128
LATENT = 512
REACH = 3
QK = NOPE + ROPE
KV = NOPE + VDIM
WIDTH = LATENT + ROPE
LANES = 128
PIECE = 256

MASKED = -1e30
FLOOR = -1e20
SCALE = 1.0 / math.sqrt(QK)
SCALE2 = SCALE * math.log2(math.e)

NT = (((1,), (1,)), ((), ()))
NN = (((1,), (0,)), ((), ()))


def dot(a, b, dims=NN):
    return lax.dot_general(a, b, dims, preferred_element_type=jnp.float32)


def head_cols(h, size):
    return slice(h * size, (h + 1) * size)


def fold(value, combine):
    return combine(value.reshape(-1, 8, value.shape[1]), axis=0)


def fold(value, combine):
    return combine(value.reshape(-1, 8, value.shape[1]), axis=0)


def lift(latent, w_ref, k_out, v_out):
    for h in range(w_ref.shape[1] // KV):
        lifted = dot(latent[:, :LATENT], w_ref[:, head_cols(h, KV)]).astype(jnp.bfloat16)
        k_out(h, jnp.concatenate([lifted[:, :NOPE], latent[:, LATENT:]], axis=1))
        v_out(h, lifted[:, NOPE:])


def score_block(key, value, q_ref, do_ref, bounds, run_ref, raw_ref, graw_ref, keep):
    rows = do_ref.shape[0]
    lower, upper = bounds
    index = lax.broadcasted_iota(jnp.int32, (LANES, LANES), 0)
    parts = [slice(r, r + LANES) for r in range(0, rows, LANES)]

    def multiply(h, first):
        cols = slice(first, first + PIECE)
        raw_ref[h, :, cols] = dot(key(h), q_ref[cols, head_cols(h, QK)], NT)
        graw_ref[h, :, cols] = dot(value(h), do_ref[cols, head_cols(h, VDIM)], NT)

    def weigh(h, first):
        for c in range(first, first + PIECE, LANES):
            cols = slice(c, c + LANES)
            high = None
            for part in parts:
                seen = index >= lower[:, cols] - part.start
                if upper is not None:
                    seen = seen & (index <= upper[:, cols] - part.start)
                scores = jnp.where(seen, raw_ref[h, part, cols] * SCALE2, MASKED)
                raw_ref[h, part, cols] = scores
                piece = fold(scores, jnp.max)
                high = piece if high is None else jnp.maximum(high, piece)
            old_top = run_ref[h, 0:1, cols]
            new_top = jnp.maximum(old_top, jnp.max(high, axis=0, keepdims=True))
            mass, cross = 0.0, 0.0
            for part in parts:
                weights = jnp.exp2(raw_ref[h, part, cols] - new_top)
                grads = graw_ref[h, part, cols]
                keep(h, part, cols, weights.astype(jnp.bfloat16), grads.astype(jnp.bfloat16))
                mass = mass + fold(weights, jnp.sum)
                cross = cross + fold(weights * grads, jnp.sum)
            factor = jnp.exp2(old_top - new_top)
            run_ref[h, 0:1, cols] = new_top
            run_ref[h, 1:2, cols] = run_ref[h, 1:2, cols] * factor + jnp.sum(
                mass, axis=0, keepdims=True
            )
            run_ref[h, 2:3, cols] = run_ref[h, 2:3, cols] * factor + jnp.sum(
                cross, axis=0, keepdims=True
            )

    alternate(rows, do_ref.shape[1] // VDIM, multiply, weigh)


def alternate(rows, heads, first, second):
    pieces = [(h, c) for h in range(heads) for c in range(0, rows, PIECE)]
    first(*pieces[0])
    for now, following in zip(pieces, pieces[1:] + [None]):
        if following:
            first(*following)
        second(*now)


def grad_block(kept, key, top, end_ref, q_t, do_t, low_ref, ds_ref, dq_acc, d_acc, r_acc, first_q, first_k):
    def put(ref, part, value, first):
        ref[part, :] = value if first else ref[part, :] + value

    rows = do_t.shape[1]
    heads = do_t.shape[0] // VDIM
    sums = {}

    def weigh(h, first):
        for c in range(first, first + PIECE, LANES):
            cols = slice(c, c + LANES)
            factor = jnp.exp2(top(h)[:, cols] - end_ref[h, 0:1, cols]) * end_ref[h, 1:2, cols]
            delta = end_ref[h, 2:3, cols]
            for r in range(0, rows, LANES):
                part = slice(r, r + LANES)
                weights, grads = kept(h, part, cols)
                probs = weights.astype(jnp.float32) * factor
                low_ref[h, part, cols] = probs.astype(jnp.bfloat16)
                ds_ref[h, part, cols] = (
                    probs * (grads.astype(jnp.float32) - delta)
                ).astype(jnp.bfloat16)

    def multiply(h, first):
        cols = slice(first, first + PIECE)
        low, dscore = low_ref[h, :, cols], ds_ref[h, :, cols]
        dvalue = dot(do_t[head_cols(h, VDIM), cols], low, NT)
        dkey = dot(q_t[head_cols(h, QK), cols], dscore, NT)
        own = head_cols(h, QK)
        dq = dot(key(h).T, dscore)
        dq_acc[own, cols] = dq if first_q else dq_acc[own, cols] + dq
        if first:
            dvalue, dkey = sums[h][0] + dvalue, sums[h][1] + dkey
        sums[h] = dvalue, dkey
        if first + PIECE == rows:
            dkey = dkey * SCALE
            put(d_acc, slice(h * KV, h * KV + NOPE), dkey[:NOPE], first_k)
            put(d_acc, slice(h * KV + NOPE, (h + 1) * KV), dvalue, first_k)
            put(r_acc, slice(0, ROPE), dkey[NOPE:], first_k and h == 0)

    alternate(rows, heads, weigh, multiply)


def start_stats(run_ref):
    count, rows = run_ref.shape[0], run_ref.shape[2]
    for h in range(count):
        run_ref[h, 0:1, :] = jnp.full((1, rows), FLOOR, jnp.float32)
        run_ref[h, 1:8, :] = jnp.zeros((7, rows), jnp.float32)


def chip_place(index_ref):
    core = lax.rem(index_ref[0], 2)
    return core, index_ref[0] - core


def order_pair(out_ref, core, own, other):
    out_ref[core] = own[...]
    out_ref[1 - core] = other[...]


LOCAL = ((1, REACH), (0, REACH), (1, REACH + 1))


def query_bounds(start_ref, chip, j, t, rows):
    lower = start_ref[j, 0:1, :] - (chip + t - REACH) * rows
    own = isinstance(t, int) and t == j + REACH
    return lower, lax.broadcasted_iota(jnp.int32, (1, rows), 1) if own else None


def find_starts(docs_ref, start_ref, chip, rows):
    for j in range(2):
        block = chip + j
        my_docs = docs_ref[:, pl.ds(pl.multiple_of(block * rows, rows), rows)]
        first_doc = my_docs[:, :1]
        key_docs = jnp.broadcast_to(my_docs, (128, rows)).T[:, :1]
        inside = jnp.sum(jnp.where(key_docs < my_docs, 1.0, 0.0), axis=0, keepdims=True)
        before = jnp.zeros((1, rows), jnp.float32)
        for back in range(1, REACH + 1):
            earlier = jnp.maximum(block - back, 0)
            docs = docs_ref[:, pl.ds(pl.multiple_of(earlier * rows, rows), rows)]
            same = (docs == first_doc) & (block >= back)
            before = before + jnp.where(same, 1.0, 0.0)
        before = jnp.sum(before, axis=1, keepdims=True)
        start = jnp.where(my_docs == first_doc, -before, inside).astype(jnp.int32)
        start_ref[j, 0:1, :] = start + block * rows


def local_kernel(
    index_ref, docs_ref, q0, do0, q1, do1, w_ref, lat0, lat1,
    e_ref, g_ref, k_ref, run_ref, top_ref, start_ref,
    q_ref, do_ref, lat_ref, v_ref, raw_ref, graw_ref,
):
    rows = q0.shape[0]
    core, chip = chip_place(index_ref)
    heads = w_ref.shape[1] // KV

    @pl.when(pl.program_id(0) == 0)
    def _():
        lat_ref[core] = lat0[...].T
        lat_ref[1 - core] = lat1[...].T
        find_starts(docs_ref, start_ref, chip, rows)

    order_pair(q_ref, core, q0, q1)
    order_pair(do_ref, core, do0, do1)
    for j in range(2):

        def k_out(h, key):
            k_ref[0, j * heads + h] = key

        def v_out(h, value):
            v_ref[j * heads + h] = value

        lift(lat_ref[j], w_ref, k_out, v_out)
        start_stats(run_ref.at[0, pl.ds(j * heads, heads)])
    for n, (j, t) in enumerate(LOCAL):
        slot = t - REACH

        def keep(h, part, cols, weights, grads):
            e_ref[0, n * heads + h, part, cols] = weights
            g_ref[0, n * heads + h, part, cols] = grads

        run = run_ref.at[0, pl.ds(j * heads, heads)]
        score_block(
            lambda h: k_ref[0, slot * heads + h], lambda h: v_ref[slot * heads + h],
            q_ref.at[j], do_ref.at[j], query_bounds(start_ref, chip, j, t, rows), run,
            raw_ref, graw_ref, keep,
        )
        for h in range(heads):
            top_ref[0, n * heads + h] = run[h]


def main_kernel(
    ranks,
    index_ref, docs_sref, q0, do0, q1, do1, w_ref,
    all_e, all_g, local_k, local_run, local_top, start_ref,
    lat_far, lat_swap, lat_mixed, lat_passed, lat_own, lat_other,
    dq0_ref, dq1_ref, keep_ref, send_ref, x_old, x_far, x_swap, x_own, x_other,
    q_ref, do_ref, lat_ref, lat_t_ref, e_ref, g_ref, k_ref, v_ref, top_ref,
    run_ref, end_ref, raw_ref, graw_ref, low_ref, ds_ref, dq_acc, d_acc, gw_acc, x_acc,
    r_acc, local_e, local_g, sems, kept_sems,
):
    step = pl.program_id(0)
    rows = q0.shape[0]
    heads = w_ref.shape[1] // KV
    blocks = REACH + 2
    kept_copies = [
        pltpu.make_async_copy(all_e.at[step], local_e, kept_sems.at[0]),
        pltpu.make_async_copy(all_g.at[step], local_g, kept_sems.at[1]),
    ]
    for copy in kept_copies:
        copy.start()
    core, chip = chip_place(index_ref)

    def active(j, t):
        block = chip + t - REACH
        last_doc = docs_sref[jnp.maximum(block, 0) * rows + rows - 1]
        return (block >= 0) & (last_doc >= docs_sref[(chip + j) * rows])

    def block_rows(t):
        return pl.ds(pl.multiple_of(t * rows, rows), rows)

    def piece_rows(t, part):
        size = part.stop - part.start
        return pl.ds(pl.multiple_of(t * rows + part.start, size), size)

    def loop(first, last, when, body):
        def visit(t, carry):
            @pl.when(when(t))
            def _():
                body(t)

            return carry

        lax.fori_loop(first, last, visit, 0)

    @pl.when(step == 0)
    def _():
        places = [(lat_far, 1 + core), (lat_swap, 2 - core), (lat_own, REACH + core),
                  (lat_other, REACH + 1 - core)]
        copies = [
            pltpu.make_async_copy(source, lat_t_ref.at[:, block_rows(t)], sems.at[i])
            for i, (source, t) in enumerate(places)
        ]
        first = lat_t_ref.at[:, block_rows(0)]
        oldest = pltpu.make_async_copy(lat_mixed, first, sems.at[4])
        passed = pltpu.make_async_copy(lat_passed, first, sems.at[4])
        for copy in copies:
            copy.start()
        pl.when(core == 0)(oldest.start)
        pl.when(core == 1)(passed.start)
        for copy in copies:
            copy.wait()
        oldest.wait()
        for t in range(REACH):
            part = slice(t * rows, (t + 1) * rows)
            lat_ref[part, :] = lat_t_ref[:, part].T

    order_pair(q_ref, core, q0, q1)
    order_pair(do_ref, core, do0, do1)

    def lift_block(t):
        def k_out(h, key):
            k_ref[h, block_rows(t), :] = key

        def v_out(h, value):
            v_ref[h, block_rows(t), :] = value

        lift(lat_ref[block_rows(t), :], w_ref, k_out, v_out)

    loop(0, REACH, lambda t: active(0, t), lift_block)

    for j in range(2):
        for h in range(heads):
            run_ref[h] = local_run[0, j * heads + h]

        def first_pass(t):
            def keep(h, part, cols, weights, grads):
                e_ref[h, piece_rows(t, part), cols] = weights
                g_ref[h, piece_rows(t, part), cols] = grads

            score_block(
                lambda h: k_ref[h, block_rows(t), :], lambda h: v_ref[h, block_rows(t), :],
                q_ref.at[j], do_ref.at[j], query_bounds(start_ref, chip, j, t, rows), run_ref,
                raw_ref, graw_ref, keep,
            )
            for h in range(heads):
                top_ref[h, t] = run_ref[h]

        loop(j, REACH, lambda t: active(j, t), first_pass)
        for h in range(heads):
            inverse = 1.0 / run_ref[h, 1:2, :]
            end_ref[h, 0:1, :] = run_ref[h, 0:1, :]
            end_ref[h, 1:2, :] = inverse
            end_ref[h, 2:3, :] = run_ref[h, 2:3, :] * inverse
        q_t, do_t = q_ref[j].T, do_ref[j].T

        def add(t, kept, key, top, first_q, first_k):
            grad_block(
                kept, key, top, end_ref, q_t, do_t, low_ref, ds_ref, dq_acc.at[j], d_acc.at[t],
                r_acc.at[t], first_q, first_k,
            )

        def second_pass(t):
            def kept(h, part, cols):
                return e_ref[h, piece_rows(t, part), cols], g_ref[h, piece_rows(t, part), cols]

            add(
                t, kept, lambda h: k_ref[h, block_rows(t), :], lambda h: top_ref[h, t, 0:1, :],
                False, j == 0,
            )

        if j == 0:
            for copy in kept_copies:
                copy.wait()
        first_q = True
        for n, (query, t) in enumerate(LOCAL):
            if query == j:
                add(
                    t,
                    lambda h, part, cols: (
                        local_e[n * heads + h, part, cols], local_g[n * heads + h, part, cols]
                    ),
                    lambda h: local_k[0, (t - REACH) * heads + h],
                    lambda h: local_top[0, n * heads + h, 0:1, :],
                    first_q, t == REACH + j,
                )
                first_q = False
        loop(j, REACH, lambda t: active(j, t), second_pass)

    def seen(t):
        return (t >= REACH) | active(0, t)

    def project(t, first):
        part = block_rows(t)
        grads = d_acc[t].astype(jnp.bfloat16)
        weight_part = dot(lat_t_ref[:LATENT, part], grads, NT)
        gw_acc[...] = weight_part if first else gw_acc[...] + weight_part
        latent_part = dot(w_ref[...], grads)

        @pl.when(step == 0)
        def _():
            x_acc[:LATENT, part] = latent_part
            x_acc[LATENT:, part] = r_acc[t]

        @pl.when(step > 0)
        def _():
            x_acc[:LATENT, part] += latent_part
            x_acc[LATENT:, part] += r_acc[t]

    @pl.when(step == 0)
    def _():
        def clear(t):
            x_acc[:, block_rows(t)] = jnp.zeros((WIDTH, rows), jnp.float32)

        loop(0, REACH, lambda t: ~seen(t), clear)

    project(REACH, True)
    loop(0, blocks, lambda t: seen(t) & (t != REACH), lambda t: project(t, False))
    dq0_ref[...] = (dq_acc[core] * SCALE).T.astype(dq0_ref.dtype)
    dq1_ref[...] = (dq_acc[1 - core] * SCALE).T.astype(dq1_ref.dtype)

    share = 2 * (LATENT // ranks)
    own_x = lax.rem(index_ref[0] // 2, 2)
    for i in range(ranks // 4):
        for out, x in ((keep_ref, own_x), (send_ref, 1 - own_x)):
            source = pl.multiple_of((2 * i + x) * share, share)
            out[i * share : (i + 1) * share, :] = gw_acc[pl.ds(source, share), :].astype(out.dtype)

    @pl.when(step == pl.num_programs(0) - 1)
    def _():
        places = ((x_old, 0), (x_far, 1 + core), (x_swap, 2 - core), (x_own, REACH + core),
                  (x_other, REACH + 1 - core))
        copies = []
        for i, (out, t) in enumerate(places):
            part = block_rows(t)
            lat_t_ref[:, part] = x_acc[:, part].astype(lat_t_ref.dtype)
            copies.append(pltpu.make_async_copy(lat_t_ref.at[:, part], out, sems.at[i]))
            copies[-1].start()
        for copy in copies:
            copy.wait()


def step_cols(height, size):
    return pl.BlockSpec((height, size), lambda i, index: (0, i))


def core_cols(height, size, first):
    def place(i, index):
        return (0, first(i, lax.rem(index[0], 2)))

    return pl.BlockSpec((height, size), place)


def step_block(*shape):
    return pl.BlockSpec((1, *shape), lambda i, index: (i, 0, 0, 0))


def fixed(*shape):
    return pl.BlockSpec(shape, lambda i, index: (0,) * len(shape))


SCALARS = pl.BlockSpec(memory_space=pltpu.SMEM)
ANYWHERE = pl.BlockSpec(memory_space=pl.ANY)


def call(body, steps, flops, in_specs, outs, scratch, name):
    return pl.pallas_call(
        body,
        grid_spec=pltpu.PrefetchScalarGridSpec(
            num_scalar_prefetch=1,
            grid=(steps,),
            in_specs=in_specs,
            out_specs=[spec for spec, _, _ in outs],
            scratch_shapes=[
                pltpu.VMEM(*entry) if isinstance(entry, tuple) else entry for entry in scratch
            ],
        ),
        out_shape=[jax.ShapeDtypeStruct(shape, kind) for _, shape, kind in outs],
        compiler_params=pltpu.CompilerParams(
            dimension_semantics=("arbitrary",), vmem_limit_bytes=58 * 1024 * 1024
        ),
        cost_estimate=pl.CostEstimate(
            flops=flops, bytes_accessed=16 * 1024 * 1024, transcendentals=0
        ),
        name=name,
    )


def head_specs(rows, heads, steps, in_place):
    def received(i, core):
        return i

    def own(i, core):
        return core * steps + i if in_place else i

    return [
        core_cols(rows, heads * QK, own), core_cols(rows, heads * VDIM, own),
        core_cols(rows, heads * QK, received), core_cols(rows, heads * VDIM, received),
        core_cols(LATENT, heads * KV, own),
    ]


def local_scores(index, docs, inputs, latents, heads, steps, in_place):
    rows = inputs[0].shape[0]
    low, full = jnp.bfloat16, jnp.float32
    count = len(LOCAL) * heads
    return call(
        local_kernel,
        steps,
        steps * heads * rows * rows,
        [
            fixed(1, docs.shape[1]), *head_specs(rows, heads, steps, in_place),
            fixed(WIDTH, rows), fixed(WIDTH, rows),
        ],
        [
            (step_block(count, rows, rows), (steps, count, rows, rows), low),
            (step_block(count, rows, rows), (steps, count, rows, rows), low),
            (step_block(2 * heads, rows, QK), (steps, 2 * heads, rows, QK), low),
            (step_block(2 * heads, 8, rows), (steps, 2 * heads, 8, rows), full),
            (step_block(count, 8, rows), (steps, count, 8, rows), full),
            (fixed(2, 8, rows), (2, 8, rows), jnp.int32),
        ],
        [
            ((2, rows, heads * QK), low),
            ((2, rows, heads * VDIM), low),
            ((2, rows, WIDTH), low),
            ((2 * heads, rows, VDIM), low),
            ((heads, rows, rows), full),
            ((heads, rows, rows), full),
        ],
        "local_scores",
    )(index, docs, *inputs, *latents)


def attention(index, doc_ids, inputs, kept, latents, heads, steps, ranks, in_place):
    rows = inputs[0].shape[0]
    low, full = jnp.bfloat16, jnp.float32
    count = len(LOCAL) * heads
    window = (REACH + 2) * rows
    far = REACH * rows
    half = (LATENT // 2, steps * heads * KV)
    return call(
        functools.partial(main_kernel, ranks),
        steps,
        2 * steps * heads * rows * rows * (5 * (QK + VDIM) + 8 * (2 * QK + VDIM) + 13 * KV),
        [
            SCALARS, *head_specs(rows, heads, steps, in_place), ANYWHERE, ANYWHERE,
            step_block(2 * heads, rows, QK), step_block(2 * heads, 8, rows),
            step_block(count, 8, rows), fixed(2, 8, rows),
        ]
        + [ANYWHERE] * len(latents),
        [(step_cols(rows, heads * QK), (rows, steps * heads * QK), low)] * 2
        + [(step_cols(LATENT // 2, heads * KV), half, low)] * 2
        + [(ANYWHERE, (WIDTH, rows), low)] * (REACH + 2),
        [
            ((2, rows, heads * QK), low),
            ((2, rows, heads * VDIM), low),
            ((far, WIDTH), low),
            ((WIDTH, window), low),
            ((heads, far, rows), low),
            ((heads, far, rows), low),
            ((heads, far, QK), low),
            ((heads, far, VDIM), low),
            ((heads, REACH, 8, rows), full),
            ((heads, 8, rows), full),
            ((heads, 8, rows), full),
            ((heads, rows, rows), full),
            ((heads, rows, rows), full),
            ((heads, rows, rows), low),
            ((heads, rows, rows), low),
            ((2, heads * QK, rows), full),
            ((REACH + 2, heads * KV, rows), full),
            ((LATENT, heads * KV), full),
            ((WIDTH, window), full),
            ((REACH + 2, ROPE, rows), full),
            ((count, rows, rows), low),
            ((count, rows, rows), low),
            pltpu.SemaphoreType.DMA((5,)),
            pltpu.SemaphoreType.DMA((2,)),
        ],
        "attention",
    )(index, doc_ids, *inputs, *kept, *latents)


def permute(value, axis, target):
    count = lax.axis_size(axis)
    pairs = [(s, target(s)) for s in range(count) if 0 <= target(s) < count]
    return lax.ppermute(value, axis, pairs)


def local(kv_latent, queries, grad_out, kv_up_weight, doc_ids):
    ranks = lax.axis_size("ctx")
    position = lax.axis_index("ctx").astype(jnp.int32)
    index, core = position[None], lax.rem(position, 2)
    low, full = jnp.bfloat16, jnp.float32
    docs = doc_ids[None]
    core_heads = kv_up_weight.shape[1] // KV // 2
    heads = min(2, core_heads)
    steps = core_heads // heads

    def own_heads(value, which):
        size = value.shape[1] // 2
        return lax.dynamic_slice_in_dim(value, which * size, size, axis=1)

    def across(value):
        return permute(value, "ctx", lambda s: s ^ 1)

    latent = kv_latent.T
    far = permute(latent, "ctx", lambda s: s + 2)
    mixed = permute(latent, "ctx", lambda s: s + 3 if s % 2 else -1)
    other = across(latent)
    in_place = heads * QK % 128 == 0
    inputs = (
        queries if in_place else own_heads(queries, core),
        grad_out if in_place else own_heads(grad_out, core),
        across(own_heads(queries, 1 - core)),
        across(own_heads(grad_out, 1 - core)),
        kv_up_weight if in_place else own_heads(kv_up_weight, core),
    )
    *kept, starts = local_scores(index, docs, inputs, (latent, other), heads, steps, in_place)
    far, mixed, starts = lax.optimization_barrier((far, mixed, starts))
    swapped = across(far)
    passed = permute(mixed, "ctx", lambda s: -1 if s % 2 else s + 1)

    dq_own, dq_other, keep, send, to_old, to_far, to_swap, mine, to_other = attention(
        index, doc_ids, inputs, (*kept, starts),
        (far, swapped, mixed, passed, latent, other), heads, steps, ranks, in_place,
    )

    head, head_count = lax.axis_index("head"), lax.axis_size("head")
    share = WIDTH // head_count

    def turned(value, turn):
        turns = [(s, (s + turn) % head_count) for s in range(head_count)]
        return lax.ppermute(value, "head", turns)

    def head_share(value):
        def rows_of(which):
            return lax.dynamic_slice_in_dim(value, which * share, share, axis=0)

        total = rows_of(head).astype(full)
        for turn in range(1, head_count):
            target = lax.rem(head + turn, head_count)
            total = total + turned(rows_of(target), turn).astype(full)
        return total

    from_x = permute(send, "ctx", lambda s: s ^ 2)
    from_swap = across(to_swap)
    from_old = permute(to_old, "ctx", lambda s: s - 1 if s % 2 else -1)
    from_other = across(to_other)
    far_sum = head_share((to_far.astype(full) + from_swap.astype(full)).astype(low)).astype(low)
    old_sum = head_share((to_old.astype(full) + from_old.astype(full)).astype(low)).astype(low)
    from_far = permute(far_sum, "ctx", lambda s: s - 2)
    from_mixed = permute(old_sum, "ctx", lambda s: -1 if s % 2 else s - 3)
    total = head_share((mine.astype(full) + from_other.astype(full)).astype(low))

    from_x, *_ = lax.optimization_barrier((from_x, far_sum, old_sum))
    plane = (keep.astype(full) + from_x.astype(full)).astype(low)
    columns = [list(range(first, ranks, 4)) for first in range(4)]
    pieces = lax.all_to_all(plane, "ctx", 0, 0, axis_index_groups=columns, tiled=True)
    rows = LATENT // ranks
    summed = jnp.sum(pieces.reshape(ranks // 4, 2 * rows, -1).astype(full), axis=0)

    def in_order(own, received):
        first = jnp.where(core == 0, own, received)
        second = jnp.where(core == 0, received, own)
        return jnp.concatenate([first, second], axis=1)

    rows_own = lax.dynamic_slice_in_dim(summed, core * rows, rows, axis=0)
    rows_other = lax.dynamic_slice_in_dim(summed, (1 - core) * rows, rows, axis=0)
    grad_weight = in_order(rows_own, across(rows_other))
    grad_queries = in_order(dq_own, across(dq_other))

    total = (total + from_mixed.astype(full) + from_far.astype(full)).astype(low)
    shares = [total] + [turned(total, turn) for turn in range(1, head_count)]
    ordered = []
    for place in range(head_count):
        picked = shares[0]
        for turn in range(1, head_count):
            picked = jnp.where(lax.rem(head - place + head_count, head_count) == turn, shares[turn], picked)
        ordered.append(picked)
    return grad_queries, jnp.concatenate(ordered, axis=0).T, grad_weight


def solution(mesh):
    return jax.shard_map(
        local,
        mesh=mesh,
        in_specs=(P("ctx", None), P("ctx", "head"), P("ctx", "head"), P(None, "head"), P()),
        out_specs=(P("ctx", "head"), P("ctx", None), P("ctx", "head")),
        check_vma=False,
    )
```

profile of v0, /device:TPU:0, one launch (start us, length us, event | category | flops | bytes accessed | tf_op | source)
XLA Modules:
  0.0 124.7 jit_solution(9471738311342460464)
XLA Ops:
  0.6 0.0 copy-start
  0.7 1.3 %constant_dynamic-slice_fusion.5 = bf16[512,768]{1,0:T(8,128)(2,1)S(1)} fusion(bf16[512,1536]{1,0:T(8,128)(2,1)} %q0.3, s32[]{:T(128)S(6)} %select_n.61), kind=kLoop, calls=%fused_computation.22 | loop fusion | bytes 1572868 | tf_op jit(solution)/shard_map/dynamic_slice | solution.py:588
  1.9 0.5 collective-permute-start
  2.4 0.1 collective-permute-start.2
  2.5 5.6 %collective-permute-start.3 = (bf16[576,512]{1,0:T(8,128)(2,1)}, bf16[576,512]{1,0:T(8,128)(2,1)}, u32[]{:S(2)}, u32[]{:S(2)}) collective-permute-start(bf16[576,512]{1,0:T(8,128)(2,1)} %bitcast.7), channel_id=1, source_target_pairs={{0,4},{2,6},{4,8},{6,10},{8,12},{10,14},{12,16},{14,18},{16,20},{1... | collective-permute-start | bytes 1769480 | tf_op jit(solution)/shard_map/ppermute | solution.py:573
  8.2 1.5 %collective-permute-start.4 = (bf16[576,512]{1,0:T(8,128)(2,1)}, bf16[576,512]{1,0:T(8,128)(2,1)}, u32[]{:S(2)}, u32[]{:S(2)}) collective-permute-start(bf16[576,512]{1,0:T(8,128)(2,1)} %bitcast.8), channel_id=1, source_target_pairs={{2,8},{6,12},{10,16},{14,20},{18,24},{22,28},{3,9},{7,13},{11,17},... | collective-permute-start | bytes 1769480 | tf_op jit(solution)/shard_map/ppermute | solution.py:573
  9.7 2.2 %collective-permute-start.1 = (bf16[512,512]{1,0:T(8,128)(2,1)S(1)}, bf16[512,512]{1,0:T(8,128)(2,1)S(1)}, u32[]{:S(2)}, u32[]{:S(2)}) collective-permute-start(bf16[512,512]{1,0:T(8,128)(2,1)S(1)} %constant_dynamic-slice_fusion.4), channel_id=1, source_target_pairs={{0,2},{2,0},{4,6},{6,4},{8,10},{10,8},{12,14},{14,12},{16,18},{18,... | collective-permute-start | bytes 1572872 | tf_op jit(solution)/shard_map/ppermute | solution.py:573
  11.9 1.5 %collective-permute-done.1.do1 = bf16[512,512]{1,0:T(8,128)(2,1)S(1)} collective-permute-done((bf16[512,512]{1,0:T(8,128)(2,1)S(1)}, bf16[512,512]{1,0:T(8,128)(2,1)S(1)}, u32[]{:S(2)}, u32[]{:S(2)}) %collective-permute-start.1) | collective-permute-done | bytes 524320 | tf_op jit(solution)/shard_map/ppermute | solution.py:573
  13.5 0.0 collective-permute-done.q1
  13.5 0.0 copy-start.1
  13.5 0.8 copy-done.6
  14.3 0.2 copy-done.3
  14.4 0.3 copy-done.1
  14.7 13.4 %local_scores.1 = (bf16[2,6,512,512]{3,2,1,0:T(8,128)(2,1)}, bf16[2,6,512,512]{3,2,1,0:T(8,128)(2,1)}, bf16[2,4,512,192]{3,2,1,0:T(8,128)(2,1)}, f32[2,4,8,512]{...) custom-call(s32[1]{0:T(128)} %bitcast.index_ref, s32[1,8192]{1,0:T(1,128)} %bitcast.11, ...), custom_call_target="tpu_custom_call" | custom-call | flops 1048576 | bytes 16777216 | tf_op jit(solution)/shard_map/local_scores/pallas_call | solution.py:492
  28.1 0.4 collective-permute-start.5
  28.5 2.3 %collective-permute-start.6 = (bf16[576,512]{1,0:T(8,128)(2,1)}, bf16[576,512]{1,0:T(8,128)(2,1)S(1)}, u32[]{:S(2)}, u32[]{:S(2)}) collective-permute-start(bf16[576,512]{1,0:T(8,128)(2,1)} %collective-permute-done.4.lat_mixed), channel_id=1, source_target_pairs={{0,2},{4,6},{8,10},{12,14},{16,18},{20,22},{24,26},{28,30},{1,3},{... | collective-permute-start | bytes 1769480 | tf_op jit(solution)/shard_map/ppermute | solution.py:573
  30.8 1.6 %collective-permute-done.6.lat_passed = bf16[576,512]{1,0:T(8,128)(2,1)S(1)} collective-permute-done((bf16[576,512]{1,0:T(8,128)(2,1)}, bf16[576,512]{1,0:T(8,128)(2,1)S(1)}, u32[]{:S(2)}, u32[]{:S(2)}) %collective-permute-start.6) | collective-permute-done | bytes 589856 | tf_op jit(solution)/shard_map/ppermute | solution.py:573
  32.4 0.8 copy-done.9
  33.2 25.5 %attention.1 = (bf16[512,768]{1,0:T(8,128)(2,1)}, bf16[512,768]{1,0:T(8,128)(2,1)}, bf16[256,1024]{1,0:T(8,128)(2,1)}, bf16[256,1024]{1,0:T(8,128)(2,1)}, bf16[5...) custom-call(s32[1]{0:T(128)} %bitcast.index_ref, ...), custom_call_target="tpu_custom_call" | custom-call | flops 18924699648 | bytes 16777216 | tf_op jit(solution)/shard_map/attention/pallas_call | solution.py:527
  58.8 1.6 %collective-permute-start.10 = (bf16[576,512]{1,0:T(8,128)(2,1)}, bf16[576,512]{1,0:T(8,128)(2,1)S(1)}, u32[]{:S(2)}, u32[]{:S(2)}) collective-permute-start(bf16[576,512]{1,0:T(8,128)(2,1)} %get-tuple-element.35), channel_id=1, source_target_pairs={{2,0},{6,4},{10,8},{14,12},{18,16},{22,20},{26,24},{30,28},{3,1},{... | collective-permute-start | bytes 1769480 | tf_op jit(solution)/shard_map/ppermute | solution.py:573
  60.4 1.2 collective-permute-start.13
  61.6 12.4 %collective-permute-start.17 = (bf16[256,1024]{1,0:T(8,128)(2,1)}, bf16[256,1024]{1,0:T(8,128)(2,1)S(1)}, u32[]{:S(2)}, u32[]{:S(2)}) collective-permute-start(bf16[256,1024]{1,0:T(8,128)(2,1)} %get-tuple-element.39), channel_id=1, source_target_pairs={{0,4},{2,6},{4,0},{6,2},{8,12},{10,14},{12,8},{14,10},{16,20},{18,... | collective-permute-start | bytes 1572872 | tf_op jit(solution)/shard_map/ppermute | solution.py:573
  74.1 0.5 collective-permute-start.7
  74.6 1.2 add_convert_fusion.1
  75.8 1.6 %collective-permute-start.11 = (bf16[288,512]{1,0:T(8,128)(2,1)S(1)}, bf16[288,512]{1,0:T(8,128)(2,1)S(1)}, u32[]{:S(2)}, u32[]{:S(2)}) collective-permute-start(bf16[288,512]{1,0:T(8,128)(2,1)S(1)} %constant_dynamic-slice_fusion.2), channel_id=1, source_target_pairs={{0,1},{1,0},{2,3},{3,2},{4,5},{5,4},{6,7},{7,6},{8,9},{9,8},{10,11... | collective-permute-start | bytes 884744 | tf_op jit(solution)/shard_map/ppermute | solution.py:620
  77.4 0.2 add_convert_fusion
  77.6 0.6 collective-permute-start.14
  78.2 0.2 add_convert_fusion.2
  78.4 0.7 constant_dynamic-slice_fusion.3
  79.1 1.5 %collective-permute-start.9 = (bf16[288,512]{1,0:T(8,128)(2,1)}, bf16[288,512]{1,0:T(8,128)(2,1)}, u32[]{:S(2)}, u32[]{:S(2)}) collective-permute-start(bf16[288,512]{1,0:T(8,128)(2,1)} %constant_dynamic-slice_fusion.3), channel_id=1, source_target_pairs={{0,1},{1,0},{2,3},{3,2},{4,5},{5,4},{6,7},{7,6},{8,9},{9,8},{10,11... | collective-permute-start | bytes 884744 | tf_op jit(solution)/shard_map/ppermute | solution.py:620
  80.6 5.2 %collective-permute-done.11 = bf16[288,512]{1,0:T(8,128)(2,1)S(1)} collective-permute-done((bf16[288,512]{1,0:T(8,128)(2,1)S(1)}, bf16[288,512]{1,0:T(8,128)(2,1)S(1)}, u32[]{:S(2)}, u32[]{:S(2)}) %collective-permute-start.11) | collective-permute-done | bytes 294944 | tf_op jit(solution)/shard_map/ppermute | solution.py:620
  85.8 0.1 add_convert_fusion.6
  85.9 1.5 %collective-permute-start.12 = (bf16[288,512]{1,0:T(8,128)(2,1)S(1)}, bf16[288,512]{1,0:T(8,128)(2,1)}, u32[]{:S(2)}, u32[]{:S(2)}) collective-permute-start(bf16[288,512]{1,0:T(8,128)(2,1)S(1)} %add_convert_fusion.6), channel_id=1, source_target_pairs={{8,2},{12,6},{16,10},{20,14},{24,18},{28,22},{9,3},{13,7},{17,11},... | collective-permute-start | bytes 884744 | tf_op jit(solution)/shard_map/ppermute | solution.py:573
  87.4 4.7 %collective-permute-done.14 = bf16[288,512]{1,0:T(8,128)(2,1)S(1)} collective-permute-done((bf16[288,512]{1,0:T(8,128)(2,1)S(1)}, bf16[288,512]{1,0:T(8,128)(2,1)S(1)}, u32[]{:S(2)}, u32[]{:S(2)}) %collective-permute-start.14) | collective-permute-done | bytes 294944 | tf_op jit(solution)/shard_map/ppermute | solution.py:620
  92.1 0.1 add_convert_fusion.5
  92.2 1.3 %collective-permute-start.15 = (bf16[288,512]{1,0:T(8,128)(2,1)S(1)}, bf16[288,512]{1,0:T(8,128)(2,1)}, u32[]{:S(2)}, u32[]{:S(2)}) collective-permute-start(bf16[288,512]{1,0:T(8,128)(2,1)S(1)} %add_convert_fusion.5), channel_id=1, source_target_pairs={{4,0},{6,2},{8,4},{10,6},{12,8},{14,10},{16,12},{18,14},{20,16},{2... | collective-permute-start | bytes 884744 | tf_op jit(solution)/shard_map/ppermute | solution.py:573
  93.5 1.0 add_convert_fusion.3
  94.5 13.9 %all-to-all-start = ((bf16[4,64,1024]{2,1,0:T(8,128)(2,1)}), bf16[4,64,1024]{2,1,0:T(8,128)(2,1)S(1)}, u32[]{:S(2)}, u32[]{:S(2)}) async-start(bf16[4,64,1024]{2,1,0:T(8,128)(2,1)} %bitcast.4), calls=%async_computation | async-start | bytes 1048576 | tf_op jit(solution)/shard_map/all_to_all | solution.py:645
  108.4 0.1 broadcast_select_fusion.1
  108.6 1.3 %add_convert_fusion.4 = bf16[288,512]{1,0:T(8,128)(2,1)S(1)} fusion(bf16[288,512]{1,0:T(8,128)(2,1)} %collective-permute-done.15, bf16[288,512]{1,0:T(8,128)(2,1)} %collective-permute-done.12, bf16[288,512]{1,0:T(8,128)(2,1)} %collective-permute-done.9, bf16[576,512]{1,0:T(8,128)(2,1)S(1)} %add_convert_fusion.2, s32[]{:T(128)S(6)} %select_n.66), kind=kLoop, calls=%fused_computation.9 | loop fusion | flops 1179648 | bytes 1474564 | tf_op jit(solution)/shard_map/convert_element_type | solution.py:659
  109.9 1.6 %collective-permute-start.16 = (bf16[288,512]{1,0:T(8,128)(2,1)S(1)}, bf16[288,512]{1,0:T(8,128)(2,1)S(1)}, u32[]{:S(2)}, u32[]{:S(2)}) collective-permute-start(bf16[288,512]{1,0:T(8,128)(2,1)S(1)} %add_convert_fusion.4), channel_id=1, source_target_pairs={{0,1},{1,0},{2,3},{3,2},{4,5},{5,4},{6,7},{7,6},{8,9},{9,8},{10,11... | collective-permute-start | bytes 884744 | tf_op jit(solution)/shard_map/ppermute | solution.py:620
  111.4 1.3 %pad_maximum_fusion = bf16[512,1536]{1,0:T(8,128)(2,1)} fusion(bf16[512,768]{1,0:T(8,128)(2,1)S(1)} %get-tuple-element.42, bf16[512,768]{1,0:T(8,128)(2,1)S(1)} %get-tuple-element.41), kind=kLoop, calls=%fused_computation | loop fusion | flops 3145728 | bytes 3145728 | tf_op jit(solution)/shard_map/concatenate | solution.py:652
  112.7 9.7 %all-to-all-done = bf16[4,64,1024]{2,1,0:T(8,128)(2,1)S(1)} async-done(((bf16[4,64,1024]{2,1,0:T(8,128)(2,1)}), bf16[4,64,1024]{2,1,0:T(8,128)(2,1)S(1)}, u32[]{:S(2)}, u32[]{:S(2)}) %all-to-all-start) | async-done | bytes 524320 | tf_op jit(solution)/shard_map/all_to_all | solution.py:645
  122.4 0.1 convert_reduce_fusion
  122.5 0.1 collective-permute-start.18
  122.7 0.9 maximum_bitcast_fusion
  123.5 0.4 collective-permute-done.18
  124.0 0.7 pad_maximum_fusion.1
  (34 shorter events, 0.2 us)
Async XLA Ops:
  0.6 9.1 %copy-start = (bf16[512,1024]{1,0:T(8,128)(2,1)S(1)}, bf16[512,1024]{1,0:T(8,128)(2,1)}, u32[]{:S(2)}) copy-start(bf16[512,1024]{1,0:T(8,128)(2,1)} %do0.3) | copy-start | bytes 3145732
  1.9 11.5 %collective-permute-start = (bf16[512,768]{1,0:T(8,128)(2,1)S(1)}, bf16[512,768]{1,0:T(8,128)(2,1)S(1)}, u32[]{:S(2)}, u32[]{:S(2)}) collective-permute-start(bf16[512,768]{1,0:T(8,128)(2,1)S(1)} %constant_dynamic-slice_fusion.5), channel_id=1, source_target_pairs={{0,2},{2,0},{4,6},{6,4},{8,10},{10,8},{12,14},{14,12},{16,18},{18,... | collective-permute-start | bytes 2359304 | tf_op jit(solution)/shard_map/ppermute | solution.py:573
  2.4 11.0 %collective-permute-start.2 = (bf16[576,512]{1,0:T(8,128)(2,1)}, bf16[576,512]{1,0:T(8,128)(2,1)S(1)}, u32[]{:S(2)}, u32[]{:S(2)}) collective-permute-start(bf16[576,512]{1,0:T(8,128)(2,1)} %bitcast.6), channel_id=1, source_target_pairs={{0,2},{2,0},{4,6},{6,4},{8,10},{10,8},{12,14},{14,12},{16,18},{18,... | collective-permute-start | bytes 1769480 | tf_op jit(solution)/shard_map/ppermute | solution.py:573
  2.5 25.6 %collective-permute-start.3 = (bf16[576,512]{1,0:T(8,128)(2,1)}, bf16[576,512]{1,0:T(8,128)(2,1)}, u32[]{:S(2)}, u32[]{:S(2)}) collective-permute-start(bf16[576,512]{1,0:T(8,128)(2,1)} %bitcast.7), channel_id=1, source_target_pairs={{0,4},{2,6},{4,8},{6,10},{8,12},{10,14},{12,16},{14,18},{16,20},{1... | collective-permute-start | bytes 1769480 | tf_op jit(solution)/shard_map/ppermute | solution.py:573
  8.2 19.9 %collective-permute-start.4 = (bf16[576,512]{1,0:T(8,128)(2,1)}, bf16[576,512]{1,0:T(8,128)(2,1)}, u32[]{:S(2)}, u32[]{:S(2)}) collective-permute-start(bf16[576,512]{1,0:T(8,128)(2,1)} %bitcast.8), channel_id=1, source_target_pairs={{2,8},{6,12},{10,16},{14,20},{18,24},{22,28},{3,9},{7,13},{11,17},... | collective-permute-start | bytes 1769480 | tf_op jit(solution)/shard_map/ppermute | solution.py:573
  9.7 3.7 %collective-permute-start.1 = (bf16[512,512]{1,0:T(8,128)(2,1)S(1)}, bf16[512,512]{1,0:T(8,128)(2,1)S(1)}, u32[]{:S(2)}, u32[]{:S(2)}) collective-permute-start(bf16[512,512]{1,0:T(8,128)(2,1)S(1)} %constant_dynamic-slice_fusion.4), channel_id=1, source_target_pairs={{0,2},{2,0},{4,6},{6,4},{8,10},{10,8},{12,14},{14,12},{16,18},{18,... | collective-permute-start | bytes 1572872 | tf_op jit(solution)/shard_map/ppermute | solution.py:573
  13.5 0.8 copy-start.6
  13.5 1.0 copy-start.3
  13.5 1.2 copy-start.1
  28.1 2.7 %collective-permute-start.5 = (bf16[576,512]{1,0:T(8,128)(2,1)}, bf16[576,512]{1,0:T(8,128)(2,1)S(1)}, u32[]{:S(2)}, u32[]{:S(2)}) collective-permute-start(bf16[576,512]{1,0:T(8,128)(2,1)} %collective-permute-done.3.lat_far), channel_id=1, source_target_pairs={{0,2},{2,0},{4,6},{6,4},{8,10},{10,8},{12,14},{14,12},{16,18},{18,... | collective-permute-start | bytes 1769480 | tf_op jit(solution)/shard_map/ppermute | solution.py:573
  28.5 3.9 %collective-permute-start.6 = (bf16[576,512]{1,0:T(8,128)(2,1)}, bf16[576,512]{1,0:T(8,128)(2,1)S(1)}, u32[]{:S(2)}, u32[]{:S(2)}) collective-permute-start(bf16[576,512]{1,0:T(8,128)(2,1)} %collective-permute-done.4.lat_mixed), channel_id=1, source_target_pairs={{0,2},{4,6},{8,10},{12,14},{16,18},{20,22},{24,26},{28,30},{1,3},{... | collective-permute-start | bytes 1769480 | tf_op jit(solution)/shard_map/ppermute | solution.py:573
  30.8 1.6 %copy-start.8 = (bf16[576,512]{1,0:T(8,128)(2,1)}, bf16[576,512]{1,0:T(8,128)(2,1)S(1)}, u32[]{:S(2)}) copy-start(bf16[576,512]{1,0:T(8,128)(2,1)S(1)} %collective-permute-done.5.lat_swap) | copy-start | bytes 1769476
  32.4 0.8 copy-start.9
  58.7 18.7 %copy-start.5 = (bf16[576,512]{1,0:T(8,128)(2,1)S(1)}, bf16[576,512]{1,0:T(8,128)(2,1)}, u32[]{:S(2)}) copy-start(bf16[576,512]{1,0:T(8,128)(2,1)} %get-tuple-element.36) | copy-start | bytes 1769476
  58.8 15.8 %collective-permute-start.10 = (bf16[576,512]{1,0:T(8,128)(2,1)}, bf16[576,512]{1,0:T(8,128)(2,1)S(1)}, u32[]{:S(2)}, u32[]{:S(2)}) collective-permute-start(bf16[576,512]{1,0:T(8,128)(2,1)} %get-tuple-element.35), channel_id=1, source_target_pairs={{2,0},{6,4},{10,8},{14,12},{18,16},{22,20},{26,24},{30,28},{3,1},{... | collective-permute-start | bytes 1769480 | tf_op jit(solution)/shard_map/ppermute | solution.py:573
  60.4 17.0 %collective-permute-start.13 = (bf16[576,512]{1,0:T(8,128)(2,1)}, bf16[576,512]{1,0:T(8,128)(2,1)S(1)}, u32[]{:S(2)}, u32[]{:S(2)}) collective-permute-start(bf16[576,512]{1,0:T(8,128)(2,1)} %get-tuple-element.37), channel_id=1, source_target_pairs={{0,2},{2,0},{4,6},{6,4},{8,10},{10,8},{12,14},{14,12},{16,18},{18,... | collective-permute-start | bytes 1769480 | tf_op jit(solution)/shard_map/ppermute | solution.py:573
  61.6 31.9 %collective-permute-start.17 = (bf16[256,1024]{1,0:T(8,128)(2,1)}, bf16[256,1024]{1,0:T(8,128)(2,1)S(1)}, u32[]{:S(2)}, u32[]{:S(2)}) collective-permute-start(bf16[256,1024]{1,0:T(8,128)(2,1)} %get-tuple-element.39), channel_id=1, source_target_pairs={{0,4},{2,6},{4,0},{6,2},{8,12},{10,14},{12,8},{14,10},{16,20},{18,... | collective-permute-start | bytes 1572872 | tf_op jit(solution)/shard_map/ppermute | solution.py:573
  74.1 4.1 %collective-permute-start.8 = (bf16[576,512]{1,0:T(8,128)(2,1)}, bf16[576,512]{1,0:T(8,128)(2,1)S(1)}, u32[]{:S(2)}, u32[]{:S(2)}) collective-permute-start(bf16[576,512]{1,0:T(8,128)(2,1)} %get-tuple-element.34), channel_id=1, source_target_pairs={{0,2},{2,0},{4,6},{6,4},{8,10},{10,8},{12,14},{14,12},{16,18},{18,... | collective-permute-start | bytes 1769480 | tf_op jit(solution)/shard_map/ppermute | solution.py:573
  74.1 34.3 %collective-permute-start.7 = (bf16[512,768]{1,0:T(8,128)(2,1)}, bf16[512,768]{1,0:T(8,128)(2,1)S(1)}, u32[]{:S(2)}, u32[]{:S(2)}) collective-permute-start(bf16[512,768]{1,0:T(8,128)(2,1)} %get-tuple-element.32), channel_id=1, source_target_pairs={{0,2},{2,0},{4,6},{6,4},{8,10},{10,8},{12,14},{14,12},{16,18},{18,... | collective-permute-start | bytes 2359304 | tf_op jit(solution)/shard_map/ppermute | solution.py:573
  75.8 2.4 %copy-start.4 = (bf16[576,512]{1,0:T(8,128)(2,1)S(1)}, bf16[576,512]{1,0:T(8,128)(2,1)}, u32[]{:S(2)}) copy-start(bf16[576,512]{1,0:T(8,128)(2,1)} %get-tuple-element.33) | copy-start | bytes 1769476
  75.8 9.9 %collective-permute-start.11 = (bf16[288,512]{1,0:T(8,128)(2,1)S(1)}, bf16[288,512]{1,0:T(8,128)(2,1)S(1)}, u32[]{:S(2)}, u32[]{:S(2)}) collective-permute-start(bf16[288,512]{1,0:T(8,128)(2,1)S(1)} %constant_dynamic-slice_fusion.2), channel_id=1, source_target_pairs={{0,1},{1,0},{2,3},{3,2},{4,5},{5,4},{6,7},{7,6},{8,9},{9,8},{10,11... | collective-permute-start | bytes 884744 | tf_op jit(solution)/shard_map/ppermute | solution.py:620
  77.6 14.5 %collective-permute-start.14 = (bf16[288,512]{1,0:T(8,128)(2,1)S(1)}, bf16[288,512]{1,0:T(8,128)(2,1)S(1)}, u32[]{:S(2)}, u32[]{:S(2)}) collective-permute-start(bf16[288,512]{1,0:T(8,128)(2,1)S(1)} %constant_dynamic-slice_fusion.1), channel_id=1, source_target_pairs={{0,1},{1,0},{2,3},{3,2},{4,5},{5,4},{6,7},{7,6},{8,9},{9,8},{10,11... | collective-permute-start | bytes 884744 | tf_op jit(solution)/shard_map/ppermute | solution.py:620
  78.4 15.1 %copy-start.7 = (bf16[256,1024]{1,0:T(8,128)(2,1)S(1)}, bf16[256,1024]{1,0:T(8,128)(2,1)}, u32[]{:S(2)}) copy-start(bf16[256,1024]{1,0:T(8,128)(2,1)} %get-tuple-element.38) | copy-start | bytes 1572868
  79.1 29.4 %collective-permute-start.9 = (bf16[288,512]{1,0:T(8,128)(2,1)}, bf16[288,512]{1,0:T(8,128)(2,1)}, u32[]{:S(2)}, u32[]{:S(2)}) collective-permute-start(bf16[288,512]{1,0:T(8,128)(2,1)} %constant_dynamic-slice_fusion.3), channel_id=1, source_target_pairs={{0,1},{1,0},{2,3},{3,2},{4,5},{5,4},{6,7},{7,6},{8,9},{9,8},{10,11... | collective-permute-start | bytes 884744 | tf_op jit(solution)/shard_map/ppermute | solution.py:620
  85.9 22.5 %copy-start.2 = (bf16[512,768]{1,0:T(8,128)(2,1)S(1)}, bf16[512,768]{1,0:T(8,128)(2,1)}, u32[]{:S(2)}) copy-start(bf16[512,768]{1,0:T(8,128)(2,1)} %get-tuple-element.31) | copy-start | bytes 2359300
  85.9 22.7 %collective-permute-start.12 = (bf16[288,512]{1,0:T(8,128)(2,1)S(1)}, bf16[288,512]{1,0:T(8,128)(2,1)}, u32[]{:S(2)}, u32[]{:S(2)}) collective-permute-start(bf16[288,512]{1,0:T(8,128)(2,1)S(1)} %add_convert_fusion.6), channel_id=1, source_target_pairs={{8,2},{12,6},{16,10},{20,14},{24,18},{28,22},{9,3},{13,7},{17,11},... | collective-permute-start | bytes 884744 | tf_op jit(solution)/shard_map/ppermute | solution.py:573
  92.2 16.4 %collective-permute-start.15 = (bf16[288,512]{1,0:T(8,128)(2,1)S(1)}, bf16[288,512]{1,0:T(8,128)(2,1)}, u32[]{:S(2)}, u32[]{:S(2)}) collective-permute-start(bf16[288,512]{1,0:T(8,128)(2,1)S(1)} %add_convert_fusion.5), channel_id=1, source_target_pairs={{4,0},{6,2},{8,4},{10,6},{12,8},{14,10},{16,12},{18,14},{20,16},{2... | collective-permute-start | bytes 884744 | tf_op jit(solution)/shard_map/ppermute | solution.py:573
  94.5 27.9 %all-to-all-start = ((bf16[4,64,1024]{2,1,0:T(8,128)(2,1)}), bf16[4,64,1024]{2,1,0:T(8,128)(2,1)S(1)}, u32[]{:S(2)}, u32[]{:S(2)}) async-start(bf16[4,64,1024]{2,1,0:T(8,128)(2,1)} %bitcast.4), calls=%async_computation | async-start | bytes 1048576 | tf_op jit(solution)/shard_map/all_to_all | solution.py:645
  109.9 12.7 %collective-permute-start.16 = (bf16[288,512]{1,0:T(8,128)(2,1)S(1)}, bf16[288,512]{1,0:T(8,128)(2,1)S(1)}, u32[]{:S(2)}, u32[]{:S(2)}) collective-permute-start(bf16[288,512]{1,0:T(8,128)(2,1)S(1)} %add_convert_fusion.4), channel_id=1, source_target_pairs={{0,1},{1,0},{2,3},{3,2},{4,5},{5,4},{6,7},{7,6},{8,9},{9,8},{10,11... | collective-permute-start | bytes 884744 | tf_op jit(solution)/shard_map/ppermute | solution.py:620
  122.5 1.4 %collective-permute-start.18 = (f32[32,1024]{1,0:T(8,128)S(1)}, f32[32,1024]{1,0:T(8,128)S(1)}, u32[]{:S(2)}, u32[]{:S(2)}) collective-permute-start(f32[32,1024]{1,0:T(8,128)S(1)} %constant_dynamic-slice_fusion), channel_id=1, source_target_pairs={{0,2},{2,0},{4,6},{6,4},{8,10},{10,8},{12,14},{14,12},{16,18},{18,... | collective-permute-start | bytes 393224 | tf_op jit(solution)/shard_map/ppermute | solution.py:573
where the time goes:
time: 126 us; the launch traced here: 125 us
  starting transfers between devices  50.5 us (40%)
  Pallas kernels  38.9 us (31%)
  waiting for transfers between devices  23.1 us (18%)
  other arithmetic  7.07 us (6%)
  local copies, waits for them, and re-layouts  4.21 us (3%)
    ppermute x15, starting transfers between devices, permute(): return lax.ppermute(value, axis, pairs)  31.3 us
    pallas_call x1, Pallas kernels, attention(): call(functools.partial(main_kernel, ranks), steps, 2 * steps * heads * ro...  25.5 us
    all_to_all x1, starting transfers between devices, local(): lax.all_to_all(plane, 'ctx', 0, 0, axis_index_groups=columns, tiled=True)  13.9 us
    pallas_call x1, Pallas kernels, local_scores(): call(local_kernel, steps, steps * heads * rows * rows, [fixed(1, docs.sha...  13.4 us
    ppermute x4, waiting for transfers between devices, turned(): return lax.ppermute(value, 'head', turns)  9.86 us
    all_to_all x1, waiting for transfers between devices, local(): lax.all_to_all(plane, 'ctx', 0, 0, axis_index_groups=columns, tiled=True)  9.71 us
    ppermute x4, starting transfers between devices, turned(): return lax.ppermute(value, 'head', turns)  5.26 us
    ppermute x15, waiting for transfers between devices, permute(): return lax.ppermute(value, axis, pairs)  3.57 us
  transfers between devices with their start and end apart: 20, of which 6 were waited for; matrix products, arithmetic and copies ran while one was open for 6% of the time, Pallas kernels for 11%

commit v1 on v0

--- a/solution.py
+++ b/solution.py
@@ -375,8 +375,21 @@
     def seen(t):
         return (t >= REACH) | active(0, t)
 
+    last = step == pl.num_programs(0) - 1
+    outs = ((x_old, x_old), (x_far, x_swap), (x_swap, x_far), (x_own, x_other), (x_other, x_own))
+
+    def out_copies(t):
+        part = slice(t * rows, (t + 1) * rows)
+        return [pltpu.make_async_copy(lat_t_ref.at[:, part], out, sems.at[t]) for out in outs[t]]
+
+    def leave(t):
+        part = slice(t * rows, (t + 1) * rows)
+        lat_t_ref[:, part] = x_acc[:, part].astype(lat_t_ref.dtype)
+        for parity, copy in enumerate(out_copies(t)):
+            pl.when(core == parity)(copy.start)
+
     def project(t, first):
-        part = block_rows(t)
+        part = slice(t * rows, (t + 1) * rows)
         grads = d_acc[t].astype(jnp.bfloat16)
         weight_part = dot(lat_t_ref[:LATENT, part], grads, NT)
         gw_acc[...] = weight_part if first else gw_acc[...] + weight_part
@@ -392,17 +405,18 @@
             x_acc[:LATENT, part] += latent_part
             x_acc[LATENT:, part] += r_acc[t]
 
-    @pl.when(step == 0)
-    def _():
-        def clear(t):
-            x_acc[:, block_rows(t)] = jnp.zeros((WIDTH, rows), jnp.float32)
-
-        loop(0, REACH, lambda t: ~seen(t), clear)
-
-    project(REACH, True)
-    loop(0, blocks, lambda t: seen(t) & (t != REACH), lambda t: project(t, False))
-    dq0_ref[...] = (dq_acc[core] * SCALE).T.astype(dq0_ref.dtype)
-    dq1_ref[...] = (dq_acc[1 - core] * SCALE).T.astype(dq1_ref.dtype)
+    def clear(t):
+        x_acc[:, t * rows : (t + 1) * rows] = jnp.zeros((WIDTH, rows), jnp.float32)
+
+    for n, t in enumerate((REACH, REACH + 1, *range(REACH))):
+        if t >= REACH:
+            project(t, n == 0)
+        else:
+            pl.when(seen(t))(functools.partial(project, t, False))
+            pl.when(~seen(t) & (step == 0))(functools.partial(clear, t))
+        pl.when(last)(functools.partial(leave, t))
+    dq0_ref[...] = (dq_acc[core] * SCALE).astype(dq0_ref.dtype).T
+    dq1_ref[...] = (dq_acc[1 - core] * SCALE).astype(dq1_ref.dtype).T
 
     share = 2 * (LATENT // ranks)
     own_x = lax.rem(index_ref[0] // 2, 2)
@@ -411,18 +425,10 @@
             source = pl.multiple_of((2 * i + x) * share, share)
             out[i * share : (i + 1) * share, :] = gw_acc[pl.ds(source, share), :].astype(out.dtype)
 
-    @pl.when(step == pl.num_programs(0) - 1)
+    @pl.when(last)
     def _():
-        places = ((x_old, 0), (x_far, 1 + core), (x_swap, 2 - core), (x_own, REACH + core),
-                  (x_other, REACH + 1 - core))
-        copies = []
-        for i, (out, t) in enumerate(places):
-            part = block_rows(t)
-            lat_t_ref[:, part] = x_acc[:, part].astype(lat_t_ref.dtype)
-            copies.append(pltpu.make_async_copy(lat_t_ref.at[:, part], out, sems.at[i]))
-            copies[-1].start()
-        for copy in copies:
-            copy.wait()
+        for t in range(blocks):
+            out_copies(t)[0].wait()
 
 
 def step_cols(height, size):
@@ -492,7 +498,7 @@
     return call(
         local_kernel,
         steps,
-        steps * heads * rows * rows,
+        2 * steps * heads * rows * rows * (3 * (QK + VDIM) + 2 * KV),
         [
             fixed(1, docs.shape[1]), *head_specs(rows, heads, steps, in_place),
             fixed(WIDTH, rows), fixed(WIDTH, rows),
@@ -615,18 +621,22 @@
     head, head_count = lax.axis_index("head"), lax.axis_size("head")
     share = WIDTH // head_count
 
-    def turned(value, turn):
-        turns = [(s, (s + turn) % head_count) for s in range(head_count)]
-        return lax.ppermute(value, "head", turns)
-
-    def head_share(value):
+    def turned(value, turn, ctx=range(ranks)):
+        turns = [
+            (c * head_count + s, c * head_count + (s + turn) % head_count)
+            for c in ctx
+            for s in range(head_count)
+        ]
+        return lax.ppermute(value, ("ctx", "head"), turns)
+
+    def head_share(value, ctx=range(ranks)):
         def rows_of(which):
             return lax.dynamic_slice_in_dim(value, which * share, share, axis=0)
 
         total = rows_of(head).astype(full)
         for turn in range(1, head_count):
             target = lax.rem(head + turn, head_count)
-            total = total + turned(rows_of(target), turn).astype(full)
+            total = total + turned(rows_of(target), turn, ctx).astype(full)
         return total
 
     from_x = permute(send, "ctx", lambda s: s ^ 2)
@@ -634,12 +644,15 @@
     from_old = permute(to_old, "ctx", lambda s: s - 1 if s % 2 else -1)
     from_other = across(to_other)
     far_sum = head_share((to_far.astype(full) + from_swap.astype(full)).astype(low)).astype(low)
-    old_sum = head_share((to_old.astype(full) + from_old.astype(full)).astype(low)).astype(low)
+    old_sum = (to_old.astype(full) + from_old.astype(full)).astype(low)
+    old_sum = head_share(old_sum, range(0, ranks, 2)).astype(low)
     from_far = permute(far_sum, "ctx", lambda s: s - 2)
     from_mixed = permute(old_sum, "ctx", lambda s: -1 if s % 2 else s - 3)
-    total = head_share((mine.astype(full) + from_other.astype(full)).astype(low))
-
-    from_x, *_ = lax.optimization_barrier((from_x, far_sum, old_sum))
+    own_sum = (mine.astype(full) + from_other.astype(full)).astype(low)
+    own_sum, *_ = lax.optimization_barrier((own_sum, far_sum))
+    total = head_share(own_sum)
+
+    from_x, *_ = lax.optimization_barrier((from_x, far_sum))
     plane = (keep.astype(full) + from_x.astype(full)).astype(low)
     columns = [list(range(first, ranks, 4)) for first in range(4)]
     pieces = lax.all_to_all(plane, "ctx", 0, 0, axis_index_groups=columns, tiled=True)

time: 126 us -> 128 us (1.016)
  the two profiles are of different devices: /device:TPU:0 before, /device:TPU:16 now
where the time goes in v1:
time: 128 us; the launch traced here: 126 us
  Pallas kernels  49 us (38%)
  starting transfers between devices  41.8 us (33%)
  waiting for transfers between devices  21.2 us (17%)
  other arithmetic  8.54 us (7%)
  local copies, waits for them, and re-layouts  4.03 us (3%)
    pallas_call x1, Pallas kernels, attention(): call(functools.partial(main_kernel, ranks), steps, 2 * steps * heads * ro...  35.7 us
    ppermute x15, starting transfers between devices, permute(): return lax.ppermute(value, axis, pairs)  29.1 us
    pallas_call x1, Pallas kernels, local_scores(): call(local_kernel, steps, 2 * steps * heads * rows * rows * (3 * (QK + VD...  13.4 us
    ppermute x4, waiting for transfers between devices, turned(): return lax.ppermute(value, ('ctx', 'head'), turns)  13 us
    ppermute x15, waiting for transfers between devices, permute(): return lax.ppermute(value, axis, pairs)  8.19 us
    ppermute x4, starting transfers between devices, turned(): return lax.ppermute(value, ('ctx', 'head'), turns)  7.16 us
    all_to_all x1, starting transfers between devices, local(): lax.all_to_all(plane, 'ctx', 0, 0, axis_index_groups=columns, tiled=True)  5.58 us
  transfers between devices with their start and end apart: 20, of which 5 were waited for; matrix products, arithmetic and copies ran while one was open for 7% of the time, Pallas kernels for 11%

profile of v1, /device:TPU:16, one launch (start us, length us, event | category | flops | bytes accessed | tf_op | source)
XLA Modules:
  0.0 125.6 jit_solution(10889922471594538049)
XLA Ops:
  0.6 0.0 copy-start.4
  0.6 0.0 copy-start.6
  0.7 1.3 %constant_dynamic-slice_fusion.5 = bf16[512,768]{1,0:T(8,128)(2,1)S(1)} fusion(bf16[512,1536]{1,0:T(8,128)(2,1)} %q0.3, s32[]{:T(128)S(6)} %select_n.61), kind=kLoop, calls=%fused_computation.22 | loop fusion | bytes 1572868 | tf_op jit(solution)/shard_map/dynamic_slice | solution.py:594
  2.0 0.1 collective-permute-start
  2.1 0.5 collective-permute-start.2
  2.6 0.1 collective-permute-start.1
  2.7 3.4 %collective-permute-start.3 = (bf16[576,512]{1,0:T(8,128)(2,1)S(1)}, bf16[576,512]{1,0:T(8,128)(2,1)S(1)}, u32[]{:S(2)}, u32[]{:S(2)}) collective-permute-start(bf16[576,512]{1,0:T(8,128)(2,1)S(1)} %bitcast.9), channel_id=1, source_target_pairs={{0,4},{2,6},{4,8},{6,10},{8,12},{10,14},{12,16},{14,18},{16,20},{1... | collective-permute-start | bytes 1769480 | tf_op jit(solution)/shard_map/ppermute | solution.py:579
  6.1 1.3 %collective-permute-start.4 = (bf16[576,512]{1,0:T(8,128)(2,1)S(1)}, bf16[576,512]{1,0:T(8,128)(2,1)S(1)}, u32[]{:S(2)}, u32[]{:S(2)}) collective-permute-start(bf16[576,512]{1,0:T(8,128)(2,1)S(1)} %bitcast.10), channel_id=1, source_target_pairs={{2,8},{6,12},{10,16},{14,20},{18,24},{22,28},{3,9},{7,13},{11,17},... | collective-permute-start | bytes 1769480 | tf_op jit(solution)/shard_map/ppermute | solution.py:579
  7.5 0.0 collective-permute-done.2.lat1.lat_other
  7.5 0.0 copy-start.5
  7.5 0.8 copy-done.11
  8.3 0.2 copy-done.5
  8.5 13.4 %local_scores.1 = (bf16[2,6,512,512]{3,2,1,0:T(8,128)(2,1)}, bf16[2,6,512,512]{3,2,1,0:T(8,128)(2,1)}, bf16[2,4,512,192]{3,2,1,0:T(8,128)(2,1)}, f32[2,4,8,512]{...) custom-call(s32[1]{0:T(128)} %bitcast.index_ref, s32[1,8192]{1,0:T(1,128)} %bitcast.11, ...), custom_call_target="tpu_custom_call" | custom-call | flops 3087007744 | bytes 16777216 | tf_op jit(solution)/shard_map/local_scores/pallas_call | solution.py:498
  21.9 0.0 copy-start.7
  21.9 2.3 %collective-permute-start.5 = (bf16[576,512]{1,0:T(8,128)(2,1)S(1)}, bf16[576,512]{1,0:T(8,128)(2,1)S(1)}, u32[]{:S(2)}, u32[]{:S(2)}) collective-permute-start(bf16[576,512]{1,0:T(8,128)(2,1)S(1)} %collective-permute-done.3.lat_far), channel_id=1, source_target_pairs={{0,2},{2,0},{4,6},{6,4},{8,10},{10,8},{12,14},{14,12},{16,18},{18,... | collective-permute-start | bytes 1769480 | tf_op jit(solution)/shard_map/ppermute | solution.py:579
  24.2 2.0 %collective-permute-start.6 = (bf16[576,512]{1,0:T(8,128)(2,1)S(1)}, bf16[576,512]{1,0:T(8,128)(2,1)S(1)}, u32[]{:S(2)}, u32[]{:S(2)}) collective-permute-start(bf16[576,512]{1,0:T(8,128)(2,1)S(1)} %collective-permute-done.4.lat_mixed), channel_id=1, source_target_pairs={{0,2},{4,6},{8,10},{12,14},{16,18},{20,22},{24,26},{28,30},{1,3},{... | collective-permute-start | bytes 1769480 | tf_op jit(solution)/shard_map/ppermute | solution.py:579
  26.2 1.6 %collective-permute-done.6.lat_passed = bf16[576,512]{1,0:T(8,128)(2,1)S(1)} collective-permute-done((bf16[576,512]{1,0:T(8,128)(2,1)S(1)}, bf16[576,512]{1,0:T(8,128)(2,1)S(1)}, u32[]{:S(2)}, u32[]{:S(2)}) %collective-permute-start.6) | collective-permute-done | bytes 589856 | tf_op jit(solution)/shard_map/ppermute | solution.py:579
  27.8 0.8 copy-done.10
  28.6 35.7 %attention.1 = (bf16[512,768]{1,0:T(8,128)(2,1)}, bf16[512,768]{1,0:T(8,128)(2,1)}, bf16[256,1024]{1,0:T(8,128)(2,1)}, bf16[256,1024]{1,0:T(8,128)(2,1)}, bf16[5...) custom-call(s32[1]{0:T(128)} %bitcast.index_ref, ...), custom_call_target="tpu_custom_call" | custom-call | flops 18924699648 | bytes 16777216 | tf_op jit(solution)/shard_map/attention/pallas_call | solution.py:533
  64.3 0.5 collective-permute-start.9
  64.8 1.3 %collective-permute-start.12 = (bf16[576,512]{1,0:T(8,128)(2,1)}, bf16[576,512]{1,0:T(8,128)(2,1)S(1)}, u32[]{:S(2)}, u32[]{:S(2)}) collective-permute-start(bf16[576,512]{1,0:T(8,128)(2,1)} %get-tuple-element.39), channel_id=1, source_target_pairs={{2,0},{6,4},{10,8},{14,12},{18,16},{22,20},{26,24},{30,28},{3,1},{... | collective-permute-start | bytes 1769480 | tf_op jit(solution)/shard_map/ppermute | solution.py:579
  66.1 13.5 %collective-permute-start.17 = (bf16[256,1024]{1,0:T(8,128)(2,1)}, bf16[256,1024]{1,0:T(8,128)(2,1)S(1)}, u32[]{:S(2)}, u32[]{:S(2)}) collective-permute-start(bf16[256,1024]{1,0:T(8,128)(2,1)} %get-tuple-element.41), channel_id=1, source_target_pairs={{0,4},{2,6},{4,0},{6,2},{8,12},{10,14},{12,8},{14,10},{16,20},{18,... | collective-permute-start | bytes 1572872 | tf_op jit(solution)/shard_map/ppermute | solution.py:579
  79.6 0.9 collective-permute-start.8
  80.4 1.2 add_convert_fusion.1
  81.7 1.6 %collective-permute-start.10 = (bf16[288,512]{1,0:T(8,128)(2,1)S(1)}, bf16[288,512]{1,0:T(8,128)(2,1)S(1)}, u32[]{:S(2)}, u32[]{:S(2)}) collective-permute-start(bf16[288,512]{1,0:T(8,128)(2,1)S(1)} %constant_dynamic-slice_fusion.3), channel_id=1, source_target_pairs={{0,1},{1,0},{2,3},{3,2},{4,5},{5,4},{6,7},{7,6},{8,9},{9,8},{10,11... | collective-permute-start | bytes 884744 | tf_op jit(solution)/shard_map/ppermute | solution.py:630
  83.3 0.2 add_convert_fusion
  83.5 0.8 constant_dynamic-slice_fusion.1
  84.2 2.4 %collective-permute-start.13 = (bf16[288,512]{1,0:T(8,128)(2,1)}, bf16[288,512]{1,0:T(8,128)(2,1)}, u32[]{:S(2)}, u32[]{:S(2)}) collective-permute-start(bf16[288,512]{1,0:T(8,128)(2,1)} %constant_dynamic-slice_fusion.1), channel_id=1, source_target_pairs={{0,1},{1,0},{4,5},{5,4},{8,9},{9,8},{12,13},{13,12},{16,17},{17,16... | collective-permute-start | bytes 884744 | tf_op jit(solution)/shard_map/ppermute | solution.py:630
  86.7 0.2 add_convert_fusion.2
  86.8 4.4 %collective-permute-done.10 = bf16[288,512]{1,0:T(8,128)(2,1)S(1)} collective-permute-done((bf16[288,512]{1,0:T(8,128)(2,1)S(1)}, bf16[288,512]{1,0:T(8,128)(2,1)S(1)}, u32[]{:S(2)}, u32[]{:S(2)}) %collective-permute-start.10) | collective-permute-done | bytes 294944 | tf_op jit(solution)/shard_map/ppermute | solution.py:630
  91.2 0.8 add_convert_fusion.6
  92.0 1.9 %collective-permute-start.15 = (bf16[288,512]{1,0:T(8,128)(2,1)}, bf16[288,512]{1,0:T(8,128)(2,1)}, u32[]{:S(2)}, u32[]{:S(2)}) collective-permute-start(bf16[288,512]{1,0:T(8,128)(2,1)} %add_convert_fusion.6), channel_id=1, source_target_pairs={{4,0},{6,2},{8,4},{10,6},{12,8},{14,10},{16,12},{18,14},{20,16},{2... | collective-permute-start | bytes 884744 | tf_op jit(solution)/shard_map/ppermute | solution.py:579
  93.9 1.0 add_convert_fusion.3
  94.9 5.6 %all-to-all-start = ((bf16[4,64,1024]{2,1,0:T(8,128)(2,1)}), bf16[4,64,1024]{2,1,0:T(8,128)(2,1)S(1)}, u32[]{:S(2)}, u32[]{:S(2)}) async-start(bf16[4,64,1024]{2,1,0:T(8,128)(2,1)} %bitcast.4), calls=%async_computation | async-start | bytes 1048576 | tf_op jit(solution)/shard_map/all_to_all | solution.py:658
  100.5 1.6 %collective-permute-start.11 = (bf16[288,512]{1,0:T(8,128)(2,1)S(1)}, bf16[288,512]{1,0:T(8,128)(2,1)S(1)}, u32[]{:S(2)}, u32[]{:S(2)}) collective-permute-start(bf16[288,512]{1,0:T(8,128)(2,1)S(1)} %constant_dynamic-slice_fusion.2), channel_id=1, source_target_pairs={{0,1},{1,0},{2,3},{3,2},{4,5},{5,4},{6,7},{7,6},{8,9},{9,8},{10,11... | collective-permute-start | bytes 884744 | tf_op jit(solution)/shard_map/ppermute | solution.py:630
  102.1 1.0 add_convert_fusion.5
  103.1 1.3 %collective-permute-start.14 = (bf16[288,512]{1,0:T(8,128)(2,1)S(1)}, bf16[288,512]{1,0:T(8,128)(2,1)S(1)}, u32[]{:S(2)}, u32[]{:S(2)}) collective-permute-start(bf16[288,512]{1,0:T(8,128)(2,1)S(1)} %add_convert_fusion.5), channel_id=1, source_target_pairs={{8,2},{12,6},{16,10},{20,14},{24,18},{28,22},{9,3},{13,7},{17,11},... | collective-permute-start | bytes 884744 | tf_op jit(solution)/shard_map/ppermute | solution.py:579
  104.5 0.1 broadcast_select_fusion.1
  104.6 3.7 %collective-permute-done.11 = bf16[288,512]{1,0:T(8,128)(2,1)S(1)} collective-permute-done((bf16[288,512]{1,0:T(8,128)(2,1)S(1)}, bf16[288,512]{1,0:T(8,128)(2,1)S(1)}, u32[]{:S(2)}, u32[]{:S(2)}) %collective-permute-start.11) | collective-permute-done | bytes 294944 | tf_op jit(solution)/shard_map/ppermute | solution.py:630
  108.3 6.6 %collective-permute-done.14 = bf16[288,512]{1,0:T(8,128)(2,1)S(1)} collective-permute-done((bf16[288,512]{1,0:T(8,128)(2,1)S(1)}, bf16[288,512]{1,0:T(8,128)(2,1)S(1)}, u32[]{:S(2)}, u32[]{:S(2)}) %collective-permute-start.14) | collective-permute-done | bytes 294944 | tf_op jit(solution)/shard_map/ppermute | solution.py:579
  114.9 1.1 add_convert_fusion.4
  116.0 1.6 %collective-permute-start.16 = (bf16[288,512]{1,0:T(8,128)(2,1)S(1)}, bf16[288,512]{1,0:T(8,128)(2,1)S(1)}, u32[]{:S(2)}, u32[]{:S(2)}) collective-permute-start(bf16[288,512]{1,0:T(8,128)(2,1)S(1)} %add_convert_fusion.4), channel_id=1, source_target_pairs={{0,1},{1,0},{2,3},{3,2},{4,5},{5,4},{6,7},{7,6},{8,9},{9,8},{10,11... | collective-permute-start | bytes 884744 | tf_op jit(solution)/shard_map/ppermute | solution.py:630
  117.6 1.3 %pad_maximum_fusion = bf16[512,1536]{1,0:T(8,128)(2,1)} fusion(bf16[512,768]{1,0:T(8,128)(2,1)S(1)} %get-tuple-element.44, bf16[512,768]{1,0:T(8,128)(2,1)S(1)} %get-tuple-element.43), kind=kLoop, calls=%fused_computation | loop fusion | flops 3145728 | bytes 3145728 | tf_op jit(solution)/shard_map/concatenate | solution.py:665
  118.9 0.1 convert_reduce_fusion
  119.0 0.1 collective-permute-start.18
  119.1 4.9 %collective-permute-done.16 = bf16[288,512]{1,0:T(8,128)(2,1)S(1)} collective-permute-done((bf16[288,512]{1,0:T(8,128)(2,1)S(1)}, bf16[288,512]{1,0:T(8,128)(2,1)S(1)}, u32[]{:S(2)}, u32[]{:S(2)}) %collective-permute-start.16) | collective-permute-done | bytes 294944 | tf_op jit(solution)/shard_map/ppermute | solution.py:630
  124.0 0.9 maximum_bitcast_fusion
  124.9 0.7 pad_maximum_fusion.1
  (38 shorter events, 0.2 us)
Async XLA Ops:
  0.6 1.9 %copy-start.4 = (bf16[512,1024]{1,0:T(8,128)(2,1)S(1)}, bf16[512,1024]{1,0:T(8,128)(2,1)}, u32[]{:S(2)}) copy-start(bf16[512,1024]{1,0:T(8,128)(2,1)} %do0.3) | copy-start | bytes 3145732
  0.6 2.1 %copy-start.6 = (bf16[512,576]{0,1:T(8,128)(2,1)S(1)}, bf16[512,576]{0,1:T(8,128)(2,1)}, u32[]{:S(2)}) copy-start(bf16[512,576]{0,1:T(8,128)(2,1)} %param.5) | copy-start | bytes 1769476
  2.0 5.5 %collective-permute-start = (bf16[512,768]{1,0:T(8,128)(2,1)S(1)}, bf16[512,768]{1,0:T(8,128)(2,1)S(1)}, u32[]{:S(2)}, u32[]{:S(2)}) collective-permute-start(bf16[512,768]{1,0:T(8,128)(2,1)S(1)} %constant_dynamic-slice_fusion.5), channel_id=1, source_target_pairs={{0,2},{2,0},{4,6},{6,4},{8,10},{10,8},{12,14},{14,12},{16,18},{18,... | collective-permute-start | bytes 2359304 | tf_op jit(solution)/shard_map/ppermute | solution.py:579
  2.1 5.4 %collective-permute-start.2 = (bf16[576,512]{1,0:T(8,128)(2,1)}, bf16[576,512]{1,0:T(8,128)(2,1)}, u32[]{:S(2)}, u32[]{:S(2)}) collective-permute-start(bf16[576,512]{1,0:T(8,128)(2,1)} %bitcast.6), channel_id=1, source_target_pairs={{0,2},{2,0},{4,6},{6,4},{8,10},{10,8},{12,14},{14,12},{16,18},{18,... | collective-permute-start | bytes 1769480 | tf_op jit(solution)/shard_map/ppermute | solution.py:579
  2.6 4.8 %collective-permute-start.1 = (bf16[512,512]{1,0:T(8,128)(2,1)S(1)}, bf16[512,512]{1,0:T(8,128)(2,1)S(1)}, u32[]{:S(2)}, u32[]{:S(2)}) collective-permute-start(bf16[512,512]{1,0:T(8,128)(2,1)S(1)} %constant_dynamic-slice_fusion.4), channel_id=1, source_target_pairs={{0,2},{2,0},{4,6},{6,4},{8,10},{10,8},{12,14},{14,12},{16,18},{18,... | collective-permute-start | bytes 1572872 | tf_op jit(solution)/shard_map/ppermute | solution.py:579
  2.7 19.1 %collective-permute-start.3 = (bf16[576,512]{1,0:T(8,128)(2,1)S(1)}, bf16[576,512]{1,0:T(8,128)(2,1)S(1)}, u32[]{:S(2)}, u32[]{:S(2)}) collective-permute-start(bf16[576,512]{1,0:T(8,128)(2,1)S(1)} %bitcast.9), channel_id=1, source_target_pairs={{0,4},{2,6},{4,8},{6,10},{8,12},{10,14},{12,16},{14,18},{16,20},{1... | collective-permute-start | bytes 1769480 | tf_op jit(solution)/shard_map/ppermute | solution.py:579
  6.1 15.7 %collective-permute-start.4 = (bf16[576,512]{1,0:T(8,128)(2,1)S(1)}, bf16[576,512]{1,0:T(8,128)(2,1)S(1)}, u32[]{:S(2)}, u32[]{:S(2)}) collective-permute-start(bf16[576,512]{1,0:T(8,128)(2,1)S(1)} %bitcast.10), channel_id=1, source_target_pairs={{2,8},{6,12},{10,16},{14,20},{18,24},{22,28},{3,9},{7,13},{11,17},... | collective-permute-start | bytes 1769480 | tf_op jit(solution)/shard_map/ppermute | solution.py:579
  7.4 0.8 copy-start.11
  7.5 1.0 copy-start.5
  21.9 5.9 %copy-start.7 = (bf16[576,512]{1,0:T(8,128)(2,1)}, bf16[576,512]{1,0:T(8,128)(2,1)S(1)}, u32[]{:S(2)}) copy-start(bf16[576,512]{1,0:T(8,128)(2,1)S(1)} %collective-permute-done.3.lat_far) | copy-start | bytes 1769476
  21.9 5.9 %copy-start.8 = (bf16[576,512]{1,0:T(8,128)(2,1)}, bf16[576,512]{1,0:T(8,128)(2,1)S(1)}, u32[]{:S(2)}) copy-start(bf16[576,512]{1,0:T(8,128)(2,1)S(1)} %collective-permute-done.4.lat_mixed) | copy-start | bytes 1769476
  21.9 4.3 %collective-permute-start.5 = (bf16[576,512]{1,0:T(8,128)(2,1)S(1)}, bf16[576,512]{1,0:T(8,128)(2,1)S(1)}, u32[]{:S(2)}, u32[]{:S(2)}) collective-permute-start(bf16[576,512]{1,0:T(8,128)(2,1)S(1)} %collective-permute-done.3.lat_far), channel_id=1, source_target_pairs={{0,2},{2,0},{4,6},{6,4},{8,10},{10,8},{12,14},{14,12},{16,18},{18,... | collective-permute-start | bytes 1769480 | tf_op jit(solution)/shard_map/ppermute | solution.py:579
  24.2 3.5 %collective-permute-start.6 = (bf16[576,512]{1,0:T(8,128)(2,1)S(1)}, bf16[576,512]{1,0:T(8,128)(2,1)S(1)}, u32[]{:S(2)}, u32[]{:S(2)}) collective-permute-start(bf16[576,512]{1,0:T(8,128)(2,1)S(1)} %collective-permute-done.4.lat_mixed), channel_id=1, source_target_pairs={{0,2},{4,6},{8,10},{12,14},{16,18},{20,22},{24,26},{28,30},{1,3},{... | collective-permute-start | bytes 1769480 | tf_op jit(solution)/shard_map/ppermute | solution.py:579
  26.2 1.6 %copy-start.9 = (bf16[576,512]{1,0:T(8,128)(2,1)}, bf16[576,512]{1,0:T(8,128)(2,1)S(1)}, u32[]{:S(2)}) copy-start(bf16[576,512]{1,0:T(8,128)(2,1)S(1)} %collective-permute-done.5.lat_swap) | copy-start | bytes 1769476
  27.8 0.8 copy-start.10
  64.3 19.0 %copy-start.2 = (bf16[576,512]{1,0:T(8,128)(2,1)S(1)}, bf16[576,512]{1,0:T(8,128)(2,1)}, u32[]{:S(2)}) copy-start(bf16[576,512]{1,0:T(8,128)(2,1)} %get-tuple-element.39) | copy-start | bytes 1769476
  64.3 16.2 %collective-permute-start.9 = (bf16[576,512]{1,0:T(8,128)(2,1)}, bf16[576,512]{1,0:T(8,128)(2,1)S(1)}, u32[]{:S(2)}, u32[]{:S(2)}) collective-permute-start(bf16[576,512]{1,0:T(8,128)(2,1)} %get-tuple-element.37), channel_id=1, source_target_pairs={{0,2},{2,0},{4,6},{6,4},{8,10},{10,8},{12,14},{14,12},{16,18},{18,... | collective-permute-start | bytes 1769480 | tf_op jit(solution)/shard_map/ppermute | solution.py:579
  64.8 18.5 %collective-permute-start.12 = (bf16[576,512]{1,0:T(8,128)(2,1)}, bf16[576,512]{1,0:T(8,128)(2,1)S(1)}, u32[]{:S(2)}, u32[]{:S(2)}) collective-permute-start(bf16[576,512]{1,0:T(8,128)(2,1)} %get-tuple-element.39), channel_id=1, source_target_pairs={{2,0},{6,4},{10,8},{14,12},{18,16},{22,20},{26,24},{30,28},{3,1},{... | collective-permute-start | bytes 1769480 | tf_op jit(solution)/shard_map/ppermute | solution.py:579
  66.1 27.8 %collective-permute-start.17 = (bf16[256,1024]{1,0:T(8,128)(2,1)}, bf16[256,1024]{1,0:T(8,128)(2,1)S(1)}, u32[]{:S(2)}, u32[]{:S(2)}) collective-permute-start(bf16[256,1024]{1,0:T(8,128)(2,1)} %get-tuple-element.41), channel_id=1, source_target_pairs={{0,4},{2,6},{4,0},{6,2},{8,12},{10,14},{12,8},{14,10},{16,20},{18,... | collective-permute-start | bytes 1572872 | tf_op jit(solution)/shard_map/ppermute | solution.py:579
  79.6 7.1 %collective-permute-start.8 = (bf16[576,512]{1,0:T(8,128)(2,1)}, bf16[576,512]{1,0:T(8,128)(2,1)S(1)}, u32[]{:S(2)}, u32[]{:S(2)}) collective-permute-start(bf16[576,512]{1,0:T(8,128)(2,1)} %get-tuple-element.35), channel_id=1, source_target_pairs={{0,2},{2,0},{4,6},{6,4},{8,10},{10,8},{12,14},{14,12},{16,18},{18,... | collective-permute-start | bytes 1769480 | tf_op jit(solution)/shard_map/ppermute | solution.py:579
  80.4 24.0 %collective-permute-start.7 = (bf16[512,768]{1,0:T(8,128)(2,1)}, bf16[512,768]{1,0:T(8,128)(2,1)S(1)}, u32[]{:S(2)}, u32[]{:S(2)}) collective-permute-start(bf16[512,768]{1,0:T(8,128)(2,1)} %get-tuple-element.33), channel_id=1, source_target_pairs={{0,2},{2,0},{4,6},{6,4},{8,10},{10,8},{12,14},{14,12},{16,18},{18,... | collective-permute-start | bytes 2359304 | tf_op jit(solution)/shard_map/ppermute | solution.py:579
  81.7 5.0 %copy-start.1 = (bf16[576,512]{1,0:T(8,128)(2,1)S(1)}, bf16[576,512]{1,0:T(8,128)(2,1)}, u32[]{:S(2)}) copy-start(bf16[576,512]{1,0:T(8,128)(2,1)} %get-tuple-element.34) | copy-start | bytes 1769476
  81.7 9.5 %collective-permute-start.10 = (bf16[288,512]{1,0:T(8,128)(2,1)S(1)}, bf16[288,512]{1,0:T(8,128)(2,1)S(1)}, u32[]{:S(2)}, u32[]{:S(2)}) collective-permute-start(bf16[288,512]{1,0:T(8,128)(2,1)S(1)} %constant_dynamic-slice_fusion.3), channel_id=1, source_target_pairs={{0,1},{1,0},{2,3},{3,2},{4,5},{5,4},{6,7},{7,6},{8,9},{9,8},{10,11... | collective-permute-start | bytes 884744 | tf_op jit(solution)/shard_map/ppermute | solution.py:630
  83.5 10.5 %copy-start.3 = (bf16[256,1024]{1,0:T(8,128)(2,1)S(1)}, bf16[256,1024]{1,0:T(8,128)(2,1)}, u32[]{:S(2)}) copy-start(bf16[256,1024]{1,0:T(8,128)(2,1)} %get-tuple-element.40) | copy-start | bytes 1572868
  84.2 17.9 %collective-permute-start.13 = (bf16[288,512]{1,0:T(8,128)(2,1)}, bf16[288,512]{1,0:T(8,128)(2,1)}, u32[]{:S(2)}, u32[]{:S(2)}) collective-permute-start(bf16[288,512]{1,0:T(8,128)(2,1)} %constant_dynamic-slice_fusion.1), channel_id=1, source_target_pairs={{0,1},{1,0},{4,5},{5,4},{8,9},{9,8},{12,13},{13,12},{16,17},{17,16... | collective-permute-start | bytes 884744 | tf_op jit(solution)/shard_map/ppermute | solution.py:630
  92.0 22.9 %collective-permute-start.15 = (bf16[288,512]{1,0:T(8,128)(2,1)}, bf16[288,512]{1,0:T(8,128)(2,1)}, u32[]{:S(2)}, u32[]{:S(2)}) collective-permute-start(bf16[288,512]{1,0:T(8,128)(2,1)} %add_convert_fusion.6), channel_id=1, source_target_pairs={{4,0},{6,2},{8,4},{10,6},{12,8},{14,10},{16,12},{18,14},{20,16},{2... | collective-permute-start | bytes 884744 | tf_op jit(solution)/shard_map/ppermute | solution.py:579
  94.9 9.6 %copy-start = (bf16[512,768]{1,0:T(8,128)(2,1)S(1)}, bf16[512,768]{1,0:T(8,128)(2,1)}, u32[]{:S(2)}) copy-start(bf16[512,768]{1,0:T(8,128)(2,1)} %get-tuple-element.32) | copy-start | bytes 2359300
  94.9 24.0 %all-to-all-start = ((bf16[4,64,1024]{2,1,0:T(8,128)(2,1)}), bf16[4,64,1024]{2,1,0:T(8,128)(2,1)S(1)}, u32[]{:S(2)}, u32[]{:S(2)}) async-start(bf16[4,64,1024]{2,1,0:T(8,128)(2,1)} %bitcast.4), calls=%async_computation | async-start | bytes 1048576 | tf_op jit(solution)/shard_map/all_to_all | solution.py:658
  100.5 7.8 %collective-permute-start.11 = (bf16[288,512]{1,0:T(8,128)(2,1)S(1)}, bf16[288,512]{1,0:T(8,128)(2,1)S(1)}, u32[]{:S(2)}, u32[]{:S(2)}) collective-permute-start(bf16[288,512]{1,0:T(8,128)(2,1)S(1)} %constant_dynamic-slice_fusion.2), channel_id=1, source_target_pairs={{0,1},{1,0},{2,3},{3,2},{4,5},{5,4},{6,7},{7,6},{8,9},{9,8},{10,11... | collective-permute-start | bytes 884744 | tf_op jit(solution)/shard_map/ppermute | solution.py:630
  103.1 11.8 %collective-permute-start.14 = (bf16[288,512]{1,0:T(8,128)(2,1)S(1)}, bf16[288,512]{1,0:T(8,128)(2,1)S(1)}, u32[]{:S(2)}, u32[]{:S(2)}) collective-permute-start(bf16[288,512]{1,0:T(8,128)(2,1)S(1)} %add_convert_fusion.5), channel_id=1, source_target_pairs={{8,2},{12,6},{16,10},{20,14},{24,18},{28,22},{9,3},{13,7},{17,11},... | collective-permute-start | bytes 884744 | tf_op jit(solution)/shard_map/ppermute | solution.py:579
  116.0 7.9 %collective-permute-start.16 = (bf16[288,512]{1,0:T(8,128)(2,1)S(1)}, bf16[288,512]{1,0:T(8,128)(2,1)S(1)}, u32[]{:S(2)}, u32[]{:S(2)}) collective-permute-start(bf16[288,512]{1,0:T(8,128)(2,1)S(1)} %add_convert_fusion.4), channel_id=1, source_target_pairs={{0,1},{1,0},{2,3},{3,2},{4,5},{5,4},{6,7},{7,6},{8,9},{9,8},{10,11... | collective-permute-start | bytes 884744 | tf_op jit(solution)/shard_map/ppermute | solution.py:630
  119.0 5.9 %collective-permute-start.18 = (f32[32,1024]{1,0:T(8,128)S(1)}, f32[32,1024]{1,0:T(8,128)S(1)}, u32[]{:S(2)}, u32[]{:S(2)}) collective-permute-start(f32[32,1024]{1,0:T(8,128)S(1)} %constant_dynamic-slice_fusion), channel_id=1, source_target_pairs={{0,2},{2,0},{4,6},{6,4},{8,10},{10,8},{12,14},{14,12},{16,18},{18,... | collective-permute-start | bytes 393224 | tf_op jit(solution)/shard_map/ppermute | solution.py:579

commit v2 on v1

--- a/solution.py
+++ b/solution.py
@@ -104,13 +104,13 @@
         second(*now)
 
 
-def grad_block(kept, key, top, end_ref, q_t, do_t, low_ref, ds_ref, dq_acc, d_acc, r_acc, first_q, first_k):
+def grad_block(kept, key, top, end_ref, q_ref, do_ref, low_ref, ds_ref, dq_acc, d_acc, r_acc, first_q, first_k):
     def put(ref, part, value, first):
-        ref[part, :] = value if first else ref[part, :] + value
-
-    rows = do_t.shape[1]
-    heads = do_t.shape[0] // VDIM
-    sums = {}
+        ref[:, part] = value if first else ref[:, part] + value
+
+    rows = do_ref.shape[0]
+    heads = do_ref.shape[1] // VDIM
+    sums, turned = {}, {}
 
     def weigh(h, first):
         for c in range(first, first + PIECE, LANES):
@@ -129,19 +129,21 @@
     def multiply(h, first):
         cols = slice(first, first + PIECE)
         low, dscore = low_ref[h, :, cols], ds_ref[h, :, cols]
-        dvalue = dot(do_t[head_cols(h, VDIM), cols], low, NT)
-        dkey = dot(q_t[head_cols(h, QK), cols], dscore, NT)
+        dvalue = dot(low, do_ref[cols, head_cols(h, VDIM)])
+        dkey = dot(dscore, q_ref[cols, head_cols(h, QK)])
         own = head_cols(h, QK)
-        dq = dot(key(h).T, dscore)
+        if not first:
+            turned[h] = key(h).T
+        dq = dot(turned[h], dscore)
         dq_acc[own, cols] = dq if first_q else dq_acc[own, cols] + dq
         if first:
             dvalue, dkey = sums[h][0] + dvalue, sums[h][1] + dkey
         sums[h] = dvalue, dkey
         if first + PIECE == rows:
             dkey = dkey * SCALE
-            put(d_acc, slice(h * KV, h * KV + NOPE), dkey[:NOPE], first_k)
+            put(d_acc, slice(h * KV, h * KV + NOPE), dkey[:, :NOPE], first_k)
             put(d_acc, slice(h * KV + NOPE, (h + 1) * KV), dvalue, first_k)
-            put(r_acc, slice(0, ROPE), dkey[NOPE:], first_k and h == 0)
+            put(r_acc, slice(0, ROPE), dkey[:, NOPE:], first_k and h == 0)
 
     alternate(rows, heads, weigh, multiply)
 
@@ -252,8 +254,6 @@
         pltpu.make_async_copy(all_e.at[step], local_e, kept_sems.at[0]),
         pltpu.make_async_copy(all_g.at[step], local_g, kept_sems.at[1]),
     ]
-    for copy in kept_copies:
-        copy.start()
     core, chip = chip_place(index_ref)
 
     def active(j, t):
@@ -293,12 +293,19 @@
             copy.start()
         pl.when(core == 0)(oldest.start)
         pl.when(core == 1)(passed.start)
+        for copy in kept_copies:
+            copy.start()
         for copy in copies:
             copy.wait()
         oldest.wait()
         for t in range(REACH):
             part = slice(t * rows, (t + 1) * rows)
             lat_ref[part, :] = lat_t_ref[:, part].T
+
+    @pl.when(step > 0)
+    def _():
+        for copy in kept_copies:
+            copy.start()
 
     order_pair(q_ref, core, q0, q1)
     order_pair(do_ref, core, do0, do1)
@@ -337,11 +344,10 @@
             end_ref[h, 0:1, :] = run_ref[h, 0:1, :]
             end_ref[h, 1:2, :] = inverse
             end_ref[h, 2:3, :] = run_ref[h, 2:3, :] * inverse
-        q_t, do_t = q_ref[j].T, do_ref[j].T
 
         def add(t, kept, key, top, first_q, first_k):
             grad_block(
-                kept, key, top, end_ref, q_t, do_t, low_ref, ds_ref, dq_acc.at[j], d_acc.at[t],
+                kept, key, top, end_ref, q_ref.at[j], do_ref.at[j], low_ref, ds_ref, dq_acc.at[j], d_acc.at[t],
                 r_acc.at[t], first_q, first_k,
             )
 
@@ -391,19 +397,20 @@
     def project(t, first):
         part = slice(t * rows, (t + 1) * rows)
         grads = d_acc[t].astype(jnp.bfloat16)
-        weight_part = dot(lat_t_ref[:LATENT, part], grads, NT)
+        weight_part = dot(lat_t_ref[:LATENT, part], grads)
         gw_acc[...] = weight_part if first else gw_acc[...] + weight_part
-        latent_part = dot(w_ref[...], grads)
+        latent_part = dot(w_ref[...], grads, NT)
+        rope_part = r_acc[t].T
 
         @pl.when(step == 0)
         def _():
             x_acc[:LATENT, part] = latent_part
-            x_acc[LATENT:, part] = r_acc[t]
+            x_acc[LATENT:, part] = rope_part
 
         @pl.when(step > 0)
         def _():
             x_acc[:LATENT, part] += latent_part
-            x_acc[LATENT:, part] += r_acc[t]
+            x_acc[LATENT:, part] += rope_part
 
     def clear(t):
         x_acc[:, t * rows : (t + 1) * rows] = jnp.zeros((WIDTH, rows), jnp.float32)
@@ -560,10 +567,10 @@
             ((heads, rows, rows), low),
             ((heads, rows, rows), low),
             ((2, heads * QK, rows), full),
-            ((REACH + 2, heads * KV, rows), full),
+            ((REACH + 2, rows, heads * KV), full),
             ((LATENT, heads * KV), full),
             ((WIDTH, window), full),
-            ((REACH + 2, ROPE, rows), full),
+            ((REACH + 2, rows, ROPE), full),
             ((count, rows, rows), low),
             ((count, rows, rows), low),
             pltpu.SemaphoreType.DMA((5,)),
@@ -652,7 +659,7 @@
     own_sum, *_ = lax.optimization_barrier((own_sum, far_sum))
     total = head_share(own_sum)
 
-    from_x, *_ = lax.optimization_barrier((from_x, far_sum))
+    from_x, *_ = lax.optimization_barrier((from_x, far_sum, old_sum))
     plane = (keep.astype(full) + from_x.astype(full)).astype(low)
     columns = [list(range(first, ranks, 4)) for first in range(4)]
     pieces = lax.all_to_all(plane, "ctx", 0, 0, axis_index_groups=columns, tiled=True)

time: 128 us -> 123 us (0.961)
  the two profiles are of different devices: /device:TPU:16 before, /device:TPU:0 now
where the time goes in v2:
time: 123 us; the launch traced here: 122 us
  starting transfers between devices  53.4 us (43%)
  Pallas kernels  37 us (30%)
  waiting for transfers between devices  20.4 us (17%)
  other arithmetic  6.97 us (6%)
  local copies, waits for them, and re-layouts  3.32 us (3%)
    ppermute x15, starting transfers between devices, permute(): return lax.ppermute(value, axis, pairs)  29.5 us
    pallas_call x1, Pallas kernels, attention(): call(functools.partial(main_kernel, ranks), steps, 2 * steps * heads * ro...  23.7 us
    ppermute x4, waiting for transfers between devices, turned(): return lax.ppermute(value, ('ctx', 'head'), turns)  18.8 us
    all_to_all x1, starting transfers between devices, local(): lax.all_to_all(plane, 'ctx', 0, 0, axis_index_groups=columns, tiled=True)  16.5 us
    pallas_call x1, Pallas kernels, local_scores(): call(local_kernel, steps, 2 * steps * heads * rows * rows * (3 * (QK + VD...  13.3 us
    ppermute x4, starting transfers between devices, turned(): return lax.ppermute(value, ('ctx', 'head'), turns)  7.3 us
  transfers between devices with their start and end apart: 20, of which 5 were waited for; matrix products, arithmetic and copies ran while one was open for 5% of the time, Pallas kernels for 11%

profile of v2, /device:TPU:0, one launch (start us, length us, event | category | flops | bytes accessed | tf_op | source)
XLA Modules:
  0.0 122.0 jit_solution(1261571045526031805)
XLA Ops:
  0.6 0.0 copy-start.4
  0.6 0.0 copy-start.6
  0.7 1.3 %constant_dynamic-slice_fusion.5 = bf16[512,768]{1,0:T(8,128)(2,1)S(1)} fusion(bf16[512,1536]{1,0:T(8,128)(2,1)} %q0.3, s32[]{:T(128)S(6)} %select_n.61), kind=kLoop, calls=%fused_computation.22 | loop fusion | bytes 1572868 | tf_op jit(solution)/shard_map/dynamic_slice | solution.py:601
  2.0 0.5 collective-permute-start
  2.5 0.1 collective-permute-start.2
  2.6 0.5 collective-permute-start.1
  3.1 4.5 %collective-permute-start.3 = (bf16[576,512]{1,0:T(8,128)(2,1)S(1)}, bf16[576,512]{1,0:T(8,128)(2,1)S(1)}, u32[]{:S(2)}, u32[]{:S(2)}) collective-permute-start(bf16[576,512]{1,0:T(8,128)(2,1)S(1)} %bitcast.9), channel_id=1, source_target_pairs={{0,4},{2,6},{4,8},{6,10},{8,12},{10,14},{12,16},{14,18},{16,20},{1... | collective-permute-start | bytes 1769480 | tf_op jit(solution)/shard_map/ppermute | solution.py:586
  7.6 0.7 collective-permute-start.4
  8.3 0.0 collective-permute-done.1.do1
  8.4 0.0 copy-start.5
  8.4 0.8 copy-done.11
  9.1 0.2 copy-done.5
  9.4 13.3 %local_scores.1 = (bf16[2,6,512,512]{3,2,1,0:T(8,128)(2,1)}, bf16[2,6,512,512]{3,2,1,0:T(8,128)(2,1)}, bf16[2,4,512,192]{3,2,1,0:T(8,128)(2,1)}, f32[2,4,8,512]{...) custom-call(s32[1]{0:T(128)} %bitcast.index_ref, s32[1,8192]{1,0:T(1,128)} %bitcast.11, ...), custom_call_target="tpu_custom_call" | custom-call | flops 3087007744 | bytes 16777216 | tf_op jit(solution)/shard_map/local_scores/pallas_call | solution.py:505
  22.7 0.0 collective-permute-done.3.lat_far
  22.7 0.0 copy-start.7
  22.8 2.9 %collective-permute-start.5 = (bf16[576,512]{1,0:T(8,128)(2,1)S(1)}, bf16[576,512]{1,0:T(8,128)(2,1)S(1)}, u32[]{:S(2)}, u32[]{:S(2)}) collective-permute-start(bf16[576,512]{1,0:T(8,128)(2,1)S(1)} %collective-permute-done.3.lat_far), channel_id=1, source_target_pairs={{0,2},{2,0},{4,6},{6,4},{8,10},{10,8},{12,14},{14,12},{16,18},{18,... | collective-permute-start | bytes 1769480 | tf_op jit(solution)/shard_map/ppermute | solution.py:586
  25.7 2.0 %collective-permute-start.6 = (bf16[576,512]{1,0:T(8,128)(2,1)S(1)}, bf16[576,512]{1,0:T(8,128)(2,1)S(1)}, u32[]{:S(2)}, u32[]{:S(2)}) collective-permute-start(bf16[576,512]{1,0:T(8,128)(2,1)S(1)} %collective-permute-done.4.lat_mixed), channel_id=1, source_target_pairs={{0,2},{4,6},{8,10},{12,14},{16,18},{20,22},{24,26},{28,30},{1,3},{... | collective-permute-start | bytes 1769480 | tf_op jit(solution)/shard_map/ppermute | solution.py:586
  27.7 1.6 %collective-permute-done.6.lat_passed = bf16[576,512]{1,0:T(8,128)(2,1)S(1)} collective-permute-done((bf16[576,512]{1,0:T(8,128)(2,1)S(1)}, bf16[576,512]{1,0:T(8,128)(2,1)S(1)}, u32[]{:S(2)}, u32[]{:S(2)}) %collective-permute-start.6) | collective-permute-done | bytes 589856 | tf_op jit(solution)/shard_map/ppermute | solution.py:586
  29.2 0.8 copy-done.10
  30.0 23.7 %attention.1 = (bf16[512,768]{1,0:T(8,128)(2,1)}, bf16[512,768]{1,0:T(8,128)(2,1)}, bf16[256,1024]{1,0:T(8,128)(2,1)}, bf16[256,1024]{1,0:T(8,128)(2,1)}, bf16[5...) custom-call(s32[1]{0:T(128)} %bitcast.index_ref, ...), custom_call_target="tpu_custom_call" | custom-call | flops 18924699648 | bytes 16777216 | tf_op jit(solution)/shard_map/attention/pallas_call | solution.py:540
  53.7 1.4 %collective-permute-start.12 = (bf16[576,512]{1,0:T(8,128)(2,1)}, bf16[576,512]{1,0:T(8,128)(2,1)S(1)}, u32[]{:S(2)}, u32[]{:S(2)}) collective-permute-start(bf16[576,512]{1,0:T(8,128)(2,1)} %get-tuple-element.39), channel_id=1, source_target_pairs={{2,0},{6,4},{10,8},{14,12},{18,16},{22,20},{26,24},{30,28},{3,1},{... | collective-permute-start | bytes 1769480 | tf_op jit(solution)/shard_map/ppermute | solution.py:586
  55.2 1.2 %collective-permute-start.9 = (bf16[576,512]{1,0:T(8,128)(2,1)}, bf16[576,512]{1,0:T(8,128)(2,1)S(1)}, u32[]{:S(2)}, u32[]{:S(2)}) collective-permute-start(bf16[576,512]{1,0:T(8,128)(2,1)} %get-tuple-element.37), channel_id=1, source_target_pairs={{0,2},{2,0},{4,6},{6,4},{8,10},{10,8},{12,14},{14,12},{16,18},{18,... | collective-permute-start | bytes 1769480 | tf_op jit(solution)/shard_map/ppermute | solution.py:586
  56.4 12.5 %collective-permute-start.17 = (bf16[256,1024]{1,0:T(8,128)(2,1)}, bf16[256,1024]{1,0:T(8,128)(2,1)S(1)}, u32[]{:S(2)}, u32[]{:S(2)}) collective-permute-start(bf16[256,1024]{1,0:T(8,128)(2,1)} %get-tuple-element.41), channel_id=1, source_target_pairs={{0,4},{2,6},{4,0},{6,2},{8,12},{10,14},{12,8},{14,10},{16,20},{18,... | collective-permute-start | bytes 1572872 | tf_op jit(solution)/shard_map/ppermute | solution.py:586
  68.9 0.5 collective-permute-start.7
  69.4 1.2 add_convert_fusion
  70.7 3.6 %collective-permute-start.13 = (bf16[288,512]{1,0:T(8,128)(2,1)S(1)}, bf16[288,512]{1,0:T(8,128)(2,1)S(1)}, u32[]{:S(2)}, u32[]{:S(2)}) collective-permute-start(bf16[288,512]{1,0:T(8,128)(2,1)S(1)} %constant_dynamic-slice_fusion.1), channel_id=1, source_target_pairs={{0,1},{1,0},{4,5},{5,4},{8,9},{9,8},{12,13},{13,12},{16,17},{17,16... | collective-permute-start | bytes 884744 | tf_op jit(solution)/shard_map/ppermute | solution.py:637
  74.3 0.2 add_convert_fusion.1
  74.5 0.6 collective-permute-start.10
  75.0 0.2 add_convert_fusion.2
  75.2 5.5 %collective-permute-done.13 = bf16[288,512]{1,0:T(8,128)(2,1)S(1)} collective-permute-done((bf16[288,512]{1,0:T(8,128)(2,1)S(1)}, bf16[288,512]{1,0:T(8,128)(2,1)S(1)}, u32[]{:S(2)}, u32[]{:S(2)}) %collective-permute-start.13) | collective-permute-done | bytes 294944 | tf_op jit(solution)/shard_map/ppermute | solution.py:637
  80.7 0.1 add_convert_fusion.5
  80.8 1.4 %collective-permute-start.14 = (bf16[288,512]{1,0:T(8,128)(2,1)S(1)}, bf16[288,512]{1,0:T(8,128)(2,1)}, u32[]{:S(2)}, u32[]{:S(2)}) collective-permute-start(bf16[288,512]{1,0:T(8,128)(2,1)S(1)} %add_convert_fusion.5), channel_id=1, source_target_pairs={{8,2},{12,6},{16,10},{20,14},{24,18},{28,22},{9,3},{13,7},{17,11},... | collective-permute-start | bytes 884744 | tf_op jit(solution)/shard_map/ppermute | solution.py:586
  82.2 1.7 %collective-permute-done.10 = bf16[288,512]{1,0:T(8,128)(2,1)S(1)} collective-permute-done((bf16[288,512]{1,0:T(8,128)(2,1)S(1)}, bf16[288,512]{1,0:T(8,128)(2,1)S(1)}, u32[]{:S(2)}, u32[]{:S(2)}) %collective-permute-start.10) | collective-permute-done | bytes 294944 | tf_op jit(solution)/shard_map/ppermute | solution.py:637
  83.8 0.1 add_convert_fusion.6
  83.9 1.3 %collective-permute-start.15 = (bf16[288,512]{1,0:T(8,128)(2,1)S(1)}, bf16[288,512]{1,0:T(8,128)(2,1)}, u32[]{:S(2)}, u32[]{:S(2)}) collective-permute-start(bf16[288,512]{1,0:T(8,128)(2,1)S(1)} %add_convert_fusion.6), channel_id=1, source_target_pairs={{4,0},{6,2},{8,4},{10,6},{12,8},{14,10},{16,12},{18,14},{20,16},{2... | collective-permute-start | bytes 884744 | tf_op jit(solution)/shard_map/ppermute | solution.py:586
  85.3 1.0 add_convert_fusion.3
  86.3 16.5 %all-to-all-start = ((bf16[4,64,1024]{2,1,0:T(8,128)(2,1)}), bf16[4,64,1024]{2,1,0:T(8,128)(2,1)S(1)}, u32[]{:S(2)}, u32[]{:S(2)}) async-start(bf16[4,64,1024]{2,1,0:T(8,128)(2,1)} %bitcast.4), calls=%async_computation | async-start | bytes 1048576 | tf_op jit(solution)/shard_map/all_to_all | solution.py:665
  102.8 1.6 %collective-permute-start.11 = (bf16[288,512]{1,0:T(8,128)(2,1)S(1)}, bf16[288,512]{1,0:T(8,128)(2,1)S(1)}, u32[]{:S(2)}, u32[]{:S(2)}) collective-permute-start(bf16[288,512]{1,0:T(8,128)(2,1)S(1)} %constant_dynamic-slice_fusion.2), channel_id=1, source_target_pairs={{0,1},{1,0},{2,3},{3,2},{4,5},{5,4},{6,7},{7,6},{8,9},{9,8},{10,11... | collective-permute-start | bytes 884744 | tf_op jit(solution)/shard_map/ppermute | solution.py:637
  104.4 0.1 broadcast_select_fusion.1
  104.5 7.9 %collective-permute-done.11 = bf16[288,512]{1,0:T(8,128)(2,1)S(1)} collective-permute-done((bf16[288,512]{1,0:T(8,128)(2,1)S(1)}, bf16[288,512]{1,0:T(8,128)(2,1)S(1)}, u32[]{:S(2)}, u32[]{:S(2)}) %collective-permute-start.11) | collective-permute-done | bytes 294944 | tf_op jit(solution)/shard_map/ppermute | solution.py:637
  112.4 1.2 add_convert_fusion.4
  113.6 1.6 %collective-permute-start.16 = (bf16[288,512]{1,0:T(8,128)(2,1)S(1)}, bf16[288,512]{1,0:T(8,128)(2,1)S(1)}, u32[]{:S(2)}, u32[]{:S(2)}) collective-permute-start(bf16[288,512]{1,0:T(8,128)(2,1)S(1)} %add_convert_fusion.4), channel_id=1, source_target_pairs={{0,1},{1,0},{2,3},{3,2},{4,5},{5,4},{6,7},{7,6},{8,9},{9,8},{10,11... | collective-permute-start | bytes 884744 | tf_op jit(solution)/shard_map/ppermute | solution.py:637
  115.2 1.3 %pad_maximum_fusion = bf16[512,1536]{1,0:T(8,128)(2,1)} fusion(bf16[512,768]{1,0:T(8,128)(2,1)S(1)} %get-tuple-element.44, bf16[512,768]{1,0:T(8,128)(2,1)S(1)} %get-tuple-element.43), kind=kLoop, calls=%fused_computation | loop fusion | flops 3145728 | bytes 3145728 | tf_op jit(solution)/shard_map/concatenate | solution.py:672
  116.4 0.1 convert_reduce_fusion
  116.6 0.1 collective-permute-start.18
  116.6 3.8 %collective-permute-done.16 = bf16[288,512]{1,0:T(8,128)(2,1)S(1)} collective-permute-done((bf16[288,512]{1,0:T(8,128)(2,1)S(1)}, bf16[288,512]{1,0:T(8,128)(2,1)S(1)}, u32[]{:S(2)}, u32[]{:S(2)}) %collective-permute-start.16) | collective-permute-done | bytes 294944 | tf_op jit(solution)/shard_map/ppermute | solution.py:637
  120.4 0.9 maximum_bitcast_fusion
  121.3 0.7 pad_maximum_fusion.1
  (38 shorter events, 0.3 us)
Async XLA Ops:
  0.6 1.9 %copy-start.4 = (bf16[512,1024]{1,0:T(8,128)(2,1)S(1)}, bf16[512,1024]{1,0:T(8,128)(2,1)}, u32[]{:S(2)}) copy-start(bf16[512,1024]{1,0:T(8,128)(2,1)} %do0.3) | copy-start | bytes 3145732
  0.6 2.5 %copy-start.6 = (bf16[512,576]{0,1:T(8,128)(2,1)S(1)}, bf16[512,576]{0,1:T(8,128)(2,1)}, u32[]{:S(2)}) copy-start(bf16[512,576]{0,1:T(8,128)(2,1)} %param.5) | copy-start | bytes 1769476
  2.0 6.4 %collective-permute-start = (bf16[512,768]{1,0:T(8,128)(2,1)S(1)}, bf16[512,768]{1,0:T(8,128)(2,1)S(1)}, u32[]{:S(2)}, u32[]{:S(2)}) collective-permute-start(bf16[512,768]{1,0:T(8,128)(2,1)S(1)} %constant_dynamic-slice_fusion.5), channel_id=1, source_target_pairs={{0,2},{2,0},{4,6},{6,4},{8,10},{10,8},{12,14},{14,12},{16,18},{18,... | collective-permute-start | bytes 2359304 | tf_op jit(solution)/shard_map/ppermute | solution.py:586
  2.5 5.9 %collective-permute-start.2 = (bf16[576,512]{1,0:T(8,128)(2,1)}, bf16[576,512]{1,0:T(8,128)(2,1)}, u32[]{:S(2)}, u32[]{:S(2)}) collective-permute-start(bf16[576,512]{1,0:T(8,128)(2,1)} %bitcast.6), channel_id=1, source_target_pairs={{0,2},{2,0},{4,6},{6,4},{8,10},{10,8},{12,14},{14,12},{16,18},{18,... | collective-permute-start | bytes 1769480 | tf_op jit(solution)/shard_map/ppermute | solution.py:586
  2.6 5.7 %collective-permute-start.1 = (bf16[512,512]{1,0:T(8,128)(2,1)S(1)}, bf16[512,512]{1,0:T(8,128)(2,1)S(1)}, u32[]{:S(2)}, u32[]{:S(2)}) collective-permute-start(bf16[512,512]{1,0:T(8,128)(2,1)S(1)} %constant_dynamic-slice_fusion.4), channel_id=1, source_target_pairs={{0,2},{2,0},{4,6},{6,4},{8,10},{10,8},{12,14},{14,12},{16,18},{18,... | collective-permute-start | bytes 1572872 | tf_op jit(solution)/shard_map/ppermute | solution.py:586
  3.1 19.6 %collective-permute-start.3 = (bf16[576,512]{1,0:T(8,128)(2,1)S(1)}, bf16[576,512]{1,0:T(8,128)(2,1)S(1)}, u32[]{:S(2)}, u32[]{:S(2)}) collective-permute-start(bf16[576,512]{1,0:T(8,128)(2,1)S(1)} %bitcast.9), channel_id=1, source_target_pairs={{0,4},{2,6},{4,8},{6,10},{8,12},{10,14},{12,16},{14,18},{16,20},{1... | collective-permute-start | bytes 1769480 | tf_op jit(solution)/shard_map/ppermute | solution.py:586
  7.6 15.1 %collective-permute-start.4 = (bf16[576,512]{1,0:T(8,128)(2,1)S(1)}, bf16[576,512]{1,0:T(8,128)(2,1)S(1)}, u32[]{:S(2)}, u32[]{:S(2)}) collective-permute-start(bf16[576,512]{1,0:T(8,128)(2,1)S(1)} %bitcast.10), channel_id=1, source_target_pairs={{2,8},{6,12},{10,16},{14,20},{18,24},{22,28},{3,9},{7,13},{11,17},... | collective-permute-start | bytes 1769480 | tf_op jit(solution)/shard_map/ppermute | solution.py:586
  8.3 0.8 copy-start.11
  8.4 1.0 copy-start.5
  22.7 6.5 %copy-start.7 = (bf16[576,512]{1,0:T(8,128)(2,1)}, bf16[576,512]{1,0:T(8,128)(2,1)S(1)}, u32[]{:S(2)}) copy-start(bf16[576,512]{1,0:T(8,128)(2,1)S(1)} %collective-permute-done.3.lat_far) | copy-start | bytes 1769476
  22.8 6.5 %copy-start.8 = (bf16[576,512]{1,0:T(8,128)(2,1)}, bf16[576,512]{1,0:T(8,128)(2,1)S(1)}, u32[]{:S(2)}) copy-start(bf16[576,512]{1,0:T(8,128)(2,1)S(1)} %collective-permute-done.4.lat_mixed) | copy-start | bytes 1769476
  22.8 4.9 %collective-permute-start.5 = (bf16[576,512]{1,0:T(8,128)(2,1)S(1)}, bf16[576,512]{1,0:T(8,128)(2,1)S(1)}, u32[]{:S(2)}, u32[]{:S(2)}) collective-permute-start(bf16[576,512]{1,0:T(8,128)(2,1)S(1)} %collective-permute-done.3.lat_far), channel_id=1, source_target_pairs={{0,2},{2,0},{4,6},{6,4},{8,10},{10,8},{12,14},{14,12},{16,18},{18,... | collective-permute-start | bytes 1769480 | tf_op jit(solution)/shard_map/ppermute | solution.py:586
  25.7 3.5 %collective-permute-start.6 = (bf16[576,512]{1,0:T(8,128)(2,1)S(1)}, bf16[576,512]{1,0:T(8,128)(2,1)S(1)}, u32[]{:S(2)}, u32[]{:S(2)}) collective-permute-start(bf16[576,512]{1,0:T(8,128)(2,1)S(1)} %collective-permute-done.4.lat_mixed), channel_id=1, source_target_pairs={{0,2},{4,6},{8,10},{12,14},{16,18},{20,22},{24,26},{28,30},{1,3},{... | collective-permute-start | bytes 1769480 | tf_op jit(solution)/shard_map/ppermute | solution.py:586
  27.6 1.6 %copy-start.9 = (bf16[576,512]{1,0:T(8,128)(2,1)}, bf16[576,512]{1,0:T(8,128)(2,1)S(1)}, u32[]{:S(2)}) copy-start(bf16[576,512]{1,0:T(8,128)(2,1)S(1)} %collective-permute-done.5.lat_swap) | copy-start | bytes 1769476
  29.2 0.8 copy-start.10
  53.7 20.5 %copy-start.2 = (bf16[576,512]{1,0:T(8,128)(2,1)S(1)}, bf16[576,512]{1,0:T(8,128)(2,1)}, u32[]{:S(2)}) copy-start(bf16[576,512]{1,0:T(8,128)(2,1)} %get-tuple-element.36) | copy-start | bytes 1769476
  53.7 15.7 %collective-permute-start.12 = (bf16[576,512]{1,0:T(8,128)(2,1)}, bf16[576,512]{1,0:T(8,128)(2,1)S(1)}, u32[]{:S(2)}, u32[]{:S(2)}) collective-permute-start(bf16[576,512]{1,0:T(8,128)(2,1)} %get-tuple-element.39), channel_id=1, source_target_pairs={{2,0},{6,4},{10,8},{14,12},{18,16},{22,20},{26,24},{30,28},{3,1},{... | collective-permute-start | bytes 1769480 | tf_op jit(solution)/shard_map/ppermute | solution.py:586
  55.2 19.1 %collective-permute-start.9 = (bf16[576,512]{1,0:T(8,128)(2,1)}, bf16[576,512]{1,0:T(8,128)(2,1)S(1)}, u32[]{:S(2)}, u32[]{:S(2)}) collective-permute-start(bf16[576,512]{1,0:T(8,128)(2,1)} %get-tuple-element.37), channel_id=1, source_target_pairs={{0,2},{2,0},{4,6},{6,4},{8,10},{10,8},{12,14},{14,12},{16,18},{18,... | collective-permute-start | bytes 1769480 | tf_op jit(solution)/shard_map/ppermute | solution.py:586
  56.4 28.8 %collective-permute-start.17 = (bf16[256,1024]{1,0:T(8,128)(2,1)}, bf16[256,1024]{1,0:T(8,128)(2,1)S(1)}, u32[]{:S(2)}, u32[]{:S(2)}) collective-permute-start(bf16[256,1024]{1,0:T(8,128)(2,1)} %get-tuple-element.41), channel_id=1, source_target_pairs={{0,4},{2,6},{4,0},{6,2},{8,12},{10,14},{12,8},{14,10},{16,20},{18,... | collective-permute-start | bytes 1572872 | tf_op jit(solution)/shard_map/ppermute | solution.py:586
  68.9 6.1 %collective-permute-start.8 = (bf16[576,512]{1,0:T(8,128)(2,1)}, bf16[576,512]{1,0:T(8,128)(2,1)S(1)}, u32[]{:S(2)}, u32[]{:S(2)}) collective-permute-start(bf16[576,512]{1,0:T(8,128)(2,1)} %get-tuple-element.35), channel_id=1, source_target_pairs={{0,2},{2,0},{4,6},{6,4},{8,10},{10,8},{12,14},{14,12},{16,18},{18,... | collective-permute-start | bytes 1769480 | tf_op jit(solution)/shard_map/ppermute | solution.py:586
  68.9 35.5 %collective-permute-start.7 = (bf16[512,768]{1,0:T(8,128)(2,1)}, bf16[512,768]{1,0:T(8,128)(2,1)S(1)}, u32[]{:S(2)}, u32[]{:S(2)}) collective-permute-start(bf16[512,768]{1,0:T(8,128)(2,1)} %get-tuple-element.33), channel_id=1, source_target_pairs={{0,2},{2,0},{4,6},{6,4},{8,10},{10,8},{12,14},{14,12},{16,18},{18,... | collective-permute-start | bytes 2359304 | tf_op jit(solution)/shard_map/ppermute | solution.py:586
  70.6 4.4 %copy-start.1 = (bf16[576,512]{1,0:T(8,128)(2,1)S(1)}, bf16[576,512]{1,0:T(8,128)(2,1)}, u32[]{:S(2)}) copy-start(bf16[576,512]{1,0:T(8,128)(2,1)} %get-tuple-element.34) | copy-start | bytes 1769476
  70.7 10.0 %collective-permute-start.13 = (bf16[288,512]{1,0:T(8,128)(2,1)S(1)}, bf16[288,512]{1,0:T(8,128)(2,1)S(1)}, u32[]{:S(2)}, u32[]{:S(2)}) collective-permute-start(bf16[288,512]{1,0:T(8,128)(2,1)S(1)} %constant_dynamic-slice_fusion.1), channel_id=1, source_target_pairs={{0,1},{1,0},{4,5},{5,4},{8,9},{9,8},{12,13},{13,12},{16,17},{17,16... | collective-permute-start | bytes 884744 | tf_op jit(solution)/shard_map/ppermute | solution.py:637
  74.5 9.4 %collective-permute-start.10 = (bf16[288,512]{1,0:T(8,128)(2,1)S(1)}, bf16[288,512]{1,0:T(8,128)(2,1)S(1)}, u32[]{:S(2)}, u32[]{:S(2)}) collective-permute-start(bf16[288,512]{1,0:T(8,128)(2,1)S(1)} %constant_dynamic-slice_fusion.3), channel_id=1, source_target_pairs={{0,1},{1,0},{2,3},{3,2},{4,5},{5,4},{6,7},{7,6},{8,9},{9,8},{10,11... | collective-permute-start | bytes 884744 | tf_op jit(solution)/shard_map/ppermute | solution.py:637
  75.0 10.2 %copy-start.3 = (bf16[256,1024]{1,0:T(8,128)(2,1)S(1)}, bf16[256,1024]{1,0:T(8,128)(2,1)}, u32[]{:S(2)}) copy-start(bf16[256,1024]{1,0:T(8,128)(2,1)} %get-tuple-element.40) | copy-start | bytes 1572868
  80.8 31.6 %collective-permute-start.14 = (bf16[288,512]{1,0:T(8,128)(2,1)S(1)}, bf16[288,512]{1,0:T(8,128)(2,1)}, u32[]{:S(2)}, u32[]{:S(2)}) collective-permute-start(bf16[288,512]{1,0:T(8,128)(2,1)S(1)} %add_convert_fusion.5), channel_id=1, source_target_pairs={{8,2},{12,6},{16,10},{20,14},{24,18},{28,22},{9,3},{13,7},{17,11},... | collective-permute-start | bytes 884744 | tf_op jit(solution)/shard_map/ppermute | solution.py:586
  83.9 28.4 %collective-permute-start.15 = (bf16[288,512]{1,0:T(8,128)(2,1)S(1)}, bf16[288,512]{1,0:T(8,128)(2,1)}, u32[]{:S(2)}, u32[]{:S(2)}) collective-permute-start(bf16[288,512]{1,0:T(8,128)(2,1)S(1)} %add_convert_fusion.6), channel_id=1, source_target_pairs={{4,0},{6,2},{8,4},{10,6},{12,8},{14,10},{16,12},{18,14},{20,16},{2... | collective-permute-start | bytes 884744 | tf_op jit(solution)/shard_map/ppermute | solution.py:586
  85.3 19.1 %copy-start = (bf16[512,768]{1,0:T(8,128)(2,1)S(1)}, bf16[512,768]{1,0:T(8,128)(2,1)}, u32[]{:S(2)}) copy-start(bf16[512,768]{1,0:T(8,128)(2,1)} %get-tuple-element.32) | copy-start | bytes 2359300
  86.3 30.2 %all-to-all-start = ((bf16[4,64,1024]{2,1,0:T(8,128)(2,1)}), bf16[4,64,1024]{2,1,0:T(8,128)(2,1)S(1)}, u32[]{:S(2)}, u32[]{:S(2)}) async-start(bf16[4,64,1024]{2,1,0:T(8,128)(2,1)} %bitcast.4), calls=%async_computation | async-start | bytes 1048576 | tf_op jit(solution)/shard_map/all_to_all | solution.py:665
  102.8 9.6 %collective-permute-start.11 = (bf16[288,512]{1,0:T(8,128)(2,1)S(1)}, bf16[288,512]{1,0:T(8,128)(2,1)S(1)}, u32[]{:S(2)}, u32[]{:S(2)}) collective-permute-start(bf16[288,512]{1,0:T(8,128)(2,1)S(1)} %constant_dynamic-slice_fusion.2), channel_id=1, source_target_pairs={{0,1},{1,0},{2,3},{3,2},{4,5},{5,4},{6,7},{7,6},{8,9},{9,8},{10,11... | collective-permute-start | bytes 884744 | tf_op jit(solution)/shard_map/ppermute | solution.py:637
  113.6 6.8 %collective-permute-start.16 = (bf16[288,512]{1,0:T(8,128)(2,1)S(1)}, bf16[288,512]{1,0:T(8,128)(2,1)S(1)}, u32[]{:S(2)}, u32[]{:S(2)}) collective-permute-start(bf16[288,512]{1,0:T(8,128)(2,1)S(1)} %add_convert_fusion.4), channel_id=1, source_target_pairs={{0,1},{1,0},{2,3},{3,2},{4,5},{5,4},{6,7},{7,6},{8,9},{9,8},{10,11... | collective-permute-start | bytes 884744 | tf_op jit(solution)/shard_map/ppermute | solution.py:637
  116.6 4.7 %collective-permute-start.18 = (f32[32,1024]{1,0:T(8,128)S(1)}, f32[32,1024]{1,0:T(8,128)S(1)}, u32[]{:S(2)}, u32[]{:S(2)}) collective-permute-start(f32[32,1024]{1,0:T(8,128)S(1)} %constant_dynamic-slice_fusion), channel_id=1, source_target_pairs={{0,2},{2,0},{4,6},{6,4},{8,10},{10,8},{12,14},{14,12},{16,18},{18,... | collective-permute-start | bytes 393224 | tf_op jit(solution)/shard_map/ppermute | solution.py:586

commit v3 on v2

--- a/solution.py
+++ b/solution.py
@@ -51,16 +51,16 @@
         v_out(h, lifted[:, NOPE:])
 
 
-def score_block(key, value, q_ref, do_ref, bounds, run_ref, raw_ref, graw_ref, keep):
-    rows = do_ref.shape[0]
+def score_block(key, value, qt_ref, dot_ref, bounds, run_ref, raw_ref, graw_ref, keep):
+    rows = dot_ref.shape[1]
     lower, upper = bounds
     index = lax.broadcasted_iota(jnp.int32, (LANES, LANES), 0)
     parts = [slice(r, r + LANES) for r in range(0, rows, LANES)]
 
     def multiply(h, first):
         cols = slice(first, first + PIECE)
-        raw_ref[h, :, cols] = dot(key(h), q_ref[cols, head_cols(h, QK)], NT)
-        graw_ref[h, :, cols] = dot(value(h), do_ref[cols, head_cols(h, VDIM)], NT)
+        raw_ref[h, :, cols] = dot(key(h), qt_ref[head_cols(h, QK), cols])
+        graw_ref[h, :, cols] = dot(value(h), dot_ref[head_cols(h, VDIM), cols])
 
     def weigh(h, first):
         for c in range(first, first + PIECE, LANES):
@@ -92,7 +92,7 @@
                 cross, axis=0, keepdims=True
             )
 
-    alternate(rows, do_ref.shape[1] // VDIM, multiply, weigh)
+    alternate(rows, dot_ref.shape[0] // VDIM, multiply, weigh)
 
 
 def alternate(rows, heads, first, second):
@@ -165,6 +165,11 @@
     out_ref[1 - core] = other[...]
 
 
+def turn_pair(out_ref, core, own, other):
+    out_ref[core] = own[...].T
+    out_ref[1 - core] = other[...].T
+
+
 LOCAL = ((1, REACH), (0, REACH), (1, REACH + 1))
 
 
@@ -195,7 +200,7 @@
 def local_kernel(
     index_ref, docs_ref, q0, do0, q1, do1, w_ref, lat0, lat1,
     e_ref, g_ref, k_ref, run_ref, top_ref, start_ref,
-    q_ref, do_ref, lat_ref, v_ref, raw_ref, graw_ref,
+    qt_ref, dot_ref, lat_ref, v_ref, raw_ref, graw_ref,
 ):
     rows = q0.shape[0]
     core, chip = chip_place(index_ref)
@@ -207,8 +212,8 @@
         lat_ref[1 - core] = lat1[...].T
         find_starts(docs_ref, start_ref, chip, rows)
 
-    order_pair(q_ref, core, q0, q1)
-    order_pair(do_ref, core, do0, do1)
+    turn_pair(qt_ref, core, q0, q1)
+    turn_pair(dot_ref, core, do0, do1)
     for j in range(2):
 
         def k_out(h, key):
@@ -229,7 +234,7 @@
         run = run_ref.at[0, pl.ds(j * heads, heads)]
         score_block(
             lambda h: k_ref[0, slot * heads + h], lambda h: v_ref[slot * heads + h],
-            q_ref.at[j], do_ref.at[j], query_bounds(start_ref, chip, j, t, rows), run,
+            qt_ref.at[j], dot_ref.at[j], query_bounds(start_ref, chip, j, t, rows), run,
             raw_ref, graw_ref, keep,
         )
         for h in range(heads):
@@ -242,7 +247,7 @@
     all_e, all_g, local_k, local_run, local_top, start_ref,
     lat_far, lat_swap, lat_mixed, lat_passed, lat_own, lat_other,
     dq0_ref, dq1_ref, keep_ref, send_ref, x_old, x_far, x_swap, x_own, x_other,
-    q_ref, do_ref, lat_ref, lat_t_ref, e_ref, g_ref, k_ref, v_ref, top_ref,
+    q_ref, do_ref, qt_ref, dot_ref, lat_ref, lat_t_ref, e_ref, g_ref, k_ref, v_ref, top_ref,
     run_ref, end_ref, raw_ref, graw_ref, low_ref, ds_ref, dq_acc, d_acc, gw_acc, x_acc,
     r_acc, local_e, local_g, sems, kept_sems,
 ):
@@ -309,6 +314,8 @@
 
     order_pair(q_ref, core, q0, q1)
     order_pair(do_ref, core, do0, do1)
+    turn_pair(qt_ref, core, q0, q1)
+    turn_pair(dot_ref, core, do0, do1)
 
     def lift_block(t):
         def k_out(h, key):
@@ -332,7 +339,7 @@
 
             score_block(
                 lambda h: k_ref[h, block_rows(t), :], lambda h: v_ref[h, block_rows(t), :],
-                q_ref.at[j], do_ref.at[j], query_bounds(start_ref, chip, j, t, rows), run_ref,
+                qt_ref.at[j], dot_ref.at[j], query_bounds(start_ref, chip, j, t, rows), run_ref,
                 raw_ref, graw_ref, keep,
             )
             for h in range(heads):
@@ -519,8 +526,8 @@
             (fixed(2, 8, rows), (2, 8, rows), jnp.int32),
         ],
         [
-            ((2, rows, heads * QK), low),
-            ((2, rows, heads * VDIM), low),
+            ((2, heads * QK, rows), low),
+            ((2, heads * VDIM, rows), low),
             ((2, rows, WIDTH), low),
             ((2 * heads, rows, VDIM), low),
             ((heads, rows, rows), full),
@@ -553,6 +560,8 @@
         [
             ((2, rows, heads * QK), low),
             ((2, rows, heads * VDIM), low),
+            ((2, heads * QK, rows), low),
+            ((2, heads * VDIM, rows), low),
             ((far, WIDTH), low),
             ((WIDTH, window), low),
             ((heads, far, rows), low),
@@ -636,14 +645,18 @@
         ]
         return lax.ppermute(value, ("ctx", "head"), turns)
 
-    def head_share(value, ctx=range(ranks)):
+    arrived = []
+
+    def head_share(value, ctx=range(ranks), after=()):
         def rows_of(which):
             return lax.dynamic_slice_in_dim(value, which * share, share, axis=0)
 
         total = rows_of(head).astype(full)
         for turn in range(1, head_count):
             target = lax.rem(head + turn, head_count)
-            total = total + turned(rows_of(target), turn, ctx).astype(full)
+            received, *_ = lax.optimization_barrier((turned(rows_of(target), turn, ctx), *after))
+            arrived.append(received)
+            total = total + received.astype(full)
         return total
 
     from_x = permute(send, "ctx", lambda s: s ^ 2)
@@ -652,14 +665,14 @@
     from_other = across(to_other)
     far_sum = head_share((to_far.astype(full) + from_swap.astype(full)).astype(low)).astype(low)
     old_sum = (to_old.astype(full) + from_old.astype(full)).astype(low)
-    old_sum = head_share(old_sum, range(0, ranks, 2)).astype(low)
+    old_sum = head_share(old_sum, range(0, ranks, 2), (far_sum,)).astype(low)
     from_far = permute(far_sum, "ctx", lambda s: s - 2)
     from_mixed = permute(old_sum, "ctx", lambda s: -1 if s % 2 else s - 3)
     own_sum = (mine.astype(full) + from_other.astype(full)).astype(low)
     own_sum, *_ = lax.optimization_barrier((own_sum, far_sum))
     total = head_share(own_sum)
 
-    from_x, *_ = lax.optimization_barrier((from_x, far_sum, old_sum))
+    from_x, *_ = lax.optimization_barrier((from_x, far_sum, old_sum, arrived[-1]))
     plane = (keep.astype(full) + from_x.astype(full)).astype(low)
     columns = [list(range(first, ranks, 4)) for first in range(4)]
     pieces = lax.all_to_all(plane, "ctx", 0, 0, axis_index_groups=columns, tiled=True)

time: 123 us -> 125 us (1.016)
  other arithmetic: 6.97 us -> 10.5 us
  starting transfers between devices: 53.4 us -> 50.9 us
  local copies, waits for them, and re-layouts: 3.32 us -> 4.73 us
    ppermute x4, waiting for transfers between devices: 18.8 us -> 7.4 us  [turned(): return lax.ppermute(value, ('ctx', 'head'), turns)]
    all_to_all x1, waiting for transfers between devices: 0.01 us -> 10 us  [local(): lax.all_to_all(plane, 'ctx', 0, 0, axis_index_groups=columns, tiled=True)]
    all_to_all x1, starting transfers between devices: 16.5 us -> 12.4 us  [local(): lax.all_to_all(plane, 'ctx', 0, 0, axis_index_groups=columns, tiled=True)]
    ppermute x15, starting transfers between devices: 29.5 us -> 32.4 us  [permute(): return lax.ppermute(value, axis, pairs)]
    convert_element_type x1, other arithmetic: 0.09 us -> 1.76 us  [local(): old_sum = head_share(old_sum, range(0, ranks, 2), (far_sum,)).astype(low)]
    dynamic_slice x3, local copies, waits for them, and re-layouts: 0.08 us -> 1.5 us  [rows_of(): return lax.dynamic_slice_in_dim(value, which * share, share, axis=0)]
  transfers between devices with their start and end apart: 20 -> 20, of which waited for: 5 -> 5; matrix products, arithmetic and copies ran while one was open for 5% -> 9% of each run, Pallas kernels for 11% -> 11%
where the time goes in v3:
time: 125 us; the launch traced here: 124 us
  starting transfers between devices  50.9 us (41%)
  Pallas kernels  37 us (30%)
  waiting for transfers between devices  19.4 us (16%)
  other arithmetic  10.5 us (8%)
  local copies, waits for them, and re-layouts  4.73 us (4%)
    ppermute x15, starting transfers between devices, permute(): return lax.ppermute(value, axis, pairs)  32.4 us
    pallas_call x1, Pallas kernels, attention(): call(functools.partial(main_kernel, ranks), steps, 2 * steps * heads * ro...  23.7 us
    pallas_call x1, Pallas kernels, local_scores(): call(local_kernel, steps, 2 * steps * heads * rows * rows * (3 * (QK + VD...  13.3 us
    all_to_all x1, starting transfers between devices, local(): lax.all_to_all(plane, 'ctx', 0, 0, axis_index_groups=columns, tiled=True)  12.4 us
    all_to_all x1, waiting for transfers between devices, local(): lax.all_to_all(plane, 'ctx', 0, 0, axis_index_groups=columns, tiled=True)  10 us
    ppermute x4, waiting for transfers between devices, turned(): return lax.ppermute(value, ('ctx', 'head'), turns)  7.4 us
    ppermute x4, starting transfers between devices, turned(): return lax.ppermute(value, ('ctx', 'head'), turns)  6.08 us
  transfers between devices with their start and end apart: 20, of which 5 were waited for; matrix products, arithmetic and copies ran while one was open for 9% of the time, Pallas kernels for 11%

profile of v3, /device:TPU:0, one launch (start us, length us, event | category | flops | bytes accessed | tf_op | source)
XLA Modules:
  0.0 123.5 jit_solution(7938937270387674800)
XLA Ops:
  0.6 0.0 copy-start.4
  0.6 0.0 copy-start.6
  0.7 1.3 %constant_dynamic-slice_fusion.5 = bf16[512,768]{1,0:T(8,128)(2,1)S(1)} fusion(bf16[512,1536]{1,0:T(8,128)(2,1)} %q0.3, s32[]{:T(128)S(6)} %select_n.61), kind=kLoop, calls=%fused_computation.22 | loop fusion | bytes 1572868 | tf_op jit(solution)/shard_map/dynamic_slice | solution.py:610
  2.0 0.5 collective-permute-start
  2.5 0.1 collective-permute-start.2
  2.6 0.5 collective-permute-start.1
  3.1 4.5 %collective-permute-start.3 = (bf16[576,512]{1,0:T(8,128)(2,1)S(1)}, bf16[576,512]{1,0:T(8,128)(2,1)S(1)}, u32[]{:S(2)}, u32[]{:S(2)}) collective-permute-start(bf16[576,512]{1,0:T(8,128)(2,1)S(1)} %bitcast.9), channel_id=1, source_target_pairs={{0,4},{2,6},{4,8},{6,10},{8,12},{10,14},{12,16},{14,18},{16,20},{1... | collective-permute-start | bytes 1769480 | tf_op jit(solution)/shard_map/ppermute | solution.py:595
  7.6 0.7 collective-permute-start.4
  8.4 0.0 copy-start.5
  8.4 0.8 copy-done.11
  9.1 0.2 copy-done.5
  9.4 13.3 %local_scores.1 = (bf16[2,6,512,512]{3,2,1,0:T(8,128)(2,1)}, bf16[2,6,512,512]{3,2,1,0:T(8,128)(2,1)}, bf16[2,4,512,192]{3,2,1,0:T(8,128)(2,1)}, f32[2,4,8,512]{...) custom-call(s32[1]{0:T(128)} %bitcast.index_ref, s32[1,8192]{1,0:T(1,128)} %bitcast.11, ...), custom_call_target="tpu_custom_call" | custom-call | flops 3087007744 | bytes 16777216 | tf_op jit(solution)/shard_map/local_scores/pallas_call | solution.py:512
  22.7 0.0 copy-start.7
  22.7 2.9 %collective-permute-start.5 = (bf16[576,512]{1,0:T(8,128)(2,1)S(1)}, bf16[576,512]{1,0:T(8,128)(2,1)S(1)}, u32[]{:S(2)}, u32[]{:S(2)}) collective-permute-start(bf16[576,512]{1,0:T(8,128)(2,1)S(1)} %collective-permute-done.3.lat_far), channel_id=1, source_target_pairs={{0,2},{2,0},{4,6},{6,4},{8,10},{10,8},{12,14},{14,12},{16,18},{18,... | collective-permute-start | bytes 1769480 | tf_op jit(solution)/shard_map/ppermute | solution.py:595
  25.7 2.0 %collective-permute-start.6 = (bf16[576,512]{1,0:T(8,128)(2,1)S(1)}, bf16[576,512]{1,0:T(8,128)(2,1)S(1)}, u32[]{:S(2)}, u32[]{:S(2)}) collective-permute-start(bf16[576,512]{1,0:T(8,128)(2,1)S(1)} %collective-permute-done.4.lat_mixed), channel_id=1, source_target_pairs={{0,2},{4,6},{8,10},{12,14},{16,18},{20,22},{24,26},{28,30},{1,3},{... | collective-permute-start | bytes 1769480 | tf_op jit(solution)/shard_map/ppermute | solution.py:595
  27.6 1.6 %collective-permute-done.6.lat_passed = bf16[576,512]{1,0:T(8,128)(2,1)S(1)} collective-permute-done((bf16[576,512]{1,0:T(8,128)(2,1)S(1)}, bf16[576,512]{1,0:T(8,128)(2,1)S(1)}, u32[]{:S(2)}, u32[]{:S(2)}) %collective-permute-start.6) | collective-permute-done | bytes 589856 | tf_op jit(solution)/shard_map/ppermute | solution.py:595
  29.2 0.8 copy-done.10
  30.0 23.7 %attention.1 = (bf16[512,768]{1,0:T(8,128)(2,1)}, bf16[512,768]{1,0:T(8,128)(2,1)}, bf16[256,1024]{1,0:T(8,128)(2,1)}, bf16[256,1024]{1,0:T(8,128)(2,1)}, bf16[5...) custom-call(s32[1]{0:T(128)} %bitcast.index_ref, ...), custom_call_target="tpu_custom_call" | custom-call | flops 18924699648 | bytes 16777216 | tf_op jit(solution)/shard_map/attention/pallas_call | solution.py:547
  53.7 0.6 collective-permute-start.9
  54.4 1.3 %collective-permute-start.12 = (bf16[576,512]{1,0:T(8,128)(2,1)}, bf16[576,512]{1,0:T(8,128)(2,1)S(1)}, u32[]{:S(2)}, u32[]{:S(2)}) collective-permute-start(bf16[576,512]{1,0:T(8,128)(2,1)} %get-tuple-element.40), channel_id=1, source_target_pairs={{2,0},{6,4},{10,8},{14,12},{18,16},{22,20},{26,24},{30,28},{3,1},{... | collective-permute-start | bytes 1769480 | tf_op jit(solution)/shard_map/ppermute | solution.py:595
  55.7 1.2 collective-permute-start.8
  56.9 15.3 %collective-permute-start.17 = (bf16[256,1024]{1,0:T(8,128)(2,1)}, bf16[256,1024]{1,0:T(8,128)(2,1)}, u32[]{:S(2)}, u32[]{:S(2)}) collective-permute-start(bf16[256,1024]{1,0:T(8,128)(2,1)} %get-tuple-element.43), channel_id=1, source_target_pairs={{0,4},{2,6},{4,0},{6,2},{8,12},{10,14},{12,8},{14,10},{16,20},{18,... | collective-permute-start | bytes 1572872 | tf_op jit(solution)/shard_map/ppermute | solution.py:595
  72.2 1.2 add_convert_fusion.1
  73.4 1.6 %collective-permute-start.10 = (bf16[288,512]{1,0:T(8,128)(2,1)S(1)}, bf16[288,512]{1,0:T(8,128)(2,1)S(1)}, u32[]{:S(2)}, u32[]{:S(2)}) collective-permute-start(bf16[288,512]{1,0:T(8,128)(2,1)S(1)} %constant_dynamic-slice_fusion.3), channel_id=1, source_target_pairs={{0,1},{1,0},{2,3},{3,2},{4,5},{5,4},{6,7},{7,6},{8,9},{9,8},{10,11... | collective-permute-start | bytes 884744 | tf_op jit(solution)/shard_map/ppermute | solution.py:646
  75.0 0.2 add_convert_fusion
  75.2 0.7 constant_dynamic-slice_fusion.1
  75.9 2.4 %collective-permute-start.13 = (bf16[288,512]{1,0:T(8,128)(2,1)}, bf16[288,512]{1,0:T(8,128)(2,1)}, u32[]{:S(2)}, u32[]{:S(2)}) collective-permute-start(bf16[288,512]{1,0:T(8,128)(2,1)} %constant_dynamic-slice_fusion.1), channel_id=1, source_target_pairs={{0,1},{1,0},{4,5},{5,4},{8,9},{9,8},{12,13},{13,12},{16,17},{17,16... | collective-permute-start | bytes 884744 | tf_op jit(solution)/shard_map/ppermute | solution.py:646
  78.3 0.2 add_convert_fusion.2
  78.5 4.4 %collective-permute-done.10 = bf16[288,512]{1,0:T(8,128)(2,1)S(1)} collective-permute-done((bf16[288,512]{1,0:T(8,128)(2,1)S(1)}, bf16[288,512]{1,0:T(8,128)(2,1)S(1)}, u32[]{:S(2)}, u32[]{:S(2)}) %collective-permute-start.10) | collective-permute-done | bytes 294944 | tf_op jit(solution)/shard_map/ppermute | solution.py:646
  82.9 0.8 add_convert_fusion.6
  83.7 0.7 constant_dynamic-slice_fusion.2
  84.4 1.5 %collective-permute-start.11 = (bf16[288,512]{1,0:T(8,128)(2,1)}, bf16[288,512]{1,0:T(8,128)(2,1)}, u32[]{:S(2)}, u32[]{:S(2)}) collective-permute-start(bf16[288,512]{1,0:T(8,128)(2,1)} %constant_dynamic-slice_fusion.2), channel_id=1, source_target_pairs={{0,1},{1,0},{2,3},{3,2},{4,5},{5,4},{6,7},{7,6},{8,9},{9,8},{10,11... | collective-permute-start | bytes 884744 | tf_op jit(solution)/shard_map/ppermute | solution.py:646
  86.0 1.4 %collective-permute-start.15 = (bf16[288,512]{1,0:T(8,128)(2,1)}, bf16[288,512]{1,0:T(8,128)(2,1)}, u32[]{:S(2)}, u32[]{:S(2)}) collective-permute-start(bf16[288,512]{1,0:T(8,128)(2,1)} %add_convert_fusion.6), channel_id=1, source_target_pairs={{4,0},{6,2},{8,4},{10,6},{12,8},{14,10},{16,12},{18,14},{20,16},{2... | collective-permute-start | bytes 884744 | tf_op jit(solution)/shard_map/ppermute | solution.py:595
  87.4 1.8 %add_convert_fusion.5 = bf16[288,512]{1,0:T(8,128)(2,1)} fusion(bf16[288,512]{1,0:T(8,128)(2,1)} %collective-permute-done.13, bf16[576,512]{1,0:T(8,128)(2,1)S(1)} %add_convert_fusion, s32[]{:T(128)S(6)} %select_n.66), kind=kLoop, calls=%fused_computation.10 | loop fusion | flops 589824 | bytes 884740 | tf_op jit(solution)/shard_map/convert_element_type | solution.py:668
  89.1 1.3 %collective-permute-start.14 = (bf16[288,512]{1,0:T(8,128)(2,1)}, bf16[288,512]{1,0:T(8,128)(2,1)}, u32[]{:S(2)}, u32[]{:S(2)}) collective-permute-start(bf16[288,512]{1,0:T(8,128)(2,1)} %add_convert_fusion.5), channel_id=1, source_target_pairs={{8,2},{12,6},{16,10},{20,14},{24,18},{28,22},{9,3},{13,7},{17,11},... | collective-permute-start | bytes 884744 | tf_op jit(solution)/shard_map/ppermute | solution.py:595
  90.5 3.0 %collective-permute-done.11 = bf16[288,512]{1,0:T(8,128)(2,1)} collective-permute-done((bf16[288,512]{1,0:T(8,128)(2,1)}, bf16[288,512]{1,0:T(8,128)(2,1)}, u32[]{:S(2)}, u32[]{:S(2)}) %collective-permute-start.11) | collective-permute-done | bytes 294944 | tf_op jit(solution)/shard_map/ppermute | solution.py:646
  93.5 2.0 %add_convert_fusion.3 = bf16[256,1024]{1,0:T(8,128)(2,1)} fusion(bf16[256,1024]{1,0:T(8,128)(2,1)} %collective-permute-done.17, bf16[256,1024]{1,0:T(8,128)(2,1)S(1)} %copy-done.3), kind=kLoop, calls=%fused_computation.5 | loop fusion | flops 1048576 | bytes 1572864 | tf_op jit(solution)/shard_map/convert_element_type | solution.py:676
  95.5 12.4 %all-to-all-start = ((bf16[4,64,1024]{2,1,0:T(8,128)(2,1)}), bf16[4,64,1024]{2,1,0:T(8,128)(2,1)S(1)}, u32[]{:S(2)}, u32[]{:S(2)}) async-start(bf16[4,64,1024]{2,1,0:T(8,128)(2,1)} %bitcast.4), calls=%async_computation | async-start | bytes 1048576 | tf_op jit(solution)/shard_map/all_to_all | solution.py:678
  107.9 0.1 broadcast_select_fusion.1
  108.1 1.3 %add_convert_fusion.4 = bf16[288,512]{1,0:T(8,128)(2,1)S(1)} fusion(bf16[288,512]{1,0:T(8,128)(2,1)} %collective-permute-done.15, bf16[288,512]{1,0:T(8,128)(2,1)} %collective-permute-done.14, bf16[288,512]{1,0:T(8,128)(2,1)} %collective-permute-done.11, bf16[576,512]{1,0:T(8,128)(2,1)S(1)} %add_convert_fusion.2, s32[]{:T(128)S(6)} %select_n.66), kind=kLoop, calls=%fused_computation.9 | loop fusion | flops 1179648 | bytes 1474564 | tf_op jit(solution)/shard_map/convert_element_type | solution.py:692
  109.4 0.6 collective-permute-start.16
  110.0 1.3 %pad_maximum_fusion = bf16[512,1536]{1,0:T(8,128)(2,1)} fusion(bf16[512,768]{1,0:T(8,128)(2,1)S(1)} %get-tuple-element.46, bf16[512,768]{1,0:T(8,128)(2,1)S(1)} %get-tuple-element.45), kind=kLoop, calls=%fused_computation | loop fusion | flops 3145728 | bytes 3145728 | tf_op jit(solution)/shard_map/concatenate | solution.py:685
  111.2 10.0 %all-to-all-done = bf16[4,64,1024]{2,1,0:T(8,128)(2,1)S(1)} async-done(((bf16[4,64,1024]{2,1,0:T(8,128)(2,1)}), bf16[4,64,1024]{2,1,0:T(8,128)(2,1)S(1)}, u32[]{:S(2)}, u32[]{:S(2)}) %all-to-all-start) | async-done | bytes 524320 | tf_op jit(solution)/shard_map/all_to_all | solution.py:678
  121.2 0.1 convert_reduce_fusion
  121.3 0.1 collective-permute-start.18
  121.5 0.9 maximum_bitcast_fusion
  122.3 0.4 collective-permute-done.18
  122.8 0.7 pad_maximum_fusion.1
  (38 shorter events, 0.2 us)
Async XLA Ops:
  0.6 1.9 %copy-start.4 = (bf16[512,1024]{1,0:T(8,128)(2,1)S(1)}, bf16[512,1024]{1,0:T(8,128)(2,1)}, u32[]{:S(2)}) copy-start(bf16[512,1024]{1,0:T(8,128)(2,1)} %do0.3) | copy-start | bytes 3145732
  0.6 2.5 %copy-start.6 = (bf16[512,576]{0,1:T(8,128)(2,1)S(1)}, bf16[512,576]{0,1:T(8,128)(2,1)}, u32[]{:S(2)}) copy-start(bf16[512,576]{0,1:T(8,128)(2,1)} %param.5) | copy-start | bytes 1769476
  2.0 6.4 %collective-permute-start = (bf16[512,768]{1,0:T(8,128)(2,1)S(1)}, bf16[512,768]{1,0:T(8,128)(2,1)S(1)}, u32[]{:S(2)}, u32[]{:S(2)}) collective-permute-start(bf16[512,768]{1,0:T(8,128)(2,1)S(1)} %constant_dynamic-slice_fusion.5), channel_id=1, source_target_pairs={{0,2},{2,0},{4,6},{6,4},{8,10},{10,8},{12,14},{14,12},{16,18},{18,... | collective-permute-start | bytes 2359304 | tf_op jit(solution)/shard_map/ppermute | solution.py:595
  2.5 5.9 %collective-permute-start.2 = (bf16[576,512]{1,0:T(8,128)(2,1)}, bf16[576,512]{1,0:T(8,128)(2,1)}, u32[]{:S(2)}, u32[]{:S(2)}) collective-permute-start(bf16[576,512]{1,0:T(8,128)(2,1)} %bitcast.6), channel_id=1, source_target_pairs={{0,2},{2,0},{4,6},{6,4},{8,10},{10,8},{12,14},{14,12},{16,18},{18,... | collective-permute-start | bytes 1769480 | tf_op jit(solution)/shard_map/ppermute | solution.py:595
  2.6 5.7 %collective-permute-start.1 = (bf16[512,512]{1,0:T(8,128)(2,1)S(1)}, bf16[512,512]{1,0:T(8,128)(2,1)S(1)}, u32[]{:S(2)}, u32[]{:S(2)}) collective-permute-start(bf16[512,512]{1,0:T(8,128)(2,1)S(1)} %constant_dynamic-slice_fusion.4), channel_id=1, source_target_pairs={{0,2},{2,0},{4,6},{6,4},{8,10},{10,8},{12,14},{14,12},{16,18},{18,... | collective-permute-start | bytes 1572872 | tf_op jit(solution)/shard_map/ppermute | solution.py:595
  3.1 19.6 %collective-permute-start.3 = (bf16[576,512]{1,0:T(8,128)(2,1)S(1)}, bf16[576,512]{1,0:T(8,128)(2,1)S(1)}, u32[]{:S(2)}, u32[]{:S(2)}) collective-permute-start(bf16[576,512]{1,0:T(8,128)(2,1)S(1)} %bitcast.9), channel_id=1, source_target_pairs={{0,4},{2,6},{4,8},{6,10},{8,12},{10,14},{12,16},{14,18},{16,20},{1... | collective-permute-start | bytes 1769480 | tf_op jit(solution)/shard_map/ppermute | solution.py:595
  7.6 15.1 %collective-permute-start.4 = (bf16[576,512]{1,0:T(8,128)(2,1)S(1)}, bf16[576,512]{1,0:T(8,128)(2,1)S(1)}, u32[]{:S(2)}, u32[]{:S(2)}) collective-permute-start(bf16[576,512]{1,0:T(8,128)(2,1)S(1)} %bitcast.10), channel_id=1, source_target_pairs={{2,8},{6,12},{10,16},{14,20},{18,24},{22,28},{3,9},{7,13},{11,17},... | collective-permute-start | bytes 1769480 | tf_op jit(solution)/shard_map/ppermute | solution.py:595
  8.3 0.8 copy-start.11
  8.4 1.0 copy-start.5
  22.7 6.5 %copy-start.7 = (bf16[576,512]{1,0:T(8,128)(2,1)}, bf16[576,512]{1,0:T(8,128)(2,1)S(1)}, u32[]{:S(2)}) copy-start(bf16[576,512]{1,0:T(8,128)(2,1)S(1)} %collective-permute-done.3.lat_far) | copy-start | bytes 1769476
  22.7 6.5 %copy-start.8 = (bf16[576,512]{1,0:T(8,128)(2,1)}, bf16[576,512]{1,0:T(8,128)(2,1)S(1)}, u32[]{:S(2)}) copy-start(bf16[576,512]{1,0:T(8,128)(2,1)S(1)} %collective-permute-done.4.lat_mixed) | copy-start | bytes 1769476
  22.7 4.9 %collective-permute-start.5 = (bf16[576,512]{1,0:T(8,128)(2,1)S(1)}, bf16[576,512]{1,0:T(8,128)(2,1)S(1)}, u32[]{:S(2)}, u32[]{:S(2)}) collective-permute-start(bf16[576,512]{1,0:T(8,128)(2,1)S(1)} %collective-permute-done.3.lat_far), channel_id=1, source_target_pairs={{0,2},{2,0},{4,6},{6,4},{8,10},{10,8},{12,14},{14,12},{16,18},{18,... | collective-permute-start | bytes 1769480 | tf_op jit(solution)/shard_map/ppermute | solution.py:595
  25.7 3.5 %collective-permute-start.6 = (bf16[576,512]{1,0:T(8,128)(2,1)S(1)}, bf16[576,512]{1,0:T(8,128)(2,1)S(1)}, u32[]{:S(2)}, u32[]{:S(2)}) collective-permute-start(bf16[576,512]{1,0:T(8,128)(2,1)S(1)} %collective-permute-done.4.lat_mixed), channel_id=1, source_target_pairs={{0,2},{4,6},{8,10},{12,14},{16,18},{20,22},{24,26},{28,30},{1,3},{... | collective-permute-start | bytes 1769480 | tf_op jit(solution)/shard_map/ppermute | solution.py:595
  27.6 1.6 %copy-start.9 = (bf16[576,512]{1,0:T(8,128)(2,1)}, bf16[576,512]{1,0:T(8,128)(2,1)S(1)}, u32[]{:S(2)}) copy-start(bf16[576,512]{1,0:T(8,128)(2,1)S(1)} %collective-permute-done.5.lat_swap) | copy-start | bytes 1769476
  29.2 0.8 copy-start.10
  53.7 21.3 %copy-start.2 = (bf16[576,512]{1,0:T(8,128)(2,1)S(1)}, bf16[576,512]{1,0:T(8,128)(2,1)}, u32[]{:S(2)}) copy-start(bf16[576,512]{1,0:T(8,128)(2,1)} %get-tuple-element.40) | copy-start | bytes 1769476
  53.7 18.4 %collective-permute-start.9 = (bf16[576,512]{1,0:T(8,128)(2,1)}, bf16[576,512]{1,0:T(8,128)(2,1)S(1)}, u32[]{:S(2)}, u32[]{:S(2)}) collective-permute-start(bf16[576,512]{1,0:T(8,128)(2,1)} %get-tuple-element.38), channel_id=1, source_target_pairs={{0,2},{2,0},{4,6},{6,4},{8,10},{10,8},{12,14},{14,12},{16,18},{18,... | collective-permute-start | bytes 1769480 | tf_op jit(solution)/shard_map/ppermute | solution.py:595
  54.4 20.6 %collective-permute-start.12 = (bf16[576,512]{1,0:T(8,128)(2,1)}, bf16[576,512]{1,0:T(8,128)(2,1)S(1)}, u32[]{:S(2)}, u32[]{:S(2)}) collective-permute-start(bf16[576,512]{1,0:T(8,128)(2,1)} %get-tuple-element.40), channel_id=1, source_target_pairs={{2,0},{6,4},{10,8},{14,12},{18,16},{22,20},{26,24},{30,28},{3,1},{... | collective-permute-start | bytes 1769480 | tf_op jit(solution)/shard_map/ppermute | solution.py:595
  55.7 22.7 %collective-permute-start.8 = (bf16[576,512]{1,0:T(8,128)(2,1)}, bf16[576,512]{1,0:T(8,128)(2,1)S(1)}, u32[]{:S(2)}, u32[]{:S(2)}) collective-permute-start(bf16[576,512]{1,0:T(8,128)(2,1)} %get-tuple-element.36), channel_id=1, source_target_pairs={{0,2},{2,0},{4,6},{6,4},{8,10},{10,8},{12,14},{14,12},{16,18},{18,... | collective-permute-start | bytes 1769480 | tf_op jit(solution)/shard_map/ppermute | solution.py:595
  56.9 36.6 %collective-permute-start.17 = (bf16[256,1024]{1,0:T(8,128)(2,1)}, bf16[256,1024]{1,0:T(8,128)(2,1)}, u32[]{:S(2)}, u32[]{:S(2)}) collective-permute-start(bf16[256,1024]{1,0:T(8,128)(2,1)} %get-tuple-element.43), channel_id=1, source_target_pairs={{0,4},{2,6},{4,0},{6,2},{8,12},{10,14},{12,8},{14,10},{16,20},{18,... | collective-permute-start | bytes 1572872 | tf_op jit(solution)/shard_map/ppermute | solution.py:595
  72.2 35.8 %collective-permute-start.7 = (bf16[512,768]{1,0:T(8,128)(2,1)}, bf16[512,768]{1,0:T(8,128)(2,1)S(1)}, u32[]{:S(2)}, u32[]{:S(2)}) collective-permute-start(bf16[512,768]{1,0:T(8,128)(2,1)} %get-tuple-element.34), channel_id=1, source_target_pairs={{0,2},{2,0},{4,6},{6,4},{8,10},{10,8},{12,14},{14,12},{16,18},{18,... | collective-permute-start | bytes 2359304 | tf_op jit(solution)/shard_map/ppermute | solution.py:595
  73.4 5.0 %copy-start.1 = (bf16[576,512]{1,0:T(8,128)(2,1)S(1)}, bf16[576,512]{1,0:T(8,128)(2,1)}, u32[]{:S(2)}) copy-start(bf16[576,512]{1,0:T(8,128)(2,1)} %get-tuple-element.35) | copy-start | bytes 1769476
  73.4 9.5 %collective-permute-start.10 = (bf16[288,512]{1,0:T(8,128)(2,1)S(1)}, bf16[288,512]{1,0:T(8,128)(2,1)S(1)}, u32[]{:S(2)}, u32[]{:S(2)}) collective-permute-start(bf16[288,512]{1,0:T(8,128)(2,1)S(1)} %constant_dynamic-slice_fusion.3), channel_id=1, source_target_pairs={{0,1},{1,0},{2,3},{3,2},{4,5},{5,4},{6,7},{7,6},{8,9},{9,8},{10,11... | collective-permute-start | bytes 884744 | tf_op jit(solution)/shard_map/ppermute | solution.py:646
  75.9 11.5 %collective-permute-start.13 = (bf16[288,512]{1,0:T(8,128)(2,1)}, bf16[288,512]{1,0:T(8,128)(2,1)}, u32[]{:S(2)}, u32[]{:S(2)}) collective-permute-start(bf16[288,512]{1,0:T(8,128)(2,1)} %constant_dynamic-slice_fusion.1), channel_id=1, source_target_pairs={{0,1},{1,0},{4,5},{5,4},{8,9},{9,8},{12,13},{13,12},{16,17},{17,16... | collective-permute-start | bytes 884744 | tf_op jit(solution)/shard_map/ppermute | solution.py:646
  78.5 15.0 %copy-start.3 = (bf16[256,1024]{1,0:T(8,128)(2,1)S(1)}, bf16[256,1024]{1,0:T(8,128)(2,1)}, u32[]{:S(2)}) copy-start(bf16[256,1024]{1,0:T(8,128)(2,1)} %get-tuple-element.42) | copy-start | bytes 1572868
  84.4 9.1 %collective-permute-start.11 = (bf16[288,512]{1,0:T(8,128)(2,1)}, bf16[288,512]{1,0:T(8,128)(2,1)}, u32[]{:S(2)}, u32[]{:S(2)}) collective-permute-start(bf16[288,512]{1,0:T(8,128)(2,1)} %constant_dynamic-slice_fusion.2), channel_id=1, source_target_pairs={{0,1},{1,0},{2,3},{3,2},{4,5},{5,4},{6,7},{7,6},{8,9},{9,8},{10,11... | collective-permute-start | bytes 884744 | tf_op jit(solution)/shard_map/ppermute | solution.py:646
  85.9 22.0 %copy-start = (bf16[512,768]{1,0:T(8,128)(2,1)S(1)}, bf16[512,768]{1,0:T(8,128)(2,1)}, u32[]{:S(2)}) copy-start(bf16[512,768]{1,0:T(8,128)(2,1)} %get-tuple-element.33) | copy-start | bytes 2359300
  86.0 22.1 %collective-permute-start.15 = (bf16[288,512]{1,0:T(8,128)(2,1)}, bf16[288,512]{1,0:T(8,128)(2,1)}, u32[]{:S(2)}, u32[]{:S(2)}) collective-permute-start(bf16[288,512]{1,0:T(8,128)(2,1)} %add_convert_fusion.6), channel_id=1, source_target_pairs={{4,0},{6,2},{8,4},{10,6},{12,8},{14,10},{16,12},{18,14},{20,16},{2... | collective-permute-start | bytes 884744 | tf_op jit(solution)/shard_map/ppermute | solution.py:595
  89.1 18.9 %collective-permute-start.14 = (bf16[288,512]{1,0:T(8,128)(2,1)}, bf16[288,512]{1,0:T(8,128)(2,1)}, u32[]{:S(2)}, u32[]{:S(2)}) collective-permute-start(bf16[288,512]{1,0:T(8,128)(2,1)} %add_convert_fusion.5), channel_id=1, source_target_pairs={{8,2},{12,6},{16,10},{20,14},{24,18},{28,22},{9,3},{13,7},{17,11},... | collective-permute-start | bytes 884744 | tf_op jit(solution)/shard_map/ppermute | solution.py:595
  95.5 25.7 %all-to-all-start = ((bf16[4,64,1024]{2,1,0:T(8,128)(2,1)}), bf16[4,64,1024]{2,1,0:T(8,128)(2,1)S(1)}, u32[]{:S(2)}, u32[]{:S(2)}) async-start(bf16[4,64,1024]{2,1,0:T(8,128)(2,1)} %bitcast.4), calls=%async_computation | async-start | bytes 1048576 | tf_op jit(solution)/shard_map/all_to_all | solution.py:678
  109.4 12.0 %collective-permute-start.16 = (bf16[288,512]{1,0:T(8,128)(2,1)S(1)}, bf16[288,512]{1,0:T(8,128)(2,1)S(1)}, u32[]{:S(2)}, u32[]{:S(2)}) collective-permute-start(bf16[288,512]{1,0:T(8,128)(2,1)S(1)} %add_convert_fusion.4), channel_id=1, source_target_pairs={{0,1},{1,0},{2,3},{3,2},{4,5},{5,4},{6,7},{7,6},{8,9},{9,8},{10,11... | collective-permute-start | bytes 884744 | tf_op jit(solution)/shard_map/ppermute | solution.py:646
  121.3 1.4 %collective-permute-start.18 = (f32[32,1024]{1,0:T(8,128)S(1)}, f32[32,1024]{1,0:T(8,128)S(1)}, u32[]{:S(2)}, u32[]{:S(2)}) collective-permute-start(f32[32,1024]{1,0:T(8,128)S(1)} %constant_dynamic-slice_fusion), channel_id=1, source_target_pairs={{0,2},{2,0},{4,6},{6,4},{8,10},{10,8},{12,14},{14,12},{16,18},{18,... | collective-permute-start | bytes 393224 | tf_op jit(solution)/shard_map/ppermute | solution.py:595

commit v4 on v2

--- a/solution.py
+++ b/solution.py
@@ -51,7 +51,7 @@
         v_out(h, lifted[:, NOPE:])
 
 
-def score_block(key, value, q_ref, do_ref, bounds, run_ref, raw_ref, graw_ref, keep):
+def score_block(key, value, q_ref, do_ref, bounds, run_ref, raw_ref, graw_ref, keep, limit):
     rows = do_ref.shape[0]
     lower, upper = bounds
     index = lax.broadcasted_iota(jnp.int32, (LANES, LANES), 0)
@@ -92,11 +92,11 @@
                 cross, axis=0, keepdims=True
             )
 
-    alternate(rows, do_ref.shape[1] // VDIM, multiply, weigh)
-
-
-def alternate(rows, heads, first, second):
-    pieces = [(h, c) for h in range(heads) for c in range(0, rows, PIECE)]
+    alternate(limit, do_ref.shape[1] // VDIM, multiply, weigh)
+
+
+def alternate(limit, heads, first, second):
+    pieces = [(h, c) for h in range(heads) for c in range(0, limit, PIECE)]
     first(*pieces[0])
     for now, following in zip(pieces, pieces[1:] + [None]):
         if following:
@@ -104,7 +104,7 @@
         second(*now)
 
 
-def grad_block(kept, key, top, end_ref, q_ref, do_ref, low_ref, ds_ref, dq_acc, d_acc, r_acc, first_q, first_k):
+def grad_block(kept, key, top, end_ref, q_ref, do_ref, low_ref, ds_ref, dq_acc, d_acc, r_acc, first_q, first_k, limit):
     def put(ref, part, value, first):
         ref[:, part] = value if first else ref[:, part] + value
 
@@ -139,13 +139,13 @@
         if first:
             dvalue, dkey = sums[h][0] + dvalue, sums[h][1] + dkey
         sums[h] = dvalue, dkey
-        if first + PIECE == rows:
+        if first + PIECE == limit:
             dkey = dkey * SCALE
             put(d_acc, slice(h * KV, h * KV + NOPE), dkey[:, :NOPE], first_k)
             put(d_acc, slice(h * KV + NOPE, (h + 1) * KV), dvalue, first_k)
             put(r_acc, slice(0, ROPE), dkey[:, NOPE:], first_k and h == 0)
 
-    alternate(rows, heads, weigh, multiply)
+    alternate(limit, heads, weigh, multiply)
 
 
 def start_stats(run_ref):
@@ -230,7 +230,7 @@
         score_block(
             lambda h: k_ref[0, slot * heads + h], lambda h: v_ref[slot * heads + h],
             q_ref.at[j], do_ref.at[j], query_bounds(start_ref, chip, j, t, rows), run,
-            raw_ref, graw_ref, keep,
+            raw_ref, graw_ref, keep, rows,
         )
         for h in range(heads):
             top_ref[0, n * heads + h] = run[h]
@@ -260,6 +260,14 @@
         block = chip + t - REACH
         last_doc = docs_sref[jnp.maximum(block, 0) * rows + rows - 1]
         return (block >= 0) & (last_doc >= docs_sref[(chip + j) * rows])
+
+    def wide(j, t):
+        last_doc = docs_sref[jnp.maximum(chip + t - REACH, 0) * rows + rows - 1]
+        return last_doc >= docs_sref[(chip + j) * rows + PIECE]
+
+    def by_width(j, t, body):
+        pl.when(wide(j, t))(lambda: body(t, rows))
+        pl.when(~wide(j, t))(lambda: body(t, PIECE))
 
     def block_rows(t):
         return pl.ds(pl.multiple_of(t * rows, rows), rows)
@@ -325,7 +333,7 @@
         for h in range(heads):
             run_ref[h] = local_run[0, j * heads + h]
 
-        def first_pass(t):
+        def first_pass(t, limit):
             def keep(h, part, cols, weights, grads):
                 e_ref[h, piece_rows(t, part), cols] = weights
                 g_ref[h, piece_rows(t, part), cols] = grads
@@ -333,31 +341,31 @@
             score_block(
                 lambda h: k_ref[h, block_rows(t), :], lambda h: v_ref[h, block_rows(t), :],
                 q_ref.at[j], do_ref.at[j], query_bounds(start_ref, chip, j, t, rows), run_ref,
-                raw_ref, graw_ref, keep,
+                raw_ref, graw_ref, keep, limit,
             )
             for h in range(heads):
                 top_ref[h, t] = run_ref[h]
 
-        loop(j, REACH, lambda t: active(j, t), first_pass)
+        loop(j, REACH, lambda t: active(j, t), lambda t: by_width(j, t, first_pass))
         for h in range(heads):
             inverse = 1.0 / run_ref[h, 1:2, :]
             end_ref[h, 0:1, :] = run_ref[h, 0:1, :]
             end_ref[h, 1:2, :] = inverse
             end_ref[h, 2:3, :] = run_ref[h, 2:3, :] * inverse
 
-        def add(t, kept, key, top, first_q, first_k):
+        def add(t, kept, key, top, first_q, first_k, limit=rows):
             grad_block(
                 kept, key, top, end_ref, q_ref.at[j], do_ref.at[j], low_ref, ds_ref, dq_acc.at[j], d_acc.at[t],
-                r_acc.at[t], first_q, first_k,
+                r_acc.at[t], first_q, first_k, limit,
             )
 
-        def second_pass(t):
+        def second_pass(t, limit):
             def kept(h, part, cols):
                 return e_ref[h, piece_rows(t, part), cols], g_ref[h, piece_rows(t, part), cols]
 
             add(
                 t, kept, lambda h: k_ref[h, block_rows(t), :], lambda h: top_ref[h, t, 0:1, :],
-                False, j == 0,
+                False, j == 0, limit,
             )
 
         if j == 0:
@@ -376,7 +384,7 @@
                     first_q, t == REACH + j,
                 )
                 first_q = False
-        loop(j, REACH, lambda t: active(j, t), second_pass)
+        loop(j, REACH, lambda t: active(j, t), lambda t: by_width(j, t, second_pass))
 
     def seen(t):
         return (t >= REACH) | active(0, t)

time: 123 us -> 123 us (level)
  the two profiles are of different devices: /device:TPU:0 before, /device:TPU:14 now
where the time goes in v4:
time: 123 us; the launch traced here: 122 us
  Pallas kernels  48 us (39%)
  starting transfers between devices  34.4 us (28%)
  waiting for transfers between devices  28 us (23%)
  other arithmetic  6.97 us (6%)
  local copies, waits for them, and re-layouts  3.32 us (3%)
    pallas_call x1, Pallas kernels, attention(): call(functools.partial(main_kernel, ranks), steps, 2 * steps * heads * ro...  34.6 us
    ppermute x4, waiting for transfers between devices, turned(): return lax.ppermute(value, ('ctx', 'head'), turns)  20.7 us
    ppermute x15, starting transfers between devices, permute(): return lax.ppermute(value, axis, pairs)  16.1 us
    pallas_call x1, Pallas kernels, local_scores(): call(local_kernel, steps, 2 * steps * heads * rows * rows * (3 * (QK + VD...  13.3 us
    all_to_all x1, starting transfers between devices, local(): lax.all_to_all(plane, 'ctx', 0, 0, axis_index_groups=columns, tiled=True)  13.1 us
    ppermute x15, waiting for transfers between devices, permute(): return lax.ppermute(value, axis, pairs)  7.32 us
    ppermute x4, starting transfers between devices, turned(): return lax.ppermute(value, ('ctx', 'head'), turns)  5.23 us
  transfers between devices with their start and end apart: 20, of which 7 were waited for; matrix products, arithmetic and copies ran while one was open for 5% of the time, Pallas kernels for 11%

profile of v4, /device:TPU:14, one launch (start us, length us, event | category | flops | bytes accessed | tf_op | source)
XLA Modules:
  0.0 121.7 jit_solution(2169904986666128509)
XLA Ops:
  0.6 0.0 copy-start.4
  0.6 0.0 copy-start.6
  0.7 1.3 %constant_dynamic-slice_fusion.5 = bf16[512,768]{1,0:T(8,128)(2,1)S(1)} fusion(bf16[512,1536]{1,0:T(8,128)(2,1)} %q0.3, s32[]{:T(128)S(6)} %select_n.61), kind=kLoop, calls=%fused_computation.22 | loop fusion | bytes 1572868 | tf_op jit(solution)/shard_map/dynamic_slice | solution.py:609
  2.0 0.1 collective-permute-start
  2.1 0.5 collective-permute-start.2
  2.6 0.1 collective-permute-start.1
  2.7 3.4 %collective-permute-start.3 = (bf16[576,512]{1,0:T(8,128)(2,1)S(1)}, bf16[576,512]{1,0:T(8,128)(2,1)S(1)}, u32[]{:S(2)}, u32[]{:S(2)}) collective-permute-start(bf16[576,512]{1,0:T(8,128)(2,1)S(1)} %bitcast.9), channel_id=1, source_target_pairs={{0,4},{2,6},{4,8},{6,10},{8,12},{10,14},{12,16},{14,18},{16,20},{1... | collective-permute-start | bytes 1769480 | tf_op jit(solution)/shard_map/ppermute | solution.py:594
  6.2 1.3 %collective-permute-start.4 = (bf16[576,512]{1,0:T(8,128)(2,1)S(1)}, bf16[576,512]{1,0:T(8,128)(2,1)S(1)}, u32[]{:S(2)}, u32[]{:S(2)}) collective-permute-start(bf16[576,512]{1,0:T(8,128)(2,1)S(1)} %bitcast.10), channel_id=1, source_target_pairs={{2,8},{6,12},{10,16},{14,20},{18,24},{22,28},{3,9},{7,13},{11,17},... | collective-permute-start | bytes 1769480 | tf_op jit(solution)/shard_map/ppermute | solution.py:594
  7.5 0.0 collective-permute-done.2.lat1.lat_other
  7.5 0.0 copy-start.5
  7.5 0.8 copy-done.11
  8.3 0.2 copy-done.5
  8.6 13.3 %local_scores.1 = (bf16[2,6,512,512]{3,2,1,0:T(8,128)(2,1)}, bf16[2,6,512,512]{3,2,1,0:T(8,128)(2,1)}, bf16[2,4,512,192]{3,2,1,0:T(8,128)(2,1)}, f32[2,4,8,512]{...) custom-call(s32[1]{0:T(128)} %bitcast.index_ref, s32[1,8192]{1,0:T(1,128)} %bitcast.11, ...), custom_call_target="tpu_custom_call" | custom-call | flops 3087007744 | bytes 16777216 | tf_op jit(solution)/shard_map/local_scores/pallas_call | solution.py:513
  21.9 0.0 copy-start.7
  21.9 4.7 %collective-permute-done.4.lat_mixed = bf16[576,512]{1,0:T(8,128)(2,1)S(1)} collective-permute-done((bf16[576,512]{1,0:T(8,128)(2,1)S(1)}, bf16[576,512]{1,0:T(8,128)(2,1)S(1)}, u32[]{:S(2)}, u32[]{:S(2)}) %collective-permute-start.4) | collective-permute-done | bytes 589856 | tf_op jit(solution)/shard_map/ppermute | solution.py:594
  26.6 2.4 %collective-permute-start.6 = (bf16[576,512]{1,0:T(8,128)(2,1)S(1)}, bf16[576,512]{1,0:T(8,128)(2,1)S(1)}, u32[]{:S(2)}, u32[]{:S(2)}) collective-permute-start(bf16[576,512]{1,0:T(8,128)(2,1)S(1)} %collective-permute-done.4.lat_mixed), channel_id=1, source_target_pairs={{0,2},{4,6},{8,10},{12,14},{16,18},{20,22},{24,26},{28,30},{1,3},{... | collective-permute-start | bytes 1769480 | tf_op jit(solution)/shard_map/ppermute | solution.py:594
  29.1 1.6 %collective-permute-done.6.lat_passed = bf16[576,512]{1,0:T(8,128)(2,1)S(1)} collective-permute-done((bf16[576,512]{1,0:T(8,128)(2,1)S(1)}, bf16[576,512]{1,0:T(8,128)(2,1)S(1)}, u32[]{:S(2)}, u32[]{:S(2)}) %collective-permute-start.6) | collective-permute-done | bytes 589856 | tf_op jit(solution)/shard_map/ppermute | solution.py:594
  30.6 0.8 copy-done.10
  31.5 34.6 %attention.1 = (bf16[512,768]{1,0:T(8,128)(2,1)}, bf16[512,768]{1,0:T(8,128)(2,1)}, bf16[256,1024]{1,0:T(8,128)(2,1)}, bf16[256,1024]{1,0:T(8,128)(2,1)}, bf16[5...) custom-call(s32[1]{0:T(128)} %bitcast.index_ref, ...), custom_call_target="tpu_custom_call" | custom-call | flops 18924699648 | bytes 16777216 | tf_op jit(solution)/shard_map/attention/pallas_call | solution.py:548
  66.1 1.4 %collective-permute-start.12 = (bf16[576,512]{1,0:T(8,128)(2,1)}, bf16[576,512]{1,0:T(8,128)(2,1)S(1)}, u32[]{:S(2)}, u32[]{:S(2)}) collective-permute-start(bf16[576,512]{1,0:T(8,128)(2,1)} %get-tuple-element.39), channel_id=1, source_target_pairs={{2,0},{6,4},{10,8},{14,12},{18,16},{22,20},{26,24},{30,28},{3,1},{... | collective-permute-start | bytes 1769480 | tf_op jit(solution)/shard_map/ppermute | solution.py:594
  67.5 1.4 %collective-permute-start.9 = (bf16[576,512]{1,0:T(8,128)(2,1)}, bf16[576,512]{1,0:T(8,128)(2,1)S(1)}, u32[]{:S(2)}, u32[]{:S(2)}) collective-permute-start(bf16[576,512]{1,0:T(8,128)(2,1)} %get-tuple-element.37), channel_id=1, source_target_pairs={{0,2},{2,0},{4,6},{6,4},{8,10},{10,8},{12,14},{14,12},{16,18},{18,... | collective-permute-start | bytes 1769480 | tf_op jit(solution)/shard_map/ppermute | solution.py:594
  68.9 0.2 collective-permute-start.8
  69.1 0.3 collective-permute-start.7
  69.5 1.1 collective-permute-done.12
  70.5 1.2 add_convert_fusion
  71.8 2.5 %collective-permute-start.13 = (bf16[288,512]{1,0:T(8,128)(2,1)S(1)}, bf16[288,512]{1,0:T(8,128)(2,1)S(1)}, u32[]{:S(2)}, u32[]{:S(2)}) collective-permute-start(bf16[288,512]{1,0:T(8,128)(2,1)S(1)} %constant_dynamic-slice_fusion.1), channel_id=1, source_target_pairs={{0,1},{1,0},{4,5},{5,4},{8,9},{9,8},{12,13},{13,12},{16,17},{17,16... | collective-permute-start | bytes 884744 | tf_op jit(solution)/shard_map/ppermute | solution.py:645
  74.4 0.2 add_convert_fusion.1
  74.6 1.6 %collective-permute-start.10 = (bf16[288,512]{1,0:T(8,128)(2,1)S(1)}, bf16[288,512]{1,0:T(8,128)(2,1)S(1)}, u32[]{:S(2)}, u32[]{:S(2)}) collective-permute-start(bf16[288,512]{1,0:T(8,128)(2,1)S(1)} %constant_dynamic-slice_fusion.3), channel_id=1, source_target_pairs={{0,1},{1,0},{2,3},{3,2},{4,5},{5,4},{6,7},{7,6},{8,9},{9,8},{10,11... | collective-permute-start | bytes 884744 | tf_op jit(solution)/shard_map/ppermute | solution.py:645
  76.2 0.2 add_convert_fusion.2
  76.3 5.6 %collective-permute-done.13 = bf16[288,512]{1,0:T(8,128)(2,1)S(1)} collective-permute-done((bf16[288,512]{1,0:T(8,128)(2,1)S(1)}, bf16[288,512]{1,0:T(8,128)(2,1)S(1)}, u32[]{:S(2)}, u32[]{:S(2)}) %collective-permute-start.13) | collective-permute-done | bytes 294944 | tf_op jit(solution)/shard_map/ppermute | solution.py:645
  81.9 0.1 add_convert_fusion.5
  82.0 2.0 %collective-permute-start.14 = (bf16[288,512]{1,0:T(8,128)(2,1)S(1)}, bf16[288,512]{1,0:T(8,128)(2,1)}, u32[]{:S(2)}, u32[]{:S(2)}) collective-permute-start(bf16[288,512]{1,0:T(8,128)(2,1)S(1)} %add_convert_fusion.5), channel_id=1, source_target_pairs={{8,2},{12,6},{16,10},{20,14},{24,18},{28,22},{9,3},{13,7},{17,11},... | collective-permute-start | bytes 884744 | tf_op jit(solution)/shard_map/ppermute | solution.py:594
  84.0 1.0 collective-permute-done.10
  85.1 0.1 add_convert_fusion.6
  85.2 2.7 %collective-permute-start.15 = (bf16[288,512]{1,0:T(8,128)(2,1)S(1)}, bf16[288,512]{1,0:T(8,128)(2,1)}, u32[]{:S(2)}, u32[]{:S(2)}) collective-permute-start(bf16[288,512]{1,0:T(8,128)(2,1)S(1)} %add_convert_fusion.6), channel_id=1, source_target_pairs={{4,0},{6,2},{8,4},{10,6},{12,8},{14,10},{16,12},{18,14},{20,16},{2... | collective-permute-start | bytes 884744 | tf_op jit(solution)/shard_map/ppermute | solution.py:594
  88.0 1.0 add_convert_fusion.3
  89.0 13.1 %all-to-all-start = ((bf16[4,64,1024]{2,1,0:T(8,128)(2,1)}), bf16[4,64,1024]{2,1,0:T(8,128)(2,1)S(1)}, u32[]{:S(2)}, u32[]{:S(2)}) async-start(bf16[4,64,1024]{2,1,0:T(8,128)(2,1)} %bitcast.4), calls=%async_computation | async-start | bytes 1048576 | tf_op jit(solution)/shard_map/all_to_all | solution.py:673
  102.1 0.5 collective-permute-start.11
  102.6 0.1 broadcast_select_fusion.1
  102.8 9.2 %collective-permute-done.11 = bf16[288,512]{1,0:T(8,128)(2,1)S(1)} collective-permute-done((bf16[288,512]{1,0:T(8,128)(2,1)S(1)}, bf16[288,512]{1,0:T(8,128)(2,1)S(1)}, u32[]{:S(2)}, u32[]{:S(2)}) %collective-permute-start.11) | collective-permute-done | bytes 294944 | tf_op jit(solution)/shard_map/ppermute | solution.py:645
  112.0 1.2 add_convert_fusion.4
  113.2 0.5 collective-permute-start.16
  113.8 1.3 %pad_maximum_fusion = bf16[512,1536]{1,0:T(8,128)(2,1)} fusion(bf16[512,768]{1,0:T(8,128)(2,1)S(1)} %get-tuple-element.44, bf16[512,768]{1,0:T(8,128)(2,1)S(1)} %get-tuple-element.43), kind=kLoop, calls=%fused_computation | loop fusion | flops 3145728 | bytes 3145728 | tf_op jit(solution)/shard_map/concatenate | solution.py:680
  115.0 0.1 convert_reduce_fusion
  115.1 0.1 collective-permute-start.18
  115.2 4.8 %collective-permute-done.16 = bf16[288,512]{1,0:T(8,128)(2,1)S(1)} collective-permute-done((bf16[288,512]{1,0:T(8,128)(2,1)S(1)}, bf16[288,512]{1,0:T(8,128)(2,1)S(1)}, u32[]{:S(2)}, u32[]{:S(2)}) %collective-permute-start.16) | collective-permute-done | bytes 294944 | tf_op jit(solution)/shard_map/ppermute | solution.py:645
  120.0 0.9 maximum_bitcast_fusion
  120.9 0.7 pad_maximum_fusion.1
  (38 shorter events, 0.3 us)
Async XLA Ops:
  0.6 1.9 %copy-start.4 = (bf16[512,1024]{1,0:T(8,128)(2,1)S(1)}, bf16[512,1024]{1,0:T(8,128)(2,1)}, u32[]{:S(2)}) copy-start(bf16[512,1024]{1,0:T(8,128)(2,1)} %do0.3) | copy-start | bytes 3145732
  0.6 2.1 %copy-start.6 = (bf16[512,576]{0,1:T(8,128)(2,1)S(1)}, bf16[512,576]{0,1:T(8,128)(2,1)}, u32[]{:S(2)}) copy-start(bf16[512,576]{0,1:T(8,128)(2,1)} %param.5) | copy-start | bytes 1769476
  2.0 5.6 %collective-permute-start = (bf16[512,768]{1,0:T(8,128)(2,1)S(1)}, bf16[512,768]{1,0:T(8,128)(2,1)S(1)}, u32[]{:S(2)}, u32[]{:S(2)}) collective-permute-start(bf16[512,768]{1,0:T(8,128)(2,1)S(1)} %constant_dynamic-slice_fusion.5), channel_id=1, source_target_pairs={{0,2},{2,0},{4,6},{6,4},{8,10},{10,8},{12,14},{14,12},{16,18},{18,... | collective-permute-start | bytes 2359304 | tf_op jit(solution)/shard_map/ppermute | solution.py:594
  2.1 5.5 %collective-permute-start.2 = (bf16[576,512]{1,0:T(8,128)(2,1)}, bf16[576,512]{1,0:T(8,128)(2,1)}, u32[]{:S(2)}, u32[]{:S(2)}) collective-permute-start(bf16[576,512]{1,0:T(8,128)(2,1)} %bitcast.6), channel_id=1, source_target_pairs={{0,2},{2,0},{4,6},{6,4},{8,10},{10,8},{12,14},{14,12},{16,18},{18,... | collective-permute-start | bytes 1769480 | tf_op jit(solution)/shard_map/ppermute | solution.py:594
  2.6 4.9 %collective-permute-start.1 = (bf16[512,512]{1,0:T(8,128)(2,1)S(1)}, bf16[512,512]{1,0:T(8,128)(2,1)S(1)}, u32[]{:S(2)}, u32[]{:S(2)}) collective-permute-start(bf16[512,512]{1,0:T(8,128)(2,1)S(1)} %constant_dynamic-slice_fusion.4), channel_id=1, source_target_pairs={{0,2},{2,0},{4,6},{6,4},{8,10},{10,8},{12,14},{14,12},{16,18},{18,... | collective-permute-start | bytes 1572872 | tf_op jit(solution)/shard_map/ppermute | solution.py:594
  2.7 19.2 %collective-permute-start.3 = (bf16[576,512]{1,0:T(8,128)(2,1)S(1)}, bf16[576,512]{1,0:T(8,128)(2,1)S(1)}, u32[]{:S(2)}, u32[]{:S(2)}) collective-permute-start(bf16[576,512]{1,0:T(8,128)(2,1)S(1)} %bitcast.9), channel_id=1, source_target_pairs={{0,4},{2,6},{4,8},{6,10},{8,12},{10,14},{12,16},{14,18},{16,20},{1... | collective-permute-start | bytes 1769480 | tf_op jit(solution)/shard_map/ppermute | solution.py:594
  6.2 20.4 %collective-permute-start.4 = (bf16[576,512]{1,0:T(8,128)(2,1)S(1)}, bf16[576,512]{1,0:T(8,128)(2,1)S(1)}, u32[]{:S(2)}, u32[]{:S(2)}) collective-permute-start(bf16[576,512]{1,0:T(8,128)(2,1)S(1)} %bitcast.10), channel_id=1, source_target_pairs={{2,8},{6,12},{10,16},{14,20},{18,24},{22,28},{3,9},{7,13},{11,17},... | collective-permute-start | bytes 1769480 | tf_op jit(solution)/shard_map/ppermute | solution.py:594
  7.5 0.8 copy-start.11
  7.5 1.0 copy-start.5
  21.9 8.7 %copy-start.7 = (bf16[576,512]{1,0:T(8,128)(2,1)}, bf16[576,512]{1,0:T(8,128)(2,1)S(1)}, u32[]{:S(2)}) copy-start(bf16[576,512]{1,0:T(8,128)(2,1)S(1)} %collective-permute-done.3.lat_far) | copy-start | bytes 1769476
  26.6 4.0 %copy-start.8 = (bf16[576,512]{1,0:T(8,128)(2,1)}, bf16[576,512]{1,0:T(8,128)(2,1)S(1)}, u32[]{:S(2)}) copy-start(bf16[576,512]{1,0:T(8,128)(2,1)S(1)} %collective-permute-done.4.lat_mixed) | copy-start | bytes 1769476
  26.6 2.5 %collective-permute-start.5 = (bf16[576,512]{1,0:T(8,128)(2,1)S(1)}, bf16[576,512]{1,0:T(8,128)(2,1)S(1)}, u32[]{:S(2)}, u32[]{:S(2)}) collective-permute-start(bf16[576,512]{1,0:T(8,128)(2,1)S(1)} %collective-permute-done.3.lat_far), channel_id=1, source_target_pairs={{0,2},{2,0},{4,6},{6,4},{8,10},{10,8},{12,14},{14,12},{16,18},{18,... | collective-permute-start | bytes 1769480 | tf_op jit(solution)/shard_map/ppermute | solution.py:594
  26.6 4.0 %collective-permute-start.6 = (bf16[576,512]{1,0:T(8,128)(2,1)S(1)}, bf16[576,512]{1,0:T(8,128)(2,1)S(1)}, u32[]{:S(2)}, u32[]{:S(2)}) collective-permute-start(bf16[576,512]{1,0:T(8,128)(2,1)S(1)} %collective-permute-done.4.lat_mixed), channel_id=1, source_target_pairs={{0,2},{4,6},{8,10},{12,14},{16,18},{20,22},{24,26},{28,30},{1,3},{... | collective-permute-start | bytes 1769480 | tf_op jit(solution)/shard_map/ppermute | solution.py:594
  29.0 1.6 %copy-start.9 = (bf16[576,512]{1,0:T(8,128)(2,1)}, bf16[576,512]{1,0:T(8,128)(2,1)S(1)}, u32[]{:S(2)}) copy-start(bf16[576,512]{1,0:T(8,128)(2,1)S(1)} %collective-permute-done.5.lat_swap) | copy-start | bytes 1769476
  30.6 0.8 copy-start.10
  66.1 8.3 %copy-start.2 = (bf16[576,512]{1,0:T(8,128)(2,1)S(1)}, bf16[576,512]{1,0:T(8,128)(2,1)}, u32[]{:S(2)}) copy-start(bf16[576,512]{1,0:T(8,128)(2,1)} %get-tuple-element.36) | copy-start | bytes 1769476
  66.1 4.4 %collective-permute-start.12 = (bf16[576,512]{1,0:T(8,128)(2,1)}, bf16[576,512]{1,0:T(8,128)(2,1)S(1)}, u32[]{:S(2)}, u32[]{:S(2)}) collective-permute-start(bf16[576,512]{1,0:T(8,128)(2,1)} %get-tuple-element.39), channel_id=1, source_target_pairs={{2,0},{6,4},{10,8},{14,12},{18,16},{22,20},{26,24},{30,28},{3,1},{... | collective-permute-start | bytes 1769480 | tf_op jit(solution)/shard_map/ppermute | solution.py:594
  67.5 6.8 %collective-permute-start.9 = (bf16[576,512]{1,0:T(8,128)(2,1)}, bf16[576,512]{1,0:T(8,128)(2,1)S(1)}, u32[]{:S(2)}, u32[]{:S(2)}) collective-permute-start(bf16[576,512]{1,0:T(8,128)(2,1)} %get-tuple-element.37), channel_id=1, source_target_pairs={{0,2},{2,0},{4,6},{6,4},{8,10},{10,8},{12,14},{14,12},{16,18},{18,... | collective-permute-start | bytes 1769480 | tf_op jit(solution)/shard_map/ppermute | solution.py:594
  68.9 19.0 %collective-permute-start.17 = (bf16[256,1024]{1,0:T(8,128)(2,1)}, bf16[256,1024]{1,0:T(8,128)(2,1)S(1)}, u32[]{:S(2)}, u32[]{:S(2)}) collective-permute-start(bf16[256,1024]{1,0:T(8,128)(2,1)} %get-tuple-element.41), channel_id=1, source_target_pairs={{0,4},{2,6},{4,0},{6,2},{8,12},{10,14},{12,8},{14,10},{16,20},{18,... | collective-permute-start | bytes 1572872 | tf_op jit(solution)/shard_map/ppermute | solution.py:594
  68.9 7.2 %collective-permute-start.8 = (bf16[576,512]{1,0:T(8,128)(2,1)}, bf16[576,512]{1,0:T(8,128)(2,1)S(1)}, u32[]{:S(2)}, u32[]{:S(2)}) collective-permute-start(bf16[576,512]{1,0:T(8,128)(2,1)} %get-tuple-element.35), channel_id=1, source_target_pairs={{0,2},{2,0},{4,6},{6,4},{8,10},{10,8},{12,14},{14,12},{16,18},{18,... | collective-permute-start | bytes 1769480 | tf_op jit(solution)/shard_map/ppermute | solution.py:594
  69.1 33.5 %collective-permute-start.7 = (bf16[512,768]{1,0:T(8,128)(2,1)}, bf16[512,768]{1,0:T(8,128)(2,1)S(1)}, u32[]{:S(2)}, u32[]{:S(2)}) collective-permute-start(bf16[512,768]{1,0:T(8,128)(2,1)} %get-tuple-element.33), channel_id=1, source_target_pairs={{0,2},{2,0},{4,6},{6,4},{8,10},{10,8},{12,14},{14,12},{16,18},{18,... | collective-permute-start | bytes 2359304 | tf_op jit(solution)/shard_map/ppermute | solution.py:594
  71.7 4.4 %copy-start.1 = (bf16[576,512]{1,0:T(8,128)(2,1)S(1)}, bf16[576,512]{1,0:T(8,128)(2,1)}, u32[]{:S(2)}) copy-start(bf16[576,512]{1,0:T(8,128)(2,1)} %get-tuple-element.34) | copy-start | bytes 1769476
  71.8 10.2 %collective-permute-start.13 = (bf16[288,512]{1,0:T(8,128)(2,1)S(1)}, bf16[288,512]{1,0:T(8,128)(2,1)S(1)}, u32[]{:S(2)}, u32[]{:S(2)}) collective-permute-start(bf16[288,512]{1,0:T(8,128)(2,1)S(1)} %constant_dynamic-slice_fusion.1), channel_id=1, source_target_pairs={{0,1},{1,0},{4,5},{5,4},{8,9},{9,8},{12,13},{13,12},{16,17},{17,16... | collective-permute-start | bytes 884744 | tf_op jit(solution)/shard_map/ppermute | solution.py:645
  74.6 10.5 %collective-permute-start.10 = (bf16[288,512]{1,0:T(8,128)(2,1)S(1)}, bf16[288,512]{1,0:T(8,128)(2,1)S(1)}, u32[]{:S(2)}, u32[]{:S(2)}) collective-permute-start(bf16[288,512]{1,0:T(8,128)(2,1)S(1)} %constant_dynamic-slice_fusion.3), channel_id=1, source_target_pairs={{0,1},{1,0},{2,3},{3,2},{4,5},{5,4},{6,7},{7,6},{8,9},{9,8},{10,11... | collective-permute-start | bytes 884744 | tf_op jit(solution)/shard_map/ppermute | solution.py:645
  76.1 11.8 %copy-start.3 = (bf16[256,1024]{1,0:T(8,128)(2,1)S(1)}, bf16[256,1024]{1,0:T(8,128)(2,1)}, u32[]{:S(2)}) copy-start(bf16[256,1024]{1,0:T(8,128)(2,1)} %get-tuple-element.40) | copy-start | bytes 1572868
  82.0 30.0 %collective-permute-start.14 = (bf16[288,512]{1,0:T(8,128)(2,1)S(1)}, bf16[288,512]{1,0:T(8,128)(2,1)}, u32[]{:S(2)}, u32[]{:S(2)}) collective-permute-start(bf16[288,512]{1,0:T(8,128)(2,1)S(1)} %add_convert_fusion.5), channel_id=1, source_target_pairs={{8,2},{12,6},{16,10},{20,14},{24,18},{28,22},{9,3},{13,7},{17,11},... | collective-permute-start | bytes 884744 | tf_op jit(solution)/shard_map/ppermute | solution.py:594
  85.2 26.8 %collective-permute-start.15 = (bf16[288,512]{1,0:T(8,128)(2,1)S(1)}, bf16[288,512]{1,0:T(8,128)(2,1)}, u32[]{:S(2)}, u32[]{:S(2)}) collective-permute-start(bf16[288,512]{1,0:T(8,128)(2,1)S(1)} %add_convert_fusion.6), channel_id=1, source_target_pairs={{4,0},{6,2},{8,4},{10,6},{12,8},{14,10},{16,12},{18,14},{20,16},{2... | collective-permute-start | bytes 884744 | tf_op jit(solution)/shard_map/ppermute | solution.py:594
  88.0 14.7 %copy-start = (bf16[512,768]{1,0:T(8,128)(2,1)S(1)}, bf16[512,768]{1,0:T(8,128)(2,1)}, u32[]{:S(2)}) copy-start(bf16[512,768]{1,0:T(8,128)(2,1)} %get-tuple-element.32) | copy-start | bytes 2359300
  89.0 26.1 %all-to-all-start = ((bf16[4,64,1024]{2,1,0:T(8,128)(2,1)}), bf16[4,64,1024]{2,1,0:T(8,128)(2,1)S(1)}, u32[]{:S(2)}, u32[]{:S(2)}) async-start(bf16[4,64,1024]{2,1,0:T(8,128)(2,1)} %bitcast.4), calls=%async_computation | async-start | bytes 1048576 | tf_op jit(solution)/shard_map/all_to_all | solution.py:673
  102.1 9.9 %collective-permute-start.11 = (bf16[288,512]{1,0:T(8,128)(2,1)S(1)}, bf16[288,512]{1,0:T(8,128)(2,1)S(1)}, u32[]{:S(2)}, u32[]{:S(2)}) collective-permute-start(bf16[288,512]{1,0:T(8,128)(2,1)S(1)} %constant_dynamic-slice_fusion.2), channel_id=1, source_target_pairs={{0,1},{1,0},{2,3},{3,2},{4,5},{5,4},{6,7},{7,6},{8,9},{9,8},{10,11... | collective-permute-start | bytes 884744 | tf_op jit(solution)/shard_map/ppermute | solution.py:645
  113.2 6.8 %collective-permute-start.16 = (bf16[288,512]{1,0:T(8,128)(2,1)S(1)}, bf16[288,512]{1,0:T(8,128)(2,1)S(1)}, u32[]{:S(2)}, u32[]{:S(2)}) collective-permute-start(bf16[288,512]{1,0:T(8,128)(2,1)S(1)} %add_convert_fusion.4), channel_id=1, source_target_pairs={{0,1},{1,0},{2,3},{3,2},{4,5},{5,4},{6,7},{7,6},{8,9},{9,8},{10,11... | collective-permute-start | bytes 884744 | tf_op jit(solution)/shard_map/ppermute | solution.py:645
  115.1 5.8 %collective-permute-start.18 = (f32[32,1024]{1,0:T(8,128)S(1)}, f32[32,1024]{1,0:T(8,128)S(1)}, u32[]{:S(2)}, u32[]{:S(2)}) collective-permute-start(f32[32,1024]{1,0:T(8,128)S(1)} %constant_dynamic-slice_fusion), channel_id=1, source_target_pairs={{0,2},{2,0},{4,6},{6,4},{8,10},{10,8},{12,14},{14,12},{16,18},{18,... | collective-permute-start | bytes 393224 | tf_op jit(solution)/shard_map/ppermute | solution.py:594

commit v5 on v2

--- a/solution.py
+++ b/solution.py
@@ -636,14 +636,15 @@
         ]
         return lax.ppermute(value, ("ctx", "head"), turns)
 
-    def head_share(value, ctx=range(ranks)):
+    def head_share(value, ctx=range(ranks), after=()):
         def rows_of(which):
             return lax.dynamic_slice_in_dim(value, which * share, share, axis=0)
 
         total = rows_of(head).astype(full)
         for turn in range(1, head_count):
             target = lax.rem(head + turn, head_count)
-            total = total + turned(rows_of(target), turn, ctx).astype(full)
+            received, *_ = lax.optimization_barrier((turned(rows_of(target), turn, ctx), *after))
+            total = total + received.astype(full)
         return total
 
     from_x = permute(send, "ctx", lambda s: s ^ 2)
@@ -652,12 +653,18 @@
     from_other = across(to_other)
     far_sum = head_share((to_far.astype(full) + from_swap.astype(full)).astype(low)).astype(low)
     old_sum = (to_old.astype(full) + from_old.astype(full)).astype(low)
-    old_sum = head_share(old_sum, range(0, ranks, 2)).astype(low)
+    old_sum = head_share(old_sum, range(0, ranks, 2), (far_sum,)).astype(low)
     from_far = permute(far_sum, "ctx", lambda s: s - 2)
     from_mixed = permute(old_sum, "ctx", lambda s: -1 if s % 2 else s - 3)
     own_sum = (mine.astype(full) + from_other.astype(full)).astype(low)
     own_sum, *_ = lax.optimization_barrier((own_sum, far_sum))
-    total = head_share(own_sum)
+    if head_count == 2:
+        kept_half = lax.dynamic_slice_in_dim(own_sum, head * share, share, axis=0)
+        sent_half = lax.dynamic_slice_in_dim(own_sum, (1 - head) * share, share, axis=0)
+        received_half = turned(sent_half, 1)
+        total = kept_half.astype(full)
+    else:
+        total = head_share(own_sum)
 
     from_x, *_ = lax.optimization_barrier((from_x, far_sum, old_sum))
     plane = (keep.astype(full) + from_x.astype(full)).astype(low)
@@ -678,6 +685,11 @@
 
     total = (total + from_mixed.astype(full) + from_far.astype(full)).astype(low)
     shares = [total] + [turned(total, turn) for turn in range(1, head_count)]
+    if head_count == 2:
+        shares = [
+            (whole.astype(full) + part.astype(full)).astype(low)
+            for whole, part in zip(shares, (received_half, sent_half))
+        ]
     ordered = []
     for place in range(head_count):
         picked = shares[0]

time: 123 us -> 122 us (level)
    ppermute x4, waiting for transfers between devices: 18.8 us -> 6.72 us  [turned(): return lax.ppermute(value, ('ctx', 'head'), turns)]
    all_to_all x1, waiting for transfers between devices: 0.01 us -> 10.7 us  [local(): lax.all_to_all(plane, 'ctx', 0, 0, axis_index_groups=columns, tiled=True)]
where the time goes in v5:
time: 122 us; the launch traced here: 121 us
  starting transfers between devices  53.7 us (44%)
  Pallas kernels  37 us (30%)
  waiting for transfers between devices  19.3 us (16%)
  other arithmetic  7.07 us (6%)
  local copies, waits for them, and re-layouts  3.33 us (3%)
    ppermute x15, starting transfers between devices, permute(): return lax.ppermute(value, axis, pairs)  29.9 us
    pallas_call x1, Pallas kernels, attention(): call(functools.partial(main_kernel, ranks), steps, 2 * steps * heads * ro...  23.7 us
    all_to_all x1, starting transfers between devices, local(): lax.all_to_all(plane, 'ctx', 0, 0, axis_index_groups=columns, tiled=True)  17.6 us
    pallas_call x1, Pallas kernels, local_scores(): call(local_kernel, steps, 2 * steps * heads * rows * rows * (3 * (QK + VD...  13.3 us
    all_to_all x1, waiting for transfers between devices, local(): lax.all_to_all(plane, 'ctx', 0, 0, axis_index_groups=columns, tiled=True)  10.7 us
    ppermute x4, waiting for transfers between devices, turned(): return lax.ppermute(value, ('ctx', 'head'), turns)  6.72 us
    ppermute x4, starting transfers between devices, turned(): return lax.ppermute(value, ('ctx', 'head'), turns)  6.16 us
  transfers between devices with their start and end apart: 20, of which 5 were waited for; matrix products, arithmetic and copies ran while one was open for 5% of the time, Pallas kernels for 11%

profile of v5, /device:TPU:0, one launch (start us, length us, event | category | flops | bytes accessed | tf_op | source)
XLA Modules:
  0.0 121.4 jit_solution(14717310155957275728)
XLA Ops:
  0.6 0.0 copy-start.4
  0.6 0.0 copy-start.6
  0.7 1.3 %constant_dynamic-slice_fusion.5 = bf16[512,768]{1,0:T(8,128)(2,1)S(1)} fusion(bf16[512,1536]{1,0:T(8,128)(2,1)} %q0.3, s32[]{:T(128)S(6)} %select_n.63), kind=kLoop, calls=%fused_computation.24 | loop fusion | bytes 1572868 | tf_op jit(solution)/shard_map/dynamic_slice | solution.py:601
  2.0 0.5 collective-permute-start
  2.5 0.1 collective-permute-start.2
  2.6 0.5 collective-permute-start.1
  3.1 4.5 %collective-permute-start.3 = (bf16[576,512]{1,0:T(8,128)(2,1)S(1)}, bf16[576,512]{1,0:T(8,128)(2,1)S(1)}, u32[]{:S(2)}, u32[]{:S(2)}) collective-permute-start(bf16[576,512]{1,0:T(8,128)(2,1)S(1)} %bitcast.9), channel_id=1, source_target_pairs={{0,4},{2,6},{4,8},{6,10},{8,12},{10,14},{12,16},{14,18},{16,20},{1... | collective-permute-start | bytes 1769480 | tf_op jit(solution)/shard_map/ppermute | solution.py:586
  7.6 0.7 collective-permute-start.4
  8.3 0.0 collective-permute-done.1.do1
  8.4 0.0 copy-start.5
  8.4 0.8 copy-done.11
  9.1 0.2 copy-done.5
  9.4 13.3 %local_scores.1 = (bf16[2,6,512,512]{3,2,1,0:T(8,128)(2,1)}, bf16[2,6,512,512]{3,2,1,0:T(8,128)(2,1)}, bf16[2,4,512,192]{3,2,1,0:T(8,128)(2,1)}, f32[2,4,8,512]{...) custom-call(s32[1]{0:T(128)} %bitcast.index_ref, s32[1,8192]{1,0:T(1,128)} %bitcast.11, ...), custom_call_target="tpu_custom_call" | custom-call | flops 3087007744 | bytes 16777216 | tf_op jit(solution)/shard_map/local_scores/pallas_call | solution.py:505
  22.7 0.0 copy-start.7
  22.8 2.9 %collective-permute-start.5 = (bf16[576,512]{1,0:T(8,128)(2,1)S(1)}, bf16[576,512]{1,0:T(8,128)(2,1)S(1)}, u32[]{:S(2)}, u32[]{:S(2)}) collective-permute-start(bf16[576,512]{1,0:T(8,128)(2,1)S(1)} %collective-permute-done.3.lat_far), channel_id=1, source_target_pairs={{0,2},{2,0},{4,6},{6,4},{8,10},{10,8},{12,14},{14,12},{16,18},{18,... | collective-permute-start | bytes 1769480 | tf_op jit(solution)/shard_map/ppermute | solution.py:586
  25.7 2.0 %collective-permute-start.6 = (bf16[576,512]{1,0:T(8,128)(2,1)S(1)}, bf16[576,512]{1,0:T(8,128)(2,1)S(1)}, u32[]{:S(2)}, u32[]{:S(2)}) collective-permute-start(bf16[576,512]{1,0:T(8,128)(2,1)S(1)} %collective-permute-done.4.lat_mixed), channel_id=1, source_target_pairs={{0,2},{4,6},{8,10},{12,14},{16,18},{20,22},{24,26},{28,30},{1,3},{... | collective-permute-start | bytes 1769480 | tf_op jit(solution)/shard_map/ppermute | solution.py:586
  27.7 1.6 %collective-permute-done.6.lat_passed = bf16[576,512]{1,0:T(8,128)(2,1)S(1)} collective-permute-done((bf16[576,512]{1,0:T(8,128)(2,1)S(1)}, bf16[576,512]{1,0:T(8,128)(2,1)S(1)}, u32[]{:S(2)}, u32[]{:S(2)}) %collective-permute-start.6) | collective-permute-done | bytes 589856 | tf_op jit(solution)/shard_map/ppermute | solution.py:586
  29.2 0.8 copy-done.10
  30.0 23.7 %attention.1 = (bf16[512,768]{1,0:T(8,128)(2,1)}, bf16[512,768]{1,0:T(8,128)(2,1)}, bf16[256,1024]{1,0:T(8,128)(2,1)}, bf16[256,1024]{1,0:T(8,128)(2,1)}, bf16[5...) custom-call(s32[1]{0:T(128)} %bitcast.index_ref, ...), custom_call_target="tpu_custom_call" | custom-call | flops 18924699648 | bytes 16777216 | tf_op jit(solution)/shard_map/attention/pallas_call | solution.py:540
  53.7 0.5 collective-permute-start.9
  54.2 1.3 %collective-permute-start.11 = (bf16[576,512]{1,0:T(8,128)(2,1)}, bf16[576,512]{1,0:T(8,128)(2,1)S(1)}, u32[]{:S(2)}, u32[]{:S(2)}) collective-permute-start(bf16[576,512]{1,0:T(8,128)(2,1)} %get-tuple-element.40), channel_id=1, source_target_pairs={{2,0},{6,4},{10,8},{14,12},{18,16},{22,20},{26,24},{30,28},{3,1},{... | collective-permute-start | bytes 1769480 | tf_op jit(solution)/shard_map/ppermute | solution.py:586
  55.6 13.2 %collective-permute-start.17 = (bf16[256,1024]{1,0:T(8,128)(2,1)}, bf16[256,1024]{1,0:T(8,128)(2,1)S(1)}, u32[]{:S(2)}, u32[]{:S(2)}) collective-permute-start(bf16[256,1024]{1,0:T(8,128)(2,1)} %get-tuple-element.43), channel_id=1, source_target_pairs={{0,4},{2,6},{4,0},{6,2},{8,12},{10,14},{12,8},{14,10},{16,20},{18,... | collective-permute-start | bytes 1572872 | tf_op jit(solution)/shard_map/ppermute | solution.py:586
  68.8 0.9 collective-permute-start.8
  69.7 1.2 %add_convert_fusion.1 = bf16[576,512]{1,0:T(8,128)(2,1)S(1)} fusion(bf16[576,512]{1,0:T(8,128)(2,1)S(1)} %collective-permute-done.9, bf16[576,512]{1,0:T(8,128)(2,1)} %get-tuple-element.37), kind=kLoop, calls=%fused_computation.2 | loop fusion | flops 1179648 | bytes 1769472 | tf_op jit(solution)/shard_map/convert_element_type | solution.py:654
  71.0 1.6 %collective-permute-start.10 = (bf16[288,512]{1,0:T(8,128)(2,1)S(1)}, bf16[288,512]{1,0:T(8,128)(2,1)S(1)}, u32[]{:S(2)}, u32[]{:S(2)}) collective-permute-start(bf16[288,512]{1,0:T(8,128)(2,1)S(1)} %constant_dynamic-slice_fusion.3), channel_id=1, source_target_pairs={{0,1},{1,0},{2,3},{3,2},{4,5},{5,4},{6,7},{7,6},{8,9},{9,8},{10,11... | collective-permute-start | bytes 884744 | tf_op jit(solution)/shard_map/ppermute | solution.py:637
  72.5 0.2 add_convert_fusion
  72.7 2.4 %collective-permute-start.12 = (bf16[288,512]{1,0:T(8,128)(2,1)S(1)}, bf16[288,512]{1,0:T(8,128)(2,1)S(1)}, u32[]{:S(2)}, u32[]{:S(2)}) collective-permute-start(bf16[288,512]{1,0:T(8,128)(2,1)S(1)} %constant_dynamic-slice_fusion.2), channel_id=1, source_target_pairs={{0,1},{1,0},{4,5},{5,4},{8,9},{9,8},{12,13},{13,12},{16,17},{17,16... | collective-permute-start | bytes 884744 | tf_op jit(solution)/shard_map/ppermute | solution.py:637
  75.2 0.2 add_convert_fusion.2
  75.4 5.1 %collective-permute-done.10 = bf16[288,512]{1,0:T(8,128)(2,1)S(1)} collective-permute-done((bf16[288,512]{1,0:T(8,128)(2,1)S(1)}, bf16[288,512]{1,0:T(8,128)(2,1)S(1)}, u32[]{:S(2)}, u32[]{:S(2)}) %collective-permute-start.10) | collective-permute-done | bytes 294944 | tf_op jit(solution)/shard_map/ppermute | solution.py:637
  80.4 0.1 add_convert_fusion.8
  80.5 1.4 %collective-permute-start.14 = (bf16[288,512]{1,0:T(8,128)(2,1)S(1)}, bf16[288,512]{1,0:T(8,128)(2,1)}, u32[]{:S(2)}, u32[]{:S(2)}) collective-permute-start(bf16[288,512]{1,0:T(8,128)(2,1)S(1)} %add_convert_fusion.8), channel_id=1, source_target_pairs={{4,0},{6,2},{8,4},{10,6},{12,8},{14,10},{16,12},{18,14},{20,16},{2... | collective-permute-start | bytes 884744 | tf_op jit(solution)/shard_map/ppermute | solution.py:586
  82.0 1.6 %collective-permute-done.12 = bf16[288,512]{1,0:T(8,128)(2,1)S(1)} collective-permute-done((bf16[288,512]{1,0:T(8,128)(2,1)S(1)}, bf16[288,512]{1,0:T(8,128)(2,1)S(1)}, u32[]{:S(2)}, u32[]{:S(2)}) %collective-permute-start.12) | collective-permute-done | bytes 294944 | tf_op jit(solution)/shard_map/ppermute | solution.py:637
  83.6 0.1 add_convert_fusion.7
  83.7 1.4 %collective-permute-start.13 = (bf16[288,512]{1,0:T(8,128)(2,1)S(1)}, bf16[288,512]{1,0:T(8,128)(2,1)}, u32[]{:S(2)}, u32[]{:S(2)}) collective-permute-start(bf16[288,512]{1,0:T(8,128)(2,1)S(1)} %add_convert_fusion.7), channel_id=1, source_target_pairs={{8,2},{12,6},{16,10},{20,14},{24,18},{28,22},{9,3},{13,7},{17,11},... | collective-permute-start | bytes 884744 | tf_op jit(solution)/shard_map/ppermute | solution.py:586
  85.1 1.0 add_convert_fusion.3
  86.1 17.6 %all-to-all-start = ((bf16[4,64,1024]{2,1,0:T(8,128)(2,1)}), bf16[4,64,1024]{2,1,0:T(8,128)(2,1)S(1)}, u32[]{:S(2)}, u32[]{:S(2)}) async-start(bf16[4,64,1024]{2,1,0:T(8,128)(2,1)} %bitcast.4), calls=%async_computation | async-start | bytes 1048576 | tf_op jit(solution)/shard_map/all_to_all | solution.py:672
  103.7 0.1 broadcast_select_fusion.1
  103.8 1.6 %collective-permute-start.16 = (bf16[288,512]{1,0:T(8,128)(2,1)S(1)}, bf16[288,512]{1,0:T(8,128)(2,1)S(1)}, u32[]{:S(2)}, u32[]{:S(2)}) collective-permute-start(bf16[288,512]{1,0:T(8,128)(2,1)S(1)} %constant_dynamic-slice_fusion.1), channel_id=1, source_target_pairs={{0,1},{1,0},{2,3},{3,2},{4,5},{5,4},{6,7},{7,6},{8,9},{9,8},{10,11... | collective-permute-start | bytes 884744 | tf_op jit(solution)/shard_map/ppermute | solution.py:637
  105.4 1.2 add_convert_fusion.6
  106.6 0.6 collective-permute-start.15
  107.2 1.3 %pad_maximum_fusion = bf16[512,1536]{1,0:T(8,128)(2,1)} fusion(bf16[512,768]{1,0:T(8,128)(2,1)S(1)} %get-tuple-element.46, bf16[512,768]{1,0:T(8,128)(2,1)S(1)} %get-tuple-element.45), kind=kLoop, calls=%fused_computation | loop fusion | flops 3145728 | bytes 3145728 | tf_op jit(solution)/shard_map/concatenate | solution.py:679
  108.4 10.7 %all-to-all-done = bf16[4,64,1024]{2,1,0:T(8,128)(2,1)S(1)} async-done(((bf16[4,64,1024]{2,1,0:T(8,128)(2,1)}), bf16[4,64,1024]{2,1,0:T(8,128)(2,1)S(1)}, u32[]{:S(2)}, u32[]{:S(2)}) %all-to-all-start) | async-done | bytes 524320 | tf_op jit(solution)/shard_map/all_to_all | solution.py:672
  119.1 0.1 convert_reduce_fusion
  119.3 0.1 collective-permute-start.18
  119.4 0.2 broadcast_select_fusion.3
  119.5 0.9 maximum_bitcast_fusion
  120.4 0.3 collective-permute-done.18
  120.7 0.7 pad_maximum_fusion.1
  (38 shorter events, 0.2 us)
Async XLA Ops:
  0.6 1.9 %copy-start.4 = (bf16[512,1024]{1,0:T(8,128)(2,1)S(1)}, bf16[512,1024]{1,0:T(8,128)(2,1)}, u32[]{:S(2)}) copy-start(bf16[512,1024]{1,0:T(8,128)(2,1)} %do0.3) | copy-start | bytes 3145732
  0.6 2.5 %copy-start.6 = (bf16[512,576]{0,1:T(8,128)(2,1)S(1)}, bf16[512,576]{0,1:T(8,128)(2,1)}, u32[]{:S(2)}) copy-start(bf16[512,576]{0,1:T(8,128)(2,1)} %param.5) | copy-start | bytes 1769476
  2.0 6.4 %collective-permute-start = (bf16[512,768]{1,0:T(8,128)(2,1)S(1)}, bf16[512,768]{1,0:T(8,128)(2,1)S(1)}, u32[]{:S(2)}, u32[]{:S(2)}) collective-permute-start(bf16[512,768]{1,0:T(8,128)(2,1)S(1)} %constant_dynamic-slice_fusion.5), channel_id=1, source_target_pairs={{0,2},{2,0},{4,6},{6,4},{8,10},{10,8},{12,14},{14,12},{16,18},{18,... | collective-permute-start | bytes 2359304 | tf_op jit(solution)/shard_map/ppermute | solution.py:586
  2.5 5.9 %collective-permute-start.2 = (bf16[576,512]{1,0:T(8,128)(2,1)}, bf16[576,512]{1,0:T(8,128)(2,1)}, u32[]{:S(2)}, u32[]{:S(2)}) collective-permute-start(bf16[576,512]{1,0:T(8,128)(2,1)} %bitcast.6), channel_id=1, source_target_pairs={{0,2},{2,0},{4,6},{6,4},{8,10},{10,8},{12,14},{14,12},{16,18},{18,... | collective-permute-start | bytes 1769480 | tf_op jit(solution)/shard_map/ppermute | solution.py:586
  2.6 5.7 %collective-permute-start.1 = (bf16[512,512]{1,0:T(8,128)(2,1)S(1)}, bf16[512,512]{1,0:T(8,128)(2,1)S(1)}, u32[]{:S(2)}, u32[]{:S(2)}) collective-permute-start(bf16[512,512]{1,0:T(8,128)(2,1)S(1)} %constant_dynamic-slice_fusion.4), channel_id=1, source_target_pairs={{0,2},{2,0},{4,6},{6,4},{8,10},{10,8},{12,14},{14,12},{16,18},{18,... | collective-permute-start | bytes 1572872 | tf_op jit(solution)/shard_map/ppermute | solution.py:586
  3.1 19.6 %collective-permute-start.3 = (bf16[576,512]{1,0:T(8,128)(2,1)S(1)}, bf16[576,512]{1,0:T(8,128)(2,1)S(1)}, u32[]{:S(2)}, u32[]{:S(2)}) collective-permute-start(bf16[576,512]{1,0:T(8,128)(2,1)S(1)} %bitcast.9), channel_id=1, source_target_pairs={{0,4},{2,6},{4,8},{6,10},{8,12},{10,14},{12,16},{14,18},{16,20},{1... | collective-permute-start | bytes 1769480 | tf_op jit(solution)/shard_map/ppermute | solution.py:586
  7.6 15.1 %collective-permute-start.4 = (bf16[576,512]{1,0:T(8,128)(2,1)S(1)}, bf16[576,512]{1,0:T(8,128)(2,1)S(1)}, u32[]{:S(2)}, u32[]{:S(2)}) collective-permute-start(bf16[576,512]{1,0:T(8,128)(2,1)S(1)} %bitcast.10), channel_id=1, source_target_pairs={{2,8},{6,12},{10,16},{14,20},{18,24},{22,28},{3,9},{7,13},{11,17},... | collective-permute-start | bytes 1769480 | tf_op jit(solution)/shard_map/ppermute | solution.py:586
  8.3 0.8 copy-start.11
  8.4 1.0 copy-start.5
  22.7 6.5 %copy-start.7 = (bf16[576,512]{1,0:T(8,128)(2,1)}, bf16[576,512]{1,0:T(8,128)(2,1)S(1)}, u32[]{:S(2)}) copy-start(bf16[576,512]{1,0:T(8,128)(2,1)S(1)} %collective-permute-done.3.lat_far) | copy-start | bytes 1769476
  22.8 6.5 %copy-start.8 = (bf16[576,512]{1,0:T(8,128)(2,1)}, bf16[576,512]{1,0:T(8,128)(2,1)S(1)}, u32[]{:S(2)}) copy-start(bf16[576,512]{1,0:T(8,128)(2,1)S(1)} %collective-permute-done.4.lat_mixed) | copy-start | bytes 1769476
  22.8 4.9 %collective-permute-start.5 = (bf16[576,512]{1,0:T(8,128)(2,1)S(1)}, bf16[576,512]{1,0:T(8,128)(2,1)S(1)}, u32[]{:S(2)}, u32[]{:S(2)}) collective-permute-start(bf16[576,512]{1,0:T(8,128)(2,1)S(1)} %collective-permute-done.3.lat_far), channel_id=1, source_target_pairs={{0,2},{2,0},{4,6},{6,4},{8,10},{10,8},{12,14},{14,12},{16,18},{18,... | collective-permute-start | bytes 1769480 | tf_op jit(solution)/shard_map/ppermute | solution.py:586
  25.7 3.5 %collective-permute-start.6 = (bf16[576,512]{1,0:T(8,128)(2,1)S(1)}, bf16[576,512]{1,0:T(8,128)(2,1)S(1)}, u32[]{:S(2)}, u32[]{:S(2)}) collective-permute-start(bf16[576,512]{1,0:T(8,128)(2,1)S(1)} %collective-permute-done.4.lat_mixed), channel_id=1, source_target_pairs={{0,2},{4,6},{8,10},{12,14},{16,18},{20,22},{24,26},{28,30},{1,3},{... | collective-permute-start | bytes 1769480 | tf_op jit(solution)/shard_map/ppermute | solution.py:586
  27.6 1.6 %copy-start.9 = (bf16[576,512]{1,0:T(8,128)(2,1)}, bf16[576,512]{1,0:T(8,128)(2,1)S(1)}, u32[]{:S(2)}) copy-start(bf16[576,512]{1,0:T(8,128)(2,1)S(1)} %collective-permute-done.5.lat_swap) | copy-start | bytes 1769476
  29.2 0.8 copy-start.10
  53.7 18.8 %copy-start.2 = (bf16[576,512]{1,0:T(8,128)(2,1)S(1)}, bf16[576,512]{1,0:T(8,128)(2,1)}, u32[]{:S(2)}) copy-start(bf16[576,512]{1,0:T(8,128)(2,1)} %get-tuple-element.40) | copy-start | bytes 1769476
  53.7 15.9 %collective-permute-start.9 = (bf16[576,512]{1,0:T(8,128)(2,1)}, bf16[576,512]{1,0:T(8,128)(2,1)S(1)}, u32[]{:S(2)}, u32[]{:S(2)}) collective-permute-start(bf16[576,512]{1,0:T(8,128)(2,1)} %get-tuple-element.38), channel_id=1, source_target_pairs={{0,2},{2,0},{4,6},{6,4},{8,10},{10,8},{12,14},{14,12},{16,18},{18,... | collective-permute-start | bytes 1769480 | tf_op jit(solution)/shard_map/ppermute | solution.py:586
  54.2 18.3 %collective-permute-start.11 = (bf16[576,512]{1,0:T(8,128)(2,1)}, bf16[576,512]{1,0:T(8,128)(2,1)S(1)}, u32[]{:S(2)}, u32[]{:S(2)}) collective-permute-start(bf16[576,512]{1,0:T(8,128)(2,1)} %get-tuple-element.40), channel_id=1, source_target_pairs={{2,0},{6,4},{10,8},{14,12},{18,16},{22,20},{26,24},{30,28},{3,1},{... | collective-permute-start | bytes 1769480 | tf_op jit(solution)/shard_map/ppermute | solution.py:586
  55.6 29.5 %collective-permute-start.17 = (bf16[256,1024]{1,0:T(8,128)(2,1)}, bf16[256,1024]{1,0:T(8,128)(2,1)S(1)}, u32[]{:S(2)}, u32[]{:S(2)}) collective-permute-start(bf16[256,1024]{1,0:T(8,128)(2,1)} %get-tuple-element.43), channel_id=1, source_target_pairs={{0,4},{2,6},{4,0},{6,2},{8,12},{10,14},{12,8},{14,10},{16,20},{18,... | collective-permute-start | bytes 1572872 | tf_op jit(solution)/shard_map/ppermute | solution.py:586
  68.8 6.4 %collective-permute-start.8 = (bf16[576,512]{1,0:T(8,128)(2,1)}, bf16[576,512]{1,0:T(8,128)(2,1)S(1)}, u32[]{:S(2)}, u32[]{:S(2)}) collective-permute-start(bf16[576,512]{1,0:T(8,128)(2,1)} %get-tuple-element.36), channel_id=1, source_target_pairs={{0,2},{2,0},{4,6},{6,4},{8,10},{10,8},{12,14},{14,12},{16,18},{18,... | collective-permute-start | bytes 1769480 | tf_op jit(solution)/shard_map/ppermute | solution.py:586
  69.7 34.0 %collective-permute-start.7 = (bf16[512,768]{1,0:T(8,128)(2,1)}, bf16[512,768]{1,0:T(8,128)(2,1)S(1)}, u32[]{:S(2)}, u32[]{:S(2)}) collective-permute-start(bf16[512,768]{1,0:T(8,128)(2,1)} %get-tuple-element.34), channel_id=1, source_target_pairs={{0,2},{2,0},{4,6},{6,4},{8,10},{10,8},{12,14},{14,12},{16,18},{18,... | collective-permute-start | bytes 2359304 | tf_op jit(solution)/shard_map/ppermute | solution.py:586
  70.9 4.3 %copy-start.1 = (bf16[576,512]{1,0:T(8,128)(2,1)S(1)}, bf16[576,512]{1,0:T(8,128)(2,1)}, u32[]{:S(2)}) copy-start(bf16[576,512]{1,0:T(8,128)(2,1)} %get-tuple-element.35) | copy-start | bytes 1769476
  71.0 9.5 %collective-permute-start.10 = (bf16[288,512]{1,0:T(8,128)(2,1)S(1)}, bf16[288,512]{1,0:T(8,128)(2,1)S(1)}, u32[]{:S(2)}, u32[]{:S(2)}) collective-permute-start(bf16[288,512]{1,0:T(8,128)(2,1)S(1)} %constant_dynamic-slice_fusion.3), channel_id=1, source_target_pairs={{0,1},{1,0},{2,3},{3,2},{4,5},{5,4},{6,7},{7,6},{8,9},{9,8},{10,11... | collective-permute-start | bytes 884744 | tf_op jit(solution)/shard_map/ppermute | solution.py:637
  72.7 10.9 %collective-permute-start.12 = (bf16[288,512]{1,0:T(8,128)(2,1)S(1)}, bf16[288,512]{1,0:T(8,128)(2,1)S(1)}, u32[]{:S(2)}, u32[]{:S(2)}) collective-permute-start(bf16[288,512]{1,0:T(8,128)(2,1)S(1)} %constant_dynamic-slice_fusion.2), channel_id=1, source_target_pairs={{0,1},{1,0},{4,5},{5,4},{8,9},{9,8},{12,13},{13,12},{16,17},{17,16... | collective-permute-start | bytes 884744 | tf_op jit(solution)/shard_map/ppermute | solution.py:637
  75.2 9.9 %copy-start.3 = (bf16[256,1024]{1,0:T(8,128)(2,1)S(1)}, bf16[256,1024]{1,0:T(8,128)(2,1)}, u32[]{:S(2)}) copy-start(bf16[256,1024]{1,0:T(8,128)(2,1)} %get-tuple-element.42) | copy-start | bytes 1572868
  80.5 23.2 %copy-start = (bf16[512,768]{1,0:T(8,128)(2,1)S(1)}, bf16[512,768]{1,0:T(8,128)(2,1)}, u32[]{:S(2)}) copy-start(bf16[512,768]{1,0:T(8,128)(2,1)} %get-tuple-element.33) | copy-start | bytes 2359300
  80.5 24.9 %collective-permute-start.14 = (bf16[288,512]{1,0:T(8,128)(2,1)S(1)}, bf16[288,512]{1,0:T(8,128)(2,1)}, u32[]{:S(2)}, u32[]{:S(2)}) collective-permute-start(bf16[288,512]{1,0:T(8,128)(2,1)S(1)} %add_convert_fusion.8), channel_id=1, source_target_pairs={{4,0},{6,2},{8,4},{10,6},{12,8},{14,10},{16,12},{18,14},{20,16},{2... | collective-permute-start | bytes 884744 | tf_op jit(solution)/shard_map/ppermute | solution.py:586
  83.7 21.7 %collective-permute-start.13 = (bf16[288,512]{1,0:T(8,128)(2,1)S(1)}, bf16[288,512]{1,0:T(8,128)(2,1)}, u32[]{:S(2)}, u32[]{:S(2)}) collective-permute-start(bf16[288,512]{1,0:T(8,128)(2,1)S(1)} %add_convert_fusion.7), channel_id=1, source_target_pairs={{8,2},{12,6},{16,10},{20,14},{24,18},{28,22},{9,3},{13,7},{17,11},... | collective-permute-start | bytes 884744 | tf_op jit(solution)/shard_map/ppermute | solution.py:586
  86.1 33.1 %all-to-all-start = ((bf16[4,64,1024]{2,1,0:T(8,128)(2,1)}), bf16[4,64,1024]{2,1,0:T(8,128)(2,1)S(1)}, u32[]{:S(2)}, u32[]{:S(2)}) async-start(bf16[4,64,1024]{2,1,0:T(8,128)(2,1)} %bitcast.4), calls=%async_computation | async-start | bytes 1048576 | tf_op jit(solution)/shard_map/all_to_all | solution.py:672
  103.8 15.5 %collective-permute-start.16 = (bf16[288,512]{1,0:T(8,128)(2,1)S(1)}, bf16[288,512]{1,0:T(8,128)(2,1)S(1)}, u32[]{:S(2)}, u32[]{:S(2)}) collective-permute-start(bf16[288,512]{1,0:T(8,128)(2,1)S(1)} %constant_dynamic-slice_fusion.1), channel_id=1, source_target_pairs={{0,1},{1,0},{2,3},{3,2},{4,5},{5,4},{6,7},{7,6},{8,9},{9,8},{10,11... | collective-permute-start | bytes 884744 | tf_op jit(solution)/shard_map/ppermute | solution.py:637
  106.6 12.7 %collective-permute-start.15 = (bf16[288,512]{1,0:T(8,128)(2,1)S(1)}, bf16[288,512]{1,0:T(8,128)(2,1)S(1)}, u32[]{:S(2)}, u32[]{:S(2)}) collective-permute-start(bf16[288,512]{1,0:T(8,128)(2,1)S(1)} %add_convert_fusion.6), channel_id=1, source_target_pairs={{0,1},{1,0},{2,3},{3,2},{4,5},{5,4},{6,7},{7,6},{8,9},{9,8},{10,11... | collective-permute-start | bytes 884744 | tf_op jit(solution)/shard_map/ppermute | solution.py:637
  119.3 1.4 %collective-permute-start.18 = (f32[32,1024]{1,0:T(8,128)S(1)}, f32[32,1024]{1,0:T(8,128)S(1)}, u32[]{:S(2)}, u32[]{:S(2)}) collective-permute-start(f32[32,1024]{1,0:T(8,128)S(1)} %constant_dynamic-slice_fusion), channel_id=1, source_target_pairs={{0,2},{2,0},{4,6},{6,4},{8,10},{10,8},{12,14},{14,12},{16,18},{18,... | collective-permute-start | bytes 393224 | tf_op jit(solution)/shard_map/ppermute | solution.py:586

commit v6 on v5

--- a/solution.py
+++ b/solution.py
@@ -666,7 +666,7 @@
     else:
         total = head_share(own_sum)
 
-    from_x, *_ = lax.optimization_barrier((from_x, far_sum, old_sum))
+    from_x, *_ = lax.optimization_barrier((from_x, far_sum))
     plane = (keep.astype(full) + from_x.astype(full)).astype(low)
     columns = [list(range(first, ranks, 4)) for first in range(4)]
     pieces = lax.all_to_all(plane, "ctx", 0, 0, axis_index_groups=columns, tiled=True)

time: 122 us -> 125 us (1.025)
  the two profiles are of different devices: /device:TPU:0 before, /device:TPU:9 now
where the time goes in v6:
time: 125 us; the launch traced here: 123 us
  Pallas kernels  55.8 us (45%)
  starting transfers between devices  28.9 us (23%)
  waiting for transfers between devices  25.1 us (20%)
  other arithmetic  8.63 us (7%)
  local copies, waits for them, and re-layouts  4.04 us (3%)
    pallas_call x1, Pallas kernels, attention(): call(functools.partial(main_kernel, ranks), steps, 2 * steps * heads * ro...  42.5 us
    ppermute x15, waiting for transfers between devices, permute(): return lax.ppermute(value, axis, pairs)  17.4 us
    ppermute x15, starting transfers between devices, permute(): return lax.ppermute(value, axis, pairs)  15.7 us
    pallas_call x1, Pallas kernels, local_scores(): call(local_kernel, steps, 2 * steps * heads * rows * rows * (3 * (QK + VD...  13.3 us
    all_to_all x1, starting transfers between devices, local(): lax.all_to_all(plane, 'ctx', 0, 0, axis_index_groups=columns, tiled=True)  7.88 us
    ppermute x4, waiting for transfers between devices, turned(): return lax.ppermute(value, ('ctx', 'head'), turns)  7.72 us
    ppermute x4, starting transfers between devices, turned(): return lax.ppermute(value, ('ctx', 'head'), turns)  5.32 us
  transfers between devices with their start and end apart: 20, of which 6 were waited for; matrix products, arithmetic and copies ran while one was open for 7% of the time, Pallas kernels for 11%

profile of v6, /device:TPU:9, one launch (start us, length us, event | category | flops | bytes accessed | tf_op | source)
XLA Modules:
  0.0 123.5 jit_solution(15569714734600538745)
XLA Ops:
  0.6 0.0 copy-start.6
  0.7 1.3 %constant_dynamic-slice_fusion.5 = bf16[512,768]{1,0:T(8,128)(2,1)S(1)} fusion(bf16[512,1536]{1,0:T(8,128)(2,1)} %q0.3, s32[]{:T(128)S(6)} %select_n.63), kind=kLoop, calls=%fused_computation.24 | loop fusion | bytes 1572868 | tf_op jit(solution)/shard_map/dynamic_slice | solution.py:601
  2.0 0.7 collective-permute-start
  2.7 0.1 collective-permute-start.2
  2.8 0.5 collective-permute-start.1
  3.3 3.1 %collective-permute-start.3 = (bf16[576,512]{1,0:T(8,128)(2,1)S(1)}, bf16[576,512]{1,0:T(8,128)(2,1)S(1)}, u32[]{:S(2)}, u32[]{:S(2)}) collective-permute-start(bf16[576,512]{1,0:T(8,128)(2,1)S(1)} %bitcast.9), channel_id=1, source_target_pairs={{0,4},{2,6},{4,8},{6,10},{8,12},{10,14},{12,16},{14,18},{16,20},{1... | collective-permute-start | bytes 1769480 | tf_op jit(solution)/shard_map/ppermute | solution.py:586
  6.5 3.5 %collective-permute-start.4 = (bf16[576,512]{1,0:T(8,128)(2,1)S(1)}, bf16[576,512]{1,0:T(8,128)(2,1)S(1)}, u32[]{:S(2)}, u32[]{:S(2)}) collective-permute-start(bf16[576,512]{1,0:T(8,128)(2,1)S(1)} %bitcast.10), channel_id=1, source_target_pairs={{2,8},{6,12},{10,16},{14,20},{18,24},{22,28},{3,9},{7,13},{11,17},... | collective-permute-start | bytes 1769480 | tf_op jit(solution)/shard_map/ppermute | solution.py:586
  10.0 0.0 copy-start.5
  10.0 0.8 copy-done.11
  10.8 0.2 copy-done.5
  11.0 13.3 %local_scores.1 = (bf16[2,6,512,512]{3,2,1,0:T(8,128)(2,1)}, bf16[2,6,512,512]{3,2,1,0:T(8,128)(2,1)}, bf16[2,4,512,192]{3,2,1,0:T(8,128)(2,1)}, f32[2,4,8,512]{...) custom-call(s32[1]{0:T(128)} %bitcast.index_ref, s32[1,8192]{1,0:T(1,128)} %bitcast.11, ...), custom_call_target="tpu_custom_call" | custom-call | flops 3087007744 | bytes 16777216 | tf_op jit(solution)/shard_map/local_scores/pallas_call | solution.py:505
  24.3 0.1 collective-permute-start.5
  24.4 1.3 %collective-permute-start.6 = (bf16[576,512]{1,0:T(8,128)(2,1)S(1)}, bf16[576,512]{1,0:T(8,128)(2,1)S(1)}, u32[]{:S(2)}, u32[]{:S(2)}) collective-permute-start(bf16[576,512]{1,0:T(8,128)(2,1)S(1)} %collective-permute-done.4.lat_mixed), channel_id=1, source_target_pairs={{0,2},{4,6},{8,10},{12,14},{16,18},{20,22},{24,26},{28,30},{1,3},{... | collective-permute-start | bytes 1769480 | tf_op jit(solution)/shard_map/ppermute | solution.py:586
  25.7 0.7 collective-permute-done.5.lat_swap
  26.4 1.9 %collective-permute-done.6.lat_passed = bf16[576,512]{1,0:T(8,128)(2,1)S(1)} collective-permute-done((bf16[576,512]{1,0:T(8,128)(2,1)S(1)}, bf16[576,512]{1,0:T(8,128)(2,1)S(1)}, u32[]{:S(2)}, u32[]{:S(2)}) %collective-permute-start.6) | collective-permute-done | bytes 589856 | tf_op jit(solution)/shard_map/ppermute | solution.py:586
  28.3 0.8 copy-done.10
  29.1 42.5 %attention.1 = (bf16[512,768]{1,0:T(8,128)(2,1)}, bf16[512,768]{1,0:T(8,128)(2,1)}, bf16[256,1024]{1,0:T(8,128)(2,1)}, bf16[256,1024]{1,0:T(8,128)(2,1)}, bf16[5...) custom-call(s32[1]{0:T(128)} %bitcast.index_ref, ...), custom_call_target="tpu_custom_call" | custom-call | flops 18924699648 | bytes 16777216 | tf_op jit(solution)/shard_map/attention/pallas_call | solution.py:540
  71.7 0.1 collective-permute-start.9
  71.7 2.4 %collective-permute-start.11 = (bf16[576,512]{1,0:T(8,128)(2,1)}, bf16[576,512]{1,0:T(8,128)(2,1)S(1)}, u32[]{:S(2)}, u32[]{:S(2)}) collective-permute-start(bf16[576,512]{1,0:T(8,128)(2,1)} %get-tuple-element.40), channel_id=1, source_target_pairs={{2,0},{6,4},{10,8},{14,12},{18,16},{22,20},{26,24},{30,28},{3,1},{... | collective-permute-start | bytes 1769480 | tf_op jit(solution)/shard_map/ppermute | solution.py:586
  74.2 0.1 collective-permute-start.17
  74.3 0.1 collective-permute-start.8
  74.3 0.5 collective-permute-start.7
  74.8 1.2 add_convert_fusion.1
  76.1 1.3 %collective-permute-start.10 = (bf16[288,512]{1,0:T(8,128)(2,1)S(1)}, bf16[288,512]{1,0:T(8,128)(2,1)S(1)}, u32[]{:S(2)}, u32[]{:S(2)}) collective-permute-start(bf16[288,512]{1,0:T(8,128)(2,1)S(1)} %constant_dynamic-slice_fusion.3), channel_id=1, source_target_pairs={{0,1},{1,0},{2,3},{3,2},{4,5},{5,4},{6,7},{7,6},{8,9},{9,8},{10,11... | collective-permute-start | bytes 884744 | tf_op jit(solution)/shard_map/ppermute | solution.py:637
  77.5 0.2 add_convert_fusion
  77.6 0.8 constant_dynamic-slice_fusion.2
  78.4 1.4 %collective-permute-start.12 = (bf16[288,512]{1,0:T(8,128)(2,1)}, bf16[288,512]{1,0:T(8,128)(2,1)}, u32[]{:S(2)}, u32[]{:S(2)}) collective-permute-start(bf16[288,512]{1,0:T(8,128)(2,1)} %constant_dynamic-slice_fusion.2), channel_id=1, source_target_pairs={{0,1},{1,0},{4,5},{5,4},{8,9},{9,8},{12,13},{13,12},{16,17},{17,16... | collective-permute-start | bytes 884744 | tf_op jit(solution)/shard_map/ppermute | solution.py:637
  79.8 0.2 add_convert_fusion.2
  79.9 4.8 %collective-permute-done.10 = bf16[288,512]{1,0:T(8,128)(2,1)S(1)} collective-permute-done((bf16[288,512]{1,0:T(8,128)(2,1)S(1)}, bf16[288,512]{1,0:T(8,128)(2,1)S(1)}, u32[]{:S(2)}, u32[]{:S(2)}) %collective-permute-start.10) | collective-permute-done | bytes 294944 | tf_op jit(solution)/shard_map/ppermute | solution.py:637
  84.8 0.8 add_convert_fusion.8
  85.6 1.9 %collective-permute-start.14 = (bf16[288,512]{1,0:T(8,128)(2,1)}, bf16[288,512]{1,0:T(8,128)(2,1)}, u32[]{:S(2)}, u32[]{:S(2)}) collective-permute-start(bf16[288,512]{1,0:T(8,128)(2,1)} %add_convert_fusion.8), channel_id=1, source_target_pairs={{4,0},{6,2},{8,4},{10,6},{12,8},{14,10},{16,12},{18,14},{20,16},{2... | collective-permute-start | bytes 884744 | tf_op jit(solution)/shard_map/ppermute | solution.py:586
  87.5 0.9 collective-permute-done.17
  88.3 1.0 add_convert_fusion.3
  89.3 7.9 %all-to-all-start = ((bf16[4,64,1024]{2,1,0:T(8,128)(2,1)}), bf16[4,64,1024]{2,1,0:T(8,128)(2,1)S(1)}, u32[]{:S(2)}, u32[]{:S(2)}) async-start(bf16[4,64,1024]{2,1,0:T(8,128)(2,1)} %bitcast.4), calls=%async_computation | async-start | bytes 1048576 | tf_op jit(solution)/shard_map/all_to_all | solution.py:672
  97.2 1.0 add_convert_fusion.7
  98.2 1.3 %collective-permute-start.13 = (bf16[288,512]{1,0:T(8,128)(2,1)S(1)}, bf16[288,512]{1,0:T(8,128)(2,1)S(1)}, u32[]{:S(2)}, u32[]{:S(2)}) collective-permute-start(bf16[288,512]{1,0:T(8,128)(2,1)S(1)} %add_convert_fusion.7), channel_id=1, source_target_pairs={{8,2},{12,6},{16,10},{20,14},{24,18},{28,22},{9,3},{13,7},{17,11},... | collective-permute-start | bytes 884744 | tf_op jit(solution)/shard_map/ppermute | solution.py:586
  99.6 0.1 broadcast_select_fusion.1
  99.7 1.3 %collective-permute-start.16 = (bf16[288,512]{1,0:T(8,128)(2,1)S(1)}, bf16[288,512]{1,0:T(8,128)(2,1)S(1)}, u32[]{:S(2)}, u32[]{:S(2)}) collective-permute-start(bf16[288,512]{1,0:T(8,128)(2,1)S(1)} %constant_dynamic-slice_fusion.1), channel_id=1, source_target_pairs={{0,1},{1,0},{2,3},{3,2},{4,5},{5,4},{6,7},{7,6},{8,9},{9,8},{10,11... | collective-permute-start | bytes 884744 | tf_op jit(solution)/shard_map/ppermute | solution.py:637
  101.0 13.9 %collective-permute-done.13 = bf16[288,512]{1,0:T(8,128)(2,1)S(1)} collective-permute-done((bf16[288,512]{1,0:T(8,128)(2,1)S(1)}, bf16[288,512]{1,0:T(8,128)(2,1)S(1)}, u32[]{:S(2)}, u32[]{:S(2)}) %collective-permute-start.13) | collective-permute-done | bytes 294944 | tf_op jit(solution)/shard_map/ppermute | solution.py:586
  115.0 1.1 add_convert_fusion.6
  116.0 1.3 %collective-permute-start.15 = (bf16[288,512]{1,0:T(8,128)(2,1)S(1)}, bf16[288,512]{1,0:T(8,128)(2,1)S(1)}, u32[]{:S(2)}, u32[]{:S(2)}) collective-permute-start(bf16[288,512]{1,0:T(8,128)(2,1)S(1)} %add_convert_fusion.6), channel_id=1, source_target_pairs={{0,1},{1,0},{2,3},{3,2},{4,5},{5,4},{6,7},{7,6},{8,9},{9,8},{10,11... | collective-permute-start | bytes 884744 | tf_op jit(solution)/shard_map/ppermute | solution.py:637
  117.3 1.3 %pad_maximum_fusion = bf16[512,1536]{1,0:T(8,128)(2,1)} fusion(bf16[512,768]{1,0:T(8,128)(2,1)S(1)} %get-tuple-element.46, bf16[512,768]{1,0:T(8,128)(2,1)S(1)} %get-tuple-element.45), kind=kLoop, calls=%fused_computation | loop fusion | flops 3145728 | bytes 3145728 | tf_op jit(solution)/shard_map/concatenate | solution.py:679
  118.6 0.1 convert_reduce_fusion
  118.7 0.1 collective-permute-start.18
  118.8 2.9 %collective-permute-done.15 = bf16[288,512]{1,0:T(8,128)(2,1)S(1)} collective-permute-done((bf16[288,512]{1,0:T(8,128)(2,1)S(1)}, bf16[288,512]{1,0:T(8,128)(2,1)S(1)}, u32[]{:S(2)}, u32[]{:S(2)}) %collective-permute-start.15) | collective-permute-done | bytes 294944 | tf_op jit(solution)/shard_map/ppermute | solution.py:637
  121.7 0.2 broadcast_select_fusion.3
  121.9 0.9 maximum_bitcast_fusion
  122.7 0.7 pad_maximum_fusion.1
  (38 shorter events, 0.2 us)
Async XLA Ops:
  0.6 2.2 %copy-start.4 = (bf16[512,1024]{1,0:T(8,128)(2,1)S(1)}, bf16[512,1024]{1,0:T(8,128)(2,1)}, u32[]{:S(2)}) copy-start(bf16[512,1024]{1,0:T(8,128)(2,1)} %do0.3) | copy-start | bytes 3145732
  0.6 2.7 %copy-start.6 = (bf16[512,576]{0,1:T(8,128)(2,1)S(1)}, bf16[512,576]{0,1:T(8,128)(2,1)}, u32[]{:S(2)}) copy-start(bf16[512,576]{0,1:T(8,128)(2,1)} %param.5) | copy-start | bytes 1769476
  2.0 8.0 %collective-permute-start = (bf16[512,768]{1,0:T(8,128)(2,1)S(1)}, bf16[512,768]{1,0:T(8,128)(2,1)S(1)}, u32[]{:S(2)}, u32[]{:S(2)}) collective-permute-start(bf16[512,768]{1,0:T(8,128)(2,1)S(1)} %constant_dynamic-slice_fusion.5), channel_id=1, source_target_pairs={{0,2},{2,0},{4,6},{6,4},{8,10},{10,8},{12,14},{14,12},{16,18},{18,... | collective-permute-start | bytes 2359304 | tf_op jit(solution)/shard_map/ppermute | solution.py:586
  2.7 7.2 %collective-permute-start.2 = (bf16[576,512]{1,0:T(8,128)(2,1)}, bf16[576,512]{1,0:T(8,128)(2,1)}, u32[]{:S(2)}, u32[]{:S(2)}) collective-permute-start(bf16[576,512]{1,0:T(8,128)(2,1)} %bitcast.6), channel_id=1, source_target_pairs={{0,2},{2,0},{4,6},{6,4},{8,10},{10,8},{12,14},{14,12},{16,18},{18,... | collective-permute-start | bytes 1769480 | tf_op jit(solution)/shard_map/ppermute | solution.py:586
  2.8 7.1 %collective-permute-start.1 = (bf16[512,512]{1,0:T(8,128)(2,1)S(1)}, bf16[512,512]{1,0:T(8,128)(2,1)S(1)}, u32[]{:S(2)}, u32[]{:S(2)}) collective-permute-start(bf16[512,512]{1,0:T(8,128)(2,1)S(1)} %constant_dynamic-slice_fusion.4), channel_id=1, source_target_pairs={{0,2},{2,0},{4,6},{6,4},{8,10},{10,8},{12,14},{14,12},{16,18},{18,... | collective-permute-start | bytes 1572872 | tf_op jit(solution)/shard_map/ppermute | solution.py:586
  3.3 21.0 %collective-permute-start.3 = (bf16[576,512]{1,0:T(8,128)(2,1)S(1)}, bf16[576,512]{1,0:T(8,128)(2,1)S(1)}, u32[]{:S(2)}, u32[]{:S(2)}) collective-permute-start(bf16[576,512]{1,0:T(8,128)(2,1)S(1)} %bitcast.9), channel_id=1, source_target_pairs={{0,4},{2,6},{4,8},{6,10},{8,12},{10,14},{12,16},{14,18},{16,20},{1... | collective-permute-start | bytes 1769480 | tf_op jit(solution)/shard_map/ppermute | solution.py:586
  6.5 17.8 %collective-permute-start.4 = (bf16[576,512]{1,0:T(8,128)(2,1)S(1)}, bf16[576,512]{1,0:T(8,128)(2,1)S(1)}, u32[]{:S(2)}, u32[]{:S(2)}) collective-permute-start(bf16[576,512]{1,0:T(8,128)(2,1)S(1)} %bitcast.10), channel_id=1, source_target_pairs={{2,8},{6,12},{10,16},{14,20},{18,24},{22,28},{3,9},{7,13},{11,17},... | collective-permute-start | bytes 1769480 | tf_op jit(solution)/shard_map/ppermute | solution.py:586
  9.9 0.8 copy-start.11
  10.0 1.0 copy-start.5
  24.3 4.0 %copy-start.7 = (bf16[576,512]{1,0:T(8,128)(2,1)}, bf16[576,512]{1,0:T(8,128)(2,1)S(1)}, u32[]{:S(2)}) copy-start(bf16[576,512]{1,0:T(8,128)(2,1)S(1)} %collective-permute-done.3.lat_far) | copy-start | bytes 1769476
  24.3 4.0 %copy-start.8 = (bf16[576,512]{1,0:T(8,128)(2,1)}, bf16[576,512]{1,0:T(8,128)(2,1)S(1)}, u32[]{:S(2)}) copy-start(bf16[576,512]{1,0:T(8,128)(2,1)S(1)} %collective-permute-done.4.lat_mixed) | copy-start | bytes 1769476
  24.3 2.1 %collective-permute-start.5 = (bf16[576,512]{1,0:T(8,128)(2,1)S(1)}, bf16[576,512]{1,0:T(8,128)(2,1)S(1)}, u32[]{:S(2)}, u32[]{:S(2)}) collective-permute-start(bf16[576,512]{1,0:T(8,128)(2,1)S(1)} %collective-permute-done.3.lat_far), channel_id=1, source_target_pairs={{0,2},{2,0},{4,6},{6,4},{8,10},{10,8},{12,14},{14,12},{16,18},{18,... | collective-permute-start | bytes 1769480 | tf_op jit(solution)/shard_map/ppermute | solution.py:586
  24.4 3.9 %collective-permute-start.6 = (bf16[576,512]{1,0:T(8,128)(2,1)S(1)}, bf16[576,512]{1,0:T(8,128)(2,1)S(1)}, u32[]{:S(2)}, u32[]{:S(2)}) collective-permute-start(bf16[576,512]{1,0:T(8,128)(2,1)S(1)} %collective-permute-done.4.lat_mixed), channel_id=1, source_target_pairs={{0,2},{4,6},{8,10},{12,14},{16,18},{20,22},{24,26},{28,30},{1,3},{... | collective-permute-start | bytes 1769480 | tf_op jit(solution)/shard_map/ppermute | solution.py:586
  26.4 1.9 %copy-start.9 = (bf16[576,512]{1,0:T(8,128)(2,1)}, bf16[576,512]{1,0:T(8,128)(2,1)S(1)}, u32[]{:S(2)}) copy-start(bf16[576,512]{1,0:T(8,128)(2,1)S(1)} %collective-permute-done.5.lat_swap) | copy-start | bytes 1769476
  28.3 0.8 copy-start.10
  71.6 5.8 %copy-start.2 = (bf16[576,512]{1,0:T(8,128)(2,1)S(1)}, bf16[576,512]{1,0:T(8,128)(2,1)}, u32[]{:S(2)}) copy-start(bf16[576,512]{1,0:T(8,128)(2,1)} %get-tuple-element.40) | copy-start | bytes 1769476
  71.7 3.2 %collective-permute-start.9 = (bf16[576,512]{1,0:T(8,128)(2,1)}, bf16[576,512]{1,0:T(8,128)(2,1)S(1)}, u32[]{:S(2)}, u32[]{:S(2)}) collective-permute-start(bf16[576,512]{1,0:T(8,128)(2,1)} %get-tuple-element.38), channel_id=1, source_target_pairs={{0,2},{2,0},{4,6},{6,4},{8,10},{10,8},{12,14},{14,12},{16,18},{18,... | collective-permute-start | bytes 1769480 | tf_op jit(solution)/shard_map/ppermute | solution.py:586
  71.7 5.7 %collective-permute-start.11 = (bf16[576,512]{1,0:T(8,128)(2,1)}, bf16[576,512]{1,0:T(8,128)(2,1)S(1)}, u32[]{:S(2)}, u32[]{:S(2)}) collective-permute-start(bf16[576,512]{1,0:T(8,128)(2,1)} %get-tuple-element.40), channel_id=1, source_target_pairs={{2,0},{6,4},{10,8},{14,12},{18,16},{22,20},{26,24},{30,28},{3,1},{... | collective-permute-start | bytes 1769480 | tf_op jit(solution)/shard_map/ppermute | solution.py:586
  74.2 14.1 %collective-permute-start.17 = (bf16[256,1024]{1,0:T(8,128)(2,1)}, bf16[256,1024]{1,0:T(8,128)(2,1)S(1)}, u32[]{:S(2)}, u32[]{:S(2)}) collective-permute-start(bf16[256,1024]{1,0:T(8,128)(2,1)} %get-tuple-element.43), channel_id=1, source_target_pairs={{0,4},{2,6},{4,0},{6,2},{8,12},{10,14},{12,8},{14,10},{16,20},{18,... | collective-permute-start | bytes 1572872 | tf_op jit(solution)/shard_map/ppermute | solution.py:586
  74.3 5.5 %collective-permute-start.8 = (bf16[576,512]{1,0:T(8,128)(2,1)}, bf16[576,512]{1,0:T(8,128)(2,1)S(1)}, u32[]{:S(2)}, u32[]{:S(2)}) collective-permute-start(bf16[576,512]{1,0:T(8,128)(2,1)} %get-tuple-element.36), channel_id=1, source_target_pairs={{0,2},{2,0},{4,6},{6,4},{8,10},{10,8},{12,14},{14,12},{16,18},{18,... | collective-permute-start | bytes 1769480 | tf_op jit(solution)/shard_map/ppermute | solution.py:586
  74.3 25.2 %collective-permute-start.7 = (bf16[512,768]{1,0:T(8,128)(2,1)}, bf16[512,768]{1,0:T(8,128)(2,1)S(1)}, u32[]{:S(2)}, u32[]{:S(2)}) collective-permute-start(bf16[512,768]{1,0:T(8,128)(2,1)} %get-tuple-element.34), channel_id=1, source_target_pairs={{0,2},{2,0},{4,6},{6,4},{8,10},{10,8},{12,14},{14,12},{16,18},{18,... | collective-permute-start | bytes 2359304 | tf_op jit(solution)/shard_map/ppermute | solution.py:586
  76.1 3.7 %copy-start.1 = (bf16[576,512]{1,0:T(8,128)(2,1)S(1)}, bf16[576,512]{1,0:T(8,128)(2,1)}, u32[]{:S(2)}) copy-start(bf16[576,512]{1,0:T(8,128)(2,1)} %get-tuple-element.35) | copy-start | bytes 1769476
  76.1 8.7 %collective-permute-start.10 = (bf16[288,512]{1,0:T(8,128)(2,1)S(1)}, bf16[288,512]{1,0:T(8,128)(2,1)S(1)}, u32[]{:S(2)}, u32[]{:S(2)}) collective-permute-start(bf16[288,512]{1,0:T(8,128)(2,1)S(1)} %constant_dynamic-slice_fusion.3), channel_id=1, source_target_pairs={{0,1},{1,0},{2,3},{3,2},{4,5},{5,4},{6,7},{7,6},{8,9},{9,8},{10,11... | collective-permute-start | bytes 884744 | tf_op jit(solution)/shard_map/ppermute | solution.py:637
  77.6 10.7 %copy-start.3 = (bf16[256,1024]{1,0:T(8,128)(2,1)S(1)}, bf16[256,1024]{1,0:T(8,128)(2,1)}, u32[]{:S(2)}) copy-start(bf16[256,1024]{1,0:T(8,128)(2,1)} %get-tuple-element.42) | copy-start | bytes 1572868
  78.4 18.8 %collective-permute-start.12 = (bf16[288,512]{1,0:T(8,128)(2,1)}, bf16[288,512]{1,0:T(8,128)(2,1)}, u32[]{:S(2)}, u32[]{:S(2)}) collective-permute-start(bf16[288,512]{1,0:T(8,128)(2,1)} %constant_dynamic-slice_fusion.2), channel_id=1, source_target_pairs={{0,1},{1,0},{4,5},{5,4},{8,9},{9,8},{12,13},{13,12},{16,17},{17,16... | collective-permute-start | bytes 884744 | tf_op jit(solution)/shard_map/ppermute | solution.py:637
  85.6 29.4 %collective-permute-start.14 = (bf16[288,512]{1,0:T(8,128)(2,1)}, bf16[288,512]{1,0:T(8,128)(2,1)}, u32[]{:S(2)}, u32[]{:S(2)}) collective-permute-start(bf16[288,512]{1,0:T(8,128)(2,1)} %add_convert_fusion.8), channel_id=1, source_target_pairs={{4,0},{6,2},{8,4},{10,6},{12,8},{14,10},{16,12},{18,14},{20,16},{2... | collective-permute-start | bytes 884744 | tf_op jit(solution)/shard_map/ppermute | solution.py:586
  88.3 11.2 %copy-start = (bf16[512,768]{1,0:T(8,128)(2,1)S(1)}, bf16[512,768]{1,0:T(8,128)(2,1)}, u32[]{:S(2)}) copy-start(bf16[512,768]{1,0:T(8,128)(2,1)} %get-tuple-element.33) | copy-start | bytes 2359300
  89.3 29.3 %all-to-all-start = ((bf16[4,64,1024]{2,1,0:T(8,128)(2,1)}), bf16[4,64,1024]{2,1,0:T(8,128)(2,1)S(1)}, u32[]{:S(2)}, u32[]{:S(2)}) async-start(bf16[4,64,1024]{2,1,0:T(8,128)(2,1)} %bitcast.4), calls=%async_computation | async-start | bytes 1048576 | tf_op jit(solution)/shard_map/all_to_all | solution.py:672
  98.2 16.7 %collective-permute-start.13 = (bf16[288,512]{1,0:T(8,128)(2,1)S(1)}, bf16[288,512]{1,0:T(8,128)(2,1)S(1)}, u32[]{:S(2)}, u32[]{:S(2)}) collective-permute-start(bf16[288,512]{1,0:T(8,128)(2,1)S(1)} %add_convert_fusion.7), channel_id=1, source_target_pairs={{8,2},{12,6},{16,10},{20,14},{24,18},{28,22},{9,3},{13,7},{17,11},... | collective-permute-start | bytes 884744 | tf_op jit(solution)/shard_map/ppermute | solution.py:586
  99.7 19.1 %collective-permute-start.16 = (bf16[288,512]{1,0:T(8,128)(2,1)S(1)}, bf16[288,512]{1,0:T(8,128)(2,1)S(1)}, u32[]{:S(2)}, u32[]{:S(2)}) collective-permute-start(bf16[288,512]{1,0:T(8,128)(2,1)S(1)} %constant_dynamic-slice_fusion.1), channel_id=1, source_target_pairs={{0,1},{1,0},{2,3},{3,2},{4,5},{5,4},{6,7},{7,6},{8,9},{9,8},{10,11... | collective-permute-start | bytes 884744 | tf_op jit(solution)/shard_map/ppermute | solution.py:637
  116.0 5.6 %collective-permute-start.15 = (bf16[288,512]{1,0:T(8,128)(2,1)S(1)}, bf16[288,512]{1,0:T(8,128)(2,1)S(1)}, u32[]{:S(2)}, u32[]{:S(2)}) collective-permute-start(bf16[288,512]{1,0:T(8,128)(2,1)S(1)} %add_convert_fusion.6), channel_id=1, source_target_pairs={{0,1},{1,0},{2,3},{3,2},{4,5},{5,4},{6,7},{7,6},{8,9},{9,8},{10,11... | collective-permute-start | bytes 884744 | tf_op jit(solution)/shard_map/ppermute | solution.py:637
  118.7 4.0 %collective-permute-start.18 = (f32[32,1024]{1,0:T(8,128)S(1)}, f32[32,1024]{1,0:T(8,128)S(1)}, u32[]{:S(2)}, u32[]{:S(2)}) collective-permute-start(f32[32,1024]{1,0:T(8,128)S(1)} %constant_dynamic-slice_fusion), channel_id=1, source_target_pairs={{0,2},{2,0},{4,6},{6,4},{8,10},{10,8},{12,14},{14,12},{16,18},{18,... | collective-permute-start | bytes 393224 | tf_op jit(solution)/shard_map/ppermute | solution.py:586
